TPU v7x, 128 devices: a whole 4x4x4 slice. The times are simulated.
128 devices in a mesh: leaf: 32 (over y, z, core), sub: 4 (over x).
Axes of the slice: x: 4, y: 4, z: 4, core: 2. Of those that a mesh axis runs over, the one named last changes fastest.
Arguments:
- sources: bfloat16 [4096, 8, 128], P(('leaf', 'sub')), may hold values from -6 to 6
- row_basis: bfloat16 [4096, 128, 128], P(('leaf', 'sub')), may hold values from -0.5 to 0.5
- col_basis: bfloat16 [4096, 128, 128], P(('leaf', 'sub')), may hold values from -0.5 to 0.5
- up_transfer: bfloat16 [8064, 128, 128], P(('leaf', 'sub')), may hold values from -0.375 to 0.375
- down_transfer: bfloat16 [8064, 128, 128], P(('leaf', 'sub')), may hold values from -0.375 to 0.375
- near_blocks: bfloat16 [32768, 128, 128], P(('leaf', 'sub')), may hold values from -0.25 to 0.25
- near_list: int32 [4096, 8], P(('leaf', 'sub')), may hold values from -1 to 4095, as said below
- far_blocks: bfloat16 [30720, 128, 128], P(('leaf', 'sub')), may hold values from -0.25 to 0.25
- far_list: int32 [7680, 4], P(('leaf', 'sub')), may hold values from -1 to 4095, as said below
- upper_blocks: bfloat16 [1024, 128, 128], P(('leaf', 'sub')), may hold values from -0.25 to 0.25
- upper_list: int32 [256, 4], P(('leaf', 'sub')), may hold values from 0 to 255, as said below
- root_blocks: bfloat16 [512, 128, 128], P(('leaf', 'sub')), may hold values from -0.25 to 0.25
- root_list: int32 [128, 4], P(('leaf', 'sub')), may hold values from 0 to 127, as said below
- group_blocks: bfloat16 [512, 128, 128], P(('leaf', 'sub')), may hold values from -0.25 to 0.25
- group_list: int32 [128, 4], P(('leaf', 'sub')), may hold values from 0 to 31, as said below
Outputs:
- adjoint_field: float32 [4096, 8, 128], P(('leaf', 'sub'))
Inputs may be any that keep to these rules, and one draw needn't show every extreme that they name: `near_list`: slot 0 of row t is t itself. Other entries are -1 for an unused slot, else a leaf s with |s // 32 - t // 32| <= 1, s != t, no leaf twice in a row; used slots come first. `far_list`: entries -1 are unused slots, used slots first and slot 0 always used. A used entry of a level-j node t is a node s of level j with |s // (32 >> j) - t // (32 >> j)| <= 1 and |s - t| >= 2, no node twice in a row. `upper_list`: targets are nodes of the level just under the roots, any subtree. `root_list`: targets are roots of any subtree. `group_list`: targets are group nodes.
All inputs are finite; a program needn't handle non-finite values.
Results may differ from a plain program's by a relative error of at most 0.024.
Values sent between devices are 32-bit elements; how exact they have to be, the bound alone decides.
No kernel may reach another device: no remote copies, remote signals or barrier semaphores. Data moves between devices by JAX's collectives and lax.ppermute only.
A program may use at most 128 MiB of HBM per device.

v0:
```python
import jax
import jax.numpy as jnp
from jax import lax
from jax.sharding import PartitionSpec as P


def padded_2(cells, sides, width):
    for axis, dim in sides:
        count = lax.axis_size(axis)
        ends = count - 1
        head = lax.slice_in_dim(cells, 0, width, axis=dim)
        tail = lax.slice_in_dim(cells, cells.shape[dim] - width, cells.shape[dim], axis=dim)
        cells = jnp.concatenate(
            [
                lax.ppermute(tail, axis, [(i, (i + 1) % count) for i in range(ends)]),
                cells,
                lax.ppermute(head, axis, [((i + 1) % count, i) for i in range(ends)]),
            ],
            axis=dim,
        )
    return cells


def node_product(coef, mats):
    return jnp.einsum("nsr,nrq->nsq", coef, mats, preferred_element_type=jnp.float32)


def exact_product(coef, mats):
    return jnp.einsum(
        "nsr,nrq->nsq", coef, mats.astype(jnp.float32), precision=lax.Precision.HIGHEST
    )


def slot_product(coef, mats, slots):
    count = coef.shape[0]
    shaped = mats.reshape(count, slots, mats.shape[1], mats.shape[2])
    terms = jnp.einsum("nsr,nkrq->nksq", coef, shaped, preferred_element_type=jnp.float32)
    return terms.reshape(count * slots, coef.shape[1] * mats.shape[2])


def exact_slots(coef, mats, slots):
    count = coef.shape[0]
    shaped = mats.reshape(count, slots, mats.shape[1], mats.shape[2]).astype(jnp.float32)
    terms = jnp.einsum("nsr,nkrq->nksq", coef, shaped, precision=lax.Precision.HIGHEST)
    return terms.reshape(count * slots, coef.shape[1] * mats.shape[2])


def window_sum(terms, targets, per_device, own_index):
    flat = targets.reshape(-1)
    place = flat - (own_index - 1) * per_device
    hits = (place[:, None] == jnp.arange(3 * per_device)[None, :]) & (flat >= 0)[:, None]
    return jnp.einsum("mw,mc->wc", hits.astype(jnp.float32), terms, precision=lax.Precision.HIGHEST)


def shards(
    sources,
    row_basis,
    col_basis,
    up_transfer,
    down_transfer,
    near_blocks,
    near_list,
    far_blocks,
    far_list,
    upper_blocks,
    upper_list,
    root_blocks,
    root_list,
    group_blocks,
    group_list,
):
    leaf_count = sources.shape[0]
    levels = leaf_count.bit_length() - 1
    columns = sources.shape[1]
    rank_size = up_transfer.shape[2]
    own_index = lax.axis_index(("leaf", "sub"))
    root_count = lax.axis_size(("leaf", "sub"))
    group_count = lax.axis_size("leaf")
    sub_count = lax.axis_size("sub")
    near_slots = near_list.shape[1]
    far_slots = far_list.shape[1]
    top_slots = root_list.shape[1]
    group_slots = group_list.shape[1]
    top_entry = 2 * leaf_count - 2
    coefs = [node_product(sources, row_basis).astype(jnp.bfloat16)]
    for level in range(levels):
        width = leaf_count >> level
        offset = 2 * leaf_count - 2 * width
        product = node_product(coefs[-1], up_transfer[offset : offset + width])
        coefs.append(
            product.reshape(width // 2, 2, columns, rank_size).sum(axis=1).astype(jnp.bfloat16)
        )
    group_term = node_product(coefs[levels], up_transfer[top_entry : top_entry + 1])
    group_coef = lax.psum(group_term, "sub")
    near_terms = slot_product(sources, near_blocks, near_slots)
    buffers = [(window_sum(near_terms, near_list, leaf_count, own_index), leaf_count)]
    for level in range(levels - 1):
        width = leaf_count >> level
        offset = 2 * leaf_count - 2 * width
        terms = slot_product(
            coefs[level], far_blocks[offset * far_slots : (offset + width) * far_slots], far_slots
        )
        buffers.append(
            (window_sum(terms, far_list[offset : offset + width], width, own_index), width)
        )
    span = sum((width for _, width in buffers))
    outgoing = jnp.concatenate(
        [buf[:width] for buf, width in buffers] + [buf[2 * width :] for buf, width in buffers],
        axis=0,
    )
    padded = padded_2(outgoing, ((("leaf", "sub"), 0),), span)
    totals = jnp.concatenate([buf[width : 2 * width] for buf, width in buffers], axis=0)
    totals = totals + padded[:span] + padded[3 * span :]
    near_total = totals[:leaf_count].reshape(leaf_count, columns, rank_size)
    fields = []
    start = leaf_count
    for level in range(levels - 1):
        width = leaf_count >> level
        fields.append(totals[start : start + width].reshape(width, columns, rank_size))
        start = start + width
    upper_terms = slot_product(coefs[levels - 1], upper_blocks, top_slots)
    upper_ids = upper_list.reshape(-1)
    upper_rows = upper_ids // 2 * 3 + upper_ids % 2
    root_terms = slot_product(coefs[levels], root_blocks, top_slots)
    root_rows = root_list.reshape(-1) * 3 + 2
    top_buffer = jnp.zeros((3 * root_count, upper_terms.shape[1]), jnp.float32)
    top_buffer = top_buffer.at[upper_rows].add(upper_terms).at[root_rows].add(root_terms)
    summed = lax.psum(top_buffer, ("leaf", "sub"))
    top_rows = lax.dynamic_slice_in_dim(summed, own_index * 3, 3, 0)
    fields.append(top_rows[0:2].reshape(2, columns, rank_size))
    group_terms = exact_slots(group_coef, group_blocks, group_slots)
    group_buffer = jnp.zeros((group_count, group_terms.shape[1]), jnp.float32)
    group_buffer = group_buffer.at[group_list.reshape(-1)].add(group_terms)
    summed_group = lax.psum(group_buffer, ("leaf", "sub"))
    group_row = lax.dynamic_slice_in_dim(summed_group, own_index // sub_count, 1, 0)
    group_field = group_row.reshape(1, columns, rank_size)
    root_field = top_rows[2:3].reshape(1, columns, rank_size)
    downward = (
        root_field + exact_product(group_field, down_transfer[top_entry : top_entry + 1])
    ).astype(jnp.bfloat16)
    for level in reversed(range(levels)):
        width = leaf_count >> level
        offset = 2 * leaf_count - 2 * width
        parent = jnp.repeat(downward, 2, axis=0)
        downward = (
            fields[level] + node_product(parent, down_transfer[offset : offset + width])
        ).astype(jnp.bfloat16)
    return near_total + node_product(downward, col_basis)


def solution(mesh):
    in_specs = (
        P(("leaf", "sub"), None, None),
        P(("leaf", "sub"), None, None),
        P(("leaf", "sub"), None, None),
        P(("leaf", "sub"), None, None),
        P(("leaf", "sub"), None, None),
        P(("leaf", "sub"), None, None),
        P(("leaf", "sub"), None),
        P(("leaf", "sub"), None, None),
        P(("leaf", "sub"), None),
        P(("leaf", "sub"), None, None),
        P(("leaf", "sub"), None),
        P(("leaf", "sub"), None, None),
        P(("leaf", "sub"), None),
        P(("leaf", "sub"), None, None),
        P(("leaf", "sub"), None),
    )
    out_specs = P(("leaf", "sub"), None, None)
    return jax.shard_map(shards, mesh=mesh, in_specs=in_specs, out_specs=out_specs, check_vma=False)
```

profile of v0, /device:TPU:0, one launch (start us, length us, event | category | flops | bytes accessed | tf_op | source)
XLA Modules:
  0.0 231.7 jit_solution(7853082087703320654)
XLA Ops:
  6.5 0.8 broadcast_compare_fusion
  7.3 0.7 broadcast_subtract_fusion
  8.0 0.7 slice_subtract_fusion.3
  8.7 0.7 slice_compare_fusion.3
  9.4 5.0 %slice.132 = bf16[128,128,128]{2,1,0:T(8,128)(2,1)} slice(bf16[240,128,128]{2,1,0:T(8,128)(2,1)} %param.22), slice={[0:128], [0:128], [0:128]} | slice | bytes 8388608 | tf_op jit(solution)/shard_map/slice | solution.py:101
  14.4 0.7 copy-done.9
  15.3 0.6 slice_compare_fusion.1
  16.0 1.1 slice.144
  17.0 0.6 slice_compare_fusion
  18.0 4.6 %convolution_bitcast_fusion = f32[32,8,8,128]{3,2,1,0:T(8,128)S(1)} fusion(bf16[32,8,128,128]{3,2,1,0:T(8,128)(2,1)} %bitcast.189, bf16[32,8,128]{2,1,0:T(8,128)(2,1)S(1)} %copy-done.7), kind=kOutput, calls=%fused_computation.3 | convolution fusion | flops 67108864 | bytes 9502720 | tf_op jit(solution)/shard_map/nsr,nkrq->nksq/dot_general | solution.py:37
  22.6 0.7 fusion.3
  23.3 0.8 slice_dynamic-update-slice_fusion.3
  24.1 0.6 sub.86
  25.2 0.7 ge.67
  26.1 0.6 sub.89
  26.7 3.0 %fusion.40 = f32[32,8,4,128]{3,1,2,0:T(8,128)S(1)} fusion(bf16[32,4,128,128]{3,2,1,0:T(8,128)(2,1)} %bitcast.188, bf16[32,8,128]{2,1,0:T(8,128)(2,1)S(1)} %convolution_convert_fusion), kind=kOutput, calls=%fused_computation.67 | convolution fusion | flops 33554432 | bytes 4784128 | tf_op jit(solution)/shard_map/nsr,nkrq->nksq/dot_general | solution.py:37
  30.3 0.4 fusion.53
  30.8 0.6 ge.70
  31.6 0.7 sub.92
  32.3 1.7 bitcast_reduce_fusion.2
  34.2 0.8 copy.32
  35.1 0.8 slice_subtract_fusion
  36.0 0.7 copy.34
  36.8 0.9 fusion.83
  37.8 1.1 fusion.12
  38.9 1.0 fusion.19
  39.9 1.0 fusion.27
  41.2 0.8 slice_dynamic-update-slice_fusion.2
  42.0 0.7 slice_dynamic-update-slice_fusion.7
  42.7 0.6 slice_dynamic-update-slice_fusion.10
  43.3 0.6 constant_dynamic-update-slice_fusion.1
  43.9 4.2 %collective-permute-start = (f32[92,1024]{1,0:T(8,128)}, f32[92,1024]{1,0:T(8,128)}, u32[]{:S(2)}, u32[]{:S(2)}) collective-permute-start(f32[92,1024]{1,0:T(8,128)} %get-tuple-element.21), channel_id=1, source_target_pairs={{0,1},{1,2},{2,3},{3,4},{4,5},{5,6},{6,7},{7,8},{8,9},{9,10},{10,1... | collective-permute-start | bytes 1130504 | tf_op jit(solution)/shard_map/ppermute | solution.py:15
  48.1 1.3 collective-permute-start.1
  49.4 1.0 bitcast_reduce_fusion.3
  50.5 1.0 fusion.1
  51.7 0.9 fusion.56
  52.6 10.9 %psum.22 = f32[8,128]{1,0:T(8,128)S(1)} all-reduce(f32[8,128]{1,0:T(8,128)S(1)} %fusion.56), channel_id=1, replica_groups=mesh['leaf'=32,'sub'=4] {'sub'}, use_global_device_ids=true, to_apply=%region_7.8 | all-reduce | flops 1024 | bytes 8192 | tf_op jit(solution)/shard_map/psum | solution.py:94
  63.7 1.1 scatter_custom_fusion
  64.8 1.2 scatter_custom_fusion.2
  66.2 1.2 scatter_custom_fusion.1
  67.4 1.1 copy-done.2
  68.6 1.3 add_add_fusion
  70.1 150.0 %all-reduce.3.cloned.1.call-done = (f32[384,1024]{1,0:T(8,128)}, f32[32,1024]{1,0:T(8,128)}) async-done(((f32[384,1024]{1,0:T(8,128)}, f32[32,1024]{1,0:T(8,128)}), (f32[384,1024]{1,0:T(8,128)}, f32[32,1024]{1,0:T(8,128)})) %all-reduce.3.cloned.1.call-update) | async-done | bytes 1703952 | tf_op jit(solution)/shard_map/psum | solution.py:128
  220.1 0.9 dynamic-slice_bitcast_fusion
  221.0 0.8 constant_dynamic-slice_fusion.1
  221.8 0.8 constant_dynamic-slice_fusion
  223.5 0.4 fusion.26
  223.9 1.0 bitcast_add_fusion.1
  (80 shorter events, 4.8 us)
Async XLA Ops:
  6.5 18.2 %copy-start = (bf16[32,128,128]{2,1,0:T(8,128)(2,1)S(1)}, bf16[32,128,128]{2,1,0:T(8,128)(2,1)}, u32[]{:S(2)}) copy-start(bf16[32,128,128]{2,1,0:T(8,128)(2,1)} %param.16) | copy-start | bytes 3145732
  6.5 213.5 %all-reduce.3.cloned.1.call-start = ((), (), s32[]{:S(2)}) async-start(), calls=%async_computation | async-start | bytes 3407872 | tf_op jit(solution)/shard_map/psum | solution.py:128
  9.4 5.9 %copy-start.1 = (bf16[240,128,128]{2,1,0:T(8,128)(2,1)S(1)}, bf16[240,128,128]{2,1,0:T(8,128)(2,1)}, u32[]{:S(2)}) copy-start(bf16[240,128,128]{2,1,0:T(8,128)(2,1)} %param.22) | copy-start | bytes 23592964
  14.4 0.7 copy-start.9
  15.1 2.9 %copy-start.7 = (bf16[32,8,128]{2,1,0:T(8,128)(2,1)S(1)}, bf16[32,8,128]{2,1,0:T(8,128)(2,1)}, u32[]{:S(2)}) copy-start(bf16[32,8,128]{2,1,0:T(8,128)(2,1)} %param.15) | copy-start | bytes 196612
  26.7 3.0 %copy-start.4 = (bf16[63,128,128]{2,1,0:T(8,128)(2,1)S(1)}, bf16[63,128,128]{2,1,0:T(8,128)(2,1)}, u32[]{:S(2)}) copy-start(bf16[63,128,128]{2,1,0:T(8,128)(2,1)} %param.18) | copy-start | bytes 6193156
  26.7 3.6 %slice-start = ((bf16[240,128,128]{2,1,0:T(8,128)(2,1)}), bf16[64,128,128]{2,1,0:T(8,128)(2,1)S(1)}, s32[]{:S(2)}) async-start(bf16[240,128,128]{2,1,0:T(8,128)(2,1)} %param.22), calls=%async_computation.1 | async-start | bytes 4194304 | tf_op jit(solution)/shard_map/slice | solution.py:101
  34.2 15.2 %copy-start.12 = (bf16[4,8,128]{2,1,0:T(8,128)(2,1)S(1)}, bf16[4,8,128]{2,1,0:T(8,128)(2,1)}, u32[]{:S(2)}) copy-start(bf16[4,8,128]{2,1,0:T(8,128)(2,1)} %bitcast_reduce_fusion.2) | copy-start | bytes 24580
  34.2 17.2 %copy-start.8 = (bf16[8,128,128]{2,1,0:T(8,128)(2,1)S(1)}, bf16[8,128,128]{2,1,0:T(8,128)(2,1)}, u32[]{:S(2)}) copy-start(bf16[8,128,128]{2,1,0:T(8,128)(2,1)} %param.24) | copy-start | bytes 786436
  36.8 14.8 %copy-start.15 = (s32[2,4]{1,0:T(2,128)S(1)}, s32[2,4]{1,0:T(2,128)}, u32[]{:S(2)}) copy-start(s32[2,4]{1,0:T(2,128)} %param.25) | copy-start | bytes 100
  36.8 26.7 %copy-start.10 = (bf16[4,128,128]{2,1,0:T(8,128)(2,1)S(1)}, bf16[4,128,128]{2,1,0:T(8,128)(2,1)}, u32[]{:S(2)}) copy-start(bf16[4,128,128]{2,1,0:T(8,128)(2,1)} %param.28) | copy-start | bytes 393220
  39.9 24.9 %copy-start.13 = (s32[1,4]{1,0:T(1,128)S(1)}, s32[1,4]{1,0:T(1,128)}, u32[]{:S(2)}) copy-start(s32[1,4]{1,0:T(1,128)} %param.27) | copy-start | bytes 52
  39.9 24.9 %copy-start.14 = (s32[1,4]{1,0:T(1,128)S(1)}, s32[1,4]{1,0:T(1,128)}, u32[]{:S(2)}) copy-start(s32[1,4]{1,0:T(1,128)} %param.29) | copy-start | bytes 52
  40.9 25.1 %copy-start.11 = (bf16[4,128,128]{2,1,0:T(8,128)(2,1)S(1)}, bf16[4,128,128]{2,1,0:T(8,128)(2,1)}, u32[]{:S(2)}) copy-start(bf16[4,128,128]{2,1,0:T(8,128)(2,1)} %param.26) | copy-start | bytes 393220
  43.9 24.7 %collective-permute-start = (f32[92,1024]{1,0:T(8,128)}, f32[92,1024]{1,0:T(8,128)}, u32[]{:S(2)}, u32[]{:S(2)}) collective-permute-start(f32[92,1024]{1,0:T(8,128)} %get-tuple-element.21), channel_id=1, source_target_pairs={{0,1},{1,2},{2,3},{3,4},{4,5},{5,6},{6,7},{7,8},{8,9},{9,10},{10,1... | collective-permute-start | bytes 1130504 | tf_op jit(solution)/shard_map/ppermute | solution.py:15
  48.1 20.5 %collective-permute-start.1 = (f32[92,1024]{1,0:T(8,128)}, f32[92,1024]{1,0:T(8,128)}, u32[]{:S(2)}, u32[]{:S(2)}) collective-permute-start(f32[92,1024]{1,0:T(8,128)} %get-tuple-element.22), channel_id=1, source_target_pairs={{1,0},{2,1},{3,2},{4,3},{5,4},{6,5},{7,6},{8,7},{9,8},{10,9},{11,1... | collective-permute-start | bytes 1130504 | tf_op jit(solution)/shard_map/ppermute | solution.py:17
  64.7 3.9 %copy-start.6 = (f32[92,1024]{1,0:T(8,128)S(1)}, f32[92,1024]{1,0:T(8,128)}, u32[]{:S(2)}) copy-start(f32[92,1024]{1,0:T(8,128)} %get-tuple-element.23) | copy-start | bytes 1130500
  67.4 1.1 copy-start.2
  68.6 154.0 %copy-start.3 = (bf16[63,128,128]{2,1,0:T(8,128)(2,1)S(1)}, bf16[63,128,128]{2,1,0:T(8,128)(2,1)}, u32[]{:S(2)}) copy-start(bf16[63,128,128]{2,1,0:T(8,128)(2,1)} %param.19) | copy-start | bytes 6193156
  220.1 3.8 %copy-start.5 = (bf16[32,128,128]{2,1,0:T(8,128)(2,1)S(1)}, bf16[32,128,128]{2,1,0:T(8,128)(2,1)}, u32[]{:S(2)}) copy-start(bf16[32,128,128]{2,1,0:T(8,128)(2,1)} %param.17) | copy-start | bytes 3145732
Sparse Core Ops, SparseCore 0:
  68.7 151.3 all-reduce.2
where the time goes:
time: 233 us; the launch traced here: 232 us
  waiting for transfers between devices  150 us (64%)
  matrix products  21.6 us (9%)
  local copies, waits for them, and re-layouts  20.2 us (9%)
  between operations  13.7 us (6%)
  blocking collectives  10.9 us (5%)
  other arithmetic  9.88 us (4%)
  starting transfers between devices  5.5 us (2%)
    psum x1, waiting for transfers between devices, shards(): summed = lax.psum(top_buffer, ('leaf', 'sub'))  150 us
    psum x1, blocking collectives, shards(): group_coef = lax.psum(group_term, 'sub')  10.9 us
    dot_general x7, matrix products, slot_product(): jnp.einsum('nsr,nkrq->nksq', coef, shaped, preferred_element_type=jnp.flo...  9.38 us
    dot_general x13, matrix products, node_product(): jnp.einsum('nsr,nrq->nsq', coef, mats, preferred_element_type=jnp.float32)  7.82 us
    slice x5, local copies, waits for them, and re-layouts, shards(): far_blocks[offset * far_slots:(offset + width) * far_slots]  6.15 us
    unnamed x43, local copies, waits for them, and re-layouts  5.91 us
  transfers between devices with their start and end apart: 3, of which 1 were waited for; matrix products, arithmetic and copies ran while one was open for 4% of the time, Pallas kernels for 0%

commit v1 on v0

v1 whole, which is shorter than its diff:
```python
import functools

import jax
import jax.numpy as jnp
from jax import lax
from jax.experimental import pallas as pl
from jax.experimental.pallas import tpu as pltpu
from jax.sharding import PartitionSpec as P

F32 = jnp.float32
BF16 = jnp.bfloat16
ANY = pl.BlockSpec(memory_space=pl.ANY)
VMEM = pl.BlockSpec(memory_space=pltpu.VMEM)
REPLICAS = 4
UPPER_TERMS, ROOT_TERMS, GROUP_TERMS = 8, 4, 4
TOP_TERMS = UPPER_TERMS + ROOT_TERMS
TERMS = TOP_TERMS + GROUP_TERMS


def rounded(x):
    return x.astype(BF16).astype(F32)


def dot(x, w):
    return jnp.dot(x.astype(BF16), w, preferred_element_type=F32)


def square(w00, w01, w10, w11):
    top = jnp.concatenate([w00, w01], axis=1)
    return jnp.concatenate([top, jnp.concatenate([w10, w11], axis=1)], axis=0)


def diagonal(x, y):
    zero = jnp.zeros_like(x)
    top = jnp.concatenate([x, zero], axis=1)
    return jnp.concatenate([top, jnp.concatenate([zero, y], axis=1)], axis=0)


def quad(xs, ws):
    left = jnp.concatenate([diagonal(xs[0], xs[1]), diagonal(xs[2], xs[3])], axis=0)
    out = dot(left, square(ws[0], ws[2], ws[1], ws[3]))
    n, m = xs[0].shape
    return [out[:n, :m], out[n : 2 * n, :m], out[2 * n : 3 * n, m:], out[3 * n :, m:]]


def exact_parts(x):
    high = rounded(x)
    rest = x - high
    middle = rounded(rest)
    return jnp.concatenate([high, middle, rest - middle], axis=0)


def exact_dot(parts, w):
    n = parts.shape[0] // 3
    out = dot(parts, w)
    return (out[2 * n :] + out[n : 2 * n]) + out[:n]


def level_offset(leaves, level):
    return 2 * leaves - 2 * (leaves >> level)


class Fetches:
    def __init__(self, sem):
        self.sem, self.count = sem, 0

    def __call__(self, src, dst):
        copy = pltpu.make_async_copy(src, dst, self.sem.at[self.count])
        copy.start()
        self.count += 1
        return copy

    def rows(self, src, dst, start, size):
        return self(src.at[pl.ds(start, size)], dst.at[pl.ds(start, size)])


def up_kernel(
    src_hbm, upper_list_hbm, root_list_hbm, rb_hbm, up_hbm, ub_hbm, rt_hbm,
    coef_ref, group_ref, top_ref, src, upper_list, root_list, rb, up, ub, rt, sem,
):
    leaves = src.shape[0]
    levels = leaves.bit_length() - 1
    quarter = leaves // 4
    fetch = Fetches(sem)
    src_copy = fetch(src_hbm, src)
    rb_copies = [fetch.rows(rb_hbm, rb, i * quarter, quarter) for i in range(4)]
    up_copies = [fetch.rows(up_hbm, up, i * quarter, quarter) for i in range(4)]
    rest = fetch.rows(up_hbm, up, leaves, leaves - 1)
    tail = [
        fetch(ub_hbm, ub), fetch(rt_hbm, rt),
        fetch(upper_list_hbm, upper_list), fetch(root_list_hbm, root_list),
    ]

    src_copy.wait()
    for t in range(0, leaves, 4):
        if t % quarter == 0:
            rb_copies[t // quarter].wait()
        span = range(t, t + 4)
        outs = quad([src[i].astype(F32) for i in span], [rb[i] for i in span])
        for i, out in zip(span, outs):
            coef_ref[i] = rounded(out)
    for level in range(levels):
        width = leaves >> level
        offset = level_offset(leaves, level)
        if level == 1:
            rest.wait()
        for t in range(0, width, 4):
            if level == 0 and t % quarter == 0:
                up_copies[t // quarter].wait()
            a = offset + t
            parent = offset + width + t // 2
            c = [coef_ref[a + i] for i in range(min(4, width))]
            if width == 2:
                left = jnp.concatenate(c, axis=1)
                out = dot(left, jnp.concatenate([up[a], up[a + 1]], axis=0))
                coef_ref[parent] = rounded(out)
            else:
                left = jnp.concatenate(
                    [jnp.concatenate(c[:2], axis=1), jnp.concatenate(c[2:], axis=1)], axis=0
                )
                out = dot(left, square(up[a], up[a + 2], up[a + 1], up[a + 3]))
                n, m = c[0].shape
                coef_ref[parent] = rounded(out[:n, :m])
                coef_ref[parent + 1] = rounded(out[n:, m:])
    top = 2 * leaves - 2
    group_ref[...] = dot(coef_ref[top], up[top])
    for c in tail:
        c.wait()
    n, m = src.shape[1:]
    left = diagonal(coef_ref[top - 2], coef_ref[top - 1])
    for k in range(0, 4, 2):
        out = dot(left, square(ub[k], ub[k + 1], ub[4 + k], ub[5 + k]))
        top_ref[k] = out[:n, :m]
        top_ref[k + 1] = out[:n, m:]
        top_ref[4 + k] = out[n:, :m]
        top_ref[5 + k] = out[n:, m:]
    for k in range(0, ROOT_TERMS, 2):
        out = dot(coef_ref[top], jnp.concatenate([rt[k], rt[k + 1]], axis=1))
        top_ref[UPPER_TERMS + k] = out[:, :m]
        top_ref[UPPER_TERMS + k + 1] = out[:, m:]
    top_ref[TOP_TERMS] = jnp.zeros((n, m), F32)
    top_ref[TOP_TERMS, 0:2, 0:4] = upper_list[...].astype(F32)
    top_ref[TOP_TERMS, 2:3, 0:4] = root_list[...].astype(F32)


def scatter_steps(left_of, mats, target_of, accs, slots, first, count, step, level, levels, start, span):
    own_index = lax.axis_index("leaf") * lax.axis_size("sub") + lax.axis_index("sub")
    shift = levels - level
    base = (own_index - 1) * (1 << shift)

    def add(replica, target, term):
        place = target - base
        row = lax.shift_right_arithmetic(place, shift) * span + start + (place & ((1 << shift) - 1))
        row = jnp.where(target >= 0, row, 3 * span)
        accs[replica][row] = accs[replica][row] + term

    def body(c, carry):
        for i in range(0, step, 2):
            t = c * step + i
            x, y = left_of(t), left_of(t + 1)
            n, m = x.shape
            left = diagonal(x, y)
            a, b = t * slots, (t + 1) * slots
            for k in range(0, slots, 2):
                out = dot(left, square(mats[a + k], mats[a + k + 1], mats[b + k], mats[b + k + 1]))
                add(0, target_of(t, k), out[:n, :m])
                add(1, target_of(t, k + 1), out[:n, m:])
                add(2, target_of(t + 1, k), out[n:, :m])
                add(3, target_of(t + 1, k + 1), out[n:, m:])
        return carry

    lax.fori_loop(first // step, (first + count) // step, body, 0)


def store_totals(accs, span, refs):
    for i, ref in enumerate(refs):
        parts = [acc[pl.ds(i * span, span)] for acc in accs]
        ref[0:span] = (parts[0] + parts[1]) + (parts[2] + parts[3])


def near_kernel(
    src_hbm, list_hbm, near, far_prev, far_own, far_next, order,
    prev_ref, own_ref, next_ref, src_ref, near_list, a0, a1, a2, a3, sem,
):
    leaves = src_ref.shape[0]
    slots = near_list.shape[0]
    fetch = Fetches(sem)
    first = [fetch(list_hbm, near_list), fetch(src_hbm, src_ref)]
    accs = (a0, a1, a2, a3)
    for acc in accs:
        acc[...] = jnp.zeros(acc.shape, F32)
    for out, part in ((prev_ref, far_prev), (own_ref, far_own), (next_ref, far_next)):
        out[leaves:] = part[...]
    for c in first:
        c.wait()
    scatter_steps(
        lambda t: src_ref[t].astype(F32), near, lambda t, k: near_list[k, t], accs,
        slots, 0, leaves, 8, 0, leaves.bit_length() - 1, 0, leaves,
    )
    store_totals(accs, leaves, (prev_ref, own_ref, next_ref))


def far_kernel(
    leaves, coef_ref, list_hbm, far, order, prev_ref, own_ref, next_ref, far_list, a0, a1, a2, a3, sem,
):
    levels = leaves.bit_length() - 1
    slots, nodes = far_list.shape
    fetch = Fetches(sem)
    first = fetch(list_hbm, far_list)
    accs = (a0, a1, a2, a3)
    for acc in accs:
        acc[...] = jnp.zeros(acc.shape, F32)
    first.wait()
    for level in range(levels - 1):
        offset = level_offset(leaves, level)
        scatter_steps(
            lambda t: coef_ref[t], far, lambda t, k: far_list[k, t], accs,
            slots, offset, leaves >> level, min(16, leaves >> level), level, levels, offset, nodes,
        )
    store_totals(accs, nodes, (prev_ref, own_ref, next_ref))


def group_kernel(g0, g1, g2, g3, top_ref, group_list, blocks, out_ref):
    coef = (g0[...] + g1[...]) + (g2[...] + g3[...])
    parts = exact_parts(coef)
    m = coef.shape[1]
    for k in range(0, GROUP_TERMS, 2):
        out = exact_dot(parts, jnp.concatenate([blocks[k], blocks[k + 1]], axis=1))
        out_ref[TOP_TERMS + k] = out[:, :m]
        out_ref[TOP_TERMS + k + 1] = out[:, m:]
    out_ref[0:TOP_TERMS] = top_ref[0:TOP_TERMS]
    out_ref[TERMS] = top_ref[TOP_TERMS]
    out_ref[TERMS, 3:4, 0:4] = group_list[...].astype(F32)


def pack_kernel(p0, p1, p2, p3, order, keep_ref, send_ref, ids, a0, a1, a2, a3, sem):
    half = keep_ref.shape[0]
    parts = (p0, p1, p2, p3)
    accs = (a0, a1, a2, a3)
    copies = [pltpu.make_async_copy(p.at[TERMS], ids.at[i], sem.at[i]) for i, p in enumerate(parts)]
    for c in copies:
        c.start()
    for acc in accs:
        acc[...] = jnp.zeros(acc.shape, F32)
    own_sub = lax.axis_index("sub")
    own_core = lax.axis_index("leaf") & 1
    for c in copies:
        c.wait()

    def place(leaf, entry):
        return (leaf & 1) * half + lax.shift_right_arithmetic(leaf, 1) * 4 + entry

    def add(acc, root, entry, term):
        row = place(lax.shift_right_arithmetic(root, 2), entry)
        row = jnp.where((root & 3) == own_sub, row, 2 * half)
        acc[row] = acc[row] + term

    for j in range(UPPER_TERMS):
        for i, (p, acc) in enumerate(zip(parts, accs)):
            node = ids[i, j // 4, j % 4].astype(jnp.int32)
            add(acc, lax.shift_right_arithmetic(node, 1), node & 1, p[j])
    for j in range(ROOT_TERMS):
        for i, (p, acc) in enumerate(zip(parts, accs)):
            root = ids[i, 2, j].astype(jnp.int32)
            add(acc, root, 2, p[UPPER_TERMS + j])
    for j in range(GROUP_TERMS):
        for i, (p, acc) in enumerate(zip(parts, accs)):
            row = place(ids[i, 3, j].astype(jnp.int32), 3)
            acc[row] = acc[row] + p[TOP_TERMS + j]

    def total(first):
        part = pl.ds(first, half)
        return (a0[part] + a1[part]) + (a2[part] + a3[part])

    keep_ref[...] = total(own_core * half)
    send_ref[...] = total((1 - own_core) * half)


def core_kernel(keep_ref, core_ref, out_ref):
    out_ref[...] = (keep_ref[...] + core_ref[...]).reshape(out_ref.shape)


def down_kernel(top, own, prev, after, down_hbm, col_hbm, out_ref, down, col, level_down, sem):
    leaves = out_ref.shape[0]
    levels = leaves.bit_length() - 1
    quarter = leaves // 4
    n, m = out_ref.shape[1:]
    fetch = Fetches(sem)
    rest = fetch.rows(down_hbm, down, leaves, leaves - 1)
    down_copies = [fetch.rows(down_hbm, down, i * quarter, quarter) for i in range(4)]
    col_copies = [fetch.rows(col_hbm, col, i * quarter, quarter) for i in range(4)]

    def total(i):
        return (own[i] + prev[i]) + after[i]

    fields = top[0]
    for i in range(1, top.shape[0]):
        fields = fields + top[i]
    rest.wait()
    root = 2 * leaves - 2
    level_down[root] = rounded(fields[2] + exact_dot(exact_parts(fields[3]), down[root]))
    out = dot(level_down[root], jnp.concatenate([down[root - 2], down[root - 1]], axis=1))
    level_down[root - 2] = rounded(fields[0] + out[:, :m])
    level_down[root - 1] = rounded(fields[1] + out[:, m:])
    for level in reversed(range(levels - 1)):
        width = leaves >> level
        offset = level_offset(leaves, level)
        for t in range(0, width, 4):
            if level == 0 and t % quarter == 0:
                down_copies[t // quarter].wait()
            a = offset + t
            parent = offset + width + t // 2
            left = diagonal(level_down[parent], level_down[parent + 1])
            out = dot(left, square(down[a], down[a + 1], down[a + 2], down[a + 3]))
            outs = (out[:n, :m], out[:n, m:], out[n:, :m], out[n:, m:])
            for i in range(4):
                level_down[a + i] = rounded(total(leaves + a + i) + outs[i])
    for t in range(0, leaves, 4):
        if t % quarter == 0:
            col_copies[t // quarter].wait()
        span = range(t, t + 4)
        outs = quad([level_down[i] for i in span], [col[i] for i in span])
        for i, out in zip(span, outs):
            out_ref[i] = total(i) + out


PARAMS = pltpu.CompilerParams(vmem_limit_bytes=24 * 1024 * 1024)


def cost(us):
    return pl.CostEstimate(flops=int(us * 1e9), bytes_accessed=0, transcendentals=0)


def shards(
    sources, row_basis, col_basis, up_transfer, down_transfer, near_blocks, near_list,
    far_blocks, far_list, upper_blocks, upper_list, root_blocks, root_list, group_blocks, group_list,
):
    in_hbm = functools.partial(pltpu.with_memory_space_constraint, memory_space=pltpu.HBM)
    sources, row_basis, col_basis, up_transfer, down_transfer = map(
        in_hbm, (sources, row_basis, col_basis, up_transfer, down_transfer)
    )
    near_list, far_list, upper_blocks, upper_list, root_blocks, root_list = map(
        in_hbm, (near_list.T, far_list.T, upper_blocks, upper_list, root_blocks, root_list)
    )
    leaves, columns, size = sources.shape
    nodes = up_transfer.shape[0]
    far_slots, far_nodes = far_list.shape
    near_slots = near_list.shape[0]
    groups = lax.axis_size("leaf")
    subs = lax.axis_size("sub")
    devices = groups * subs
    row = (columns, size)

    def shape(*lead):
        return jax.ShapeDtypeStruct(lead + row, F32)

    def buffer(count):
        return pltpu.VMEM((count, size, size), BF16)

    def plane(*lead):
        return pltpu.VMEM(lead + row, F32)

    def copies(count):
        return pltpu.SemaphoreType.DMA((count,))

    def around(x, axis, size, shift):
        return lax.ppermute(x, axis, [(i, (i + shift) % size) for i in range(size)])

    def call(kernel, name, us, outs, operands, specs, scratch):
        return pl.pallas_call(
            kernel,
            out_shape=outs,
            in_specs=specs,
            out_specs=jax.tree.map(lambda _: VMEM, outs),
            scratch_shapes=scratch,
            compiler_params=PARAMS,
            cost_estimate=cost(us),
            name=name,
        )(*operands)

    accumulators = lambda count: [plane(3 * count + 1)] * REPLICAS

    def permuted(x, axis, target):
        return lax.ppermute(x, axis, [(i, target(i)) for i in range(lax.axis_size(axis))])

    def gathered(x):
        return [x] + [permuted(x, "sub", lambda i, s=s: (i + s) % subs) for s in range(1, subs)]

    coef, group, top = call(
        up_kernel, "upward", 4, (shape(nodes), shape(), shape(TOP_TERMS + 1)),
        (sources, upper_list, root_list, row_basis, up_transfer, upper_blocks, root_blocks),
        [ANY] * 7,
        [
            pltpu.VMEM((leaves,) + row, BF16),
            pltpu.VMEM(upper_list.shape, jnp.int32), pltpu.VMEM(root_list.shape, jnp.int32),
            buffer(leaves), buffer(nodes), buffer(UPPER_TERMS), buffer(ROOT_TERMS), copies(14),
        ],
    )
    group_parts = gathered(group)
    far_prev, far_own, far_next = call(
        functools.partial(far_kernel, leaves), "far", 4, (shape(far_nodes),) * 3,
        (coef, far_list, far_blocks, group),
        [VMEM, ANY, VMEM, ANY],
        [pltpu.SMEM((far_slots, far_nodes), jnp.int32)] + accumulators(far_nodes) + [copies(1)],
    )
    terms = call(
        group_kernel, "group", 1, shape(TERMS + 1), (*group_parts, top, group_list, group_blocks),
        [VMEM] * 7, [],
    )
    term_parts = gathered(terms)
    to_prev, own, to_next = call(
        near_kernel, "near", 4, (shape(leaves + far_nodes),) * 3,
        (sources, near_list, near_blocks, far_prev, far_own, far_next, terms),
        [ANY, ANY, VMEM, VMEM, VMEM, VMEM, ANY],
        [pltpu.VMEM((leaves,) + row, BF16), pltpu.SMEM((near_slots, leaves), jnp.int32)]
        + accumulators(leaves) + [copies(2)],
    )
    from_prev = around(to_next, ("leaf", "sub"), devices, 1)
    from_next = around(to_prev, ("leaf", "sub"), devices, -1)

    half = groups // 2 * 4
    keep, send = call(
        pack_kernel, "pack", 0, (shape(half), shape(half)), (*term_parts, own), [VMEM] * 4 + [ANY],
        [pltpu.SMEM((subs,) + row, F32)] + [plane(2 * half + 1)] * 4 + [copies(subs)],
    )
    from_core = permuted(send, "leaf", lambda i: i ^ 1)
    planes = call(core_kernel, "core", 0, shape(groups // 2, 4), (keep, from_core), [VMEM] * 2, [])
    fields = lax.all_to_all(
        planes, "leaf", 0, 0, tiled=True, axis_index_groups=[list(range(c, groups, 2)) for c in range(2)]
    )
    return call(
        down_kernel, "downward", 0, shape(leaves),
        (fields, own, from_prev, from_next, down_transfer, col_basis), [VMEM] * 4 + [ANY] * 2,
        [buffer(nodes), buffer(leaves), plane(nodes), copies(9)],
    )


def solution(mesh):
    blocks = P(("leaf", "sub"), None, None)
    lists = P(("leaf", "sub"), None)
    in_specs = (
        blocks, blocks, blocks, blocks, blocks, blocks, lists,
        blocks, lists, blocks, lists, blocks, lists, blocks, lists,
    )
    return jax.shard_map(shards, mesh=mesh, in_specs=in_specs, out_specs=blocks, check_vma=False)
```

time: 233 us -> 46.6 us (0.20)
  waiting for transfers between devices: 150 us -> 10.2 us
  matrix products: 21.6 us -> 0 us
  local copies, waits for them, and re-layouts: 20.2 us -> 0.02 us
  starting transfers between devices: 5.5 us -> 21.7 us
  Pallas kernels: 0 us -> 14.2 us
  between operations: 13.7 us -> 0.12 us
  blocking collectives: 10.9 us -> 0 us
  other arithmetic: 9.88 us -> 0.01 us
    psum x1 -> x0, waiting for transfers between devices: 150 us -> none  [shards(): summed = lax.psum(top_buffer, ('leaf', 'sub'))]
    dot_general x27 -> x0, matrix products: 21.6 us -> none  [the longest x7 9.38 us: slot_product(): jnp.einsum('nsr,nkrq->nksq', coef, shaped, preferred_element_type=jnp.flo...]
    pallas_call x0 -> x7, Pallas kernels: none -> 14.2 us  [call(): pl.pallas_call(kernel, out_shape=outs, in_specs=specs, out_specs=jax.tree...]
    ppermute x2 -> x9, starting transfers between devices: 5.49 us -> 17.4 us  [the longest x7 9.73 us: permuted(): lax.ppermute(x, axis, [(i, target(i)) for i in range(lax.axis_size(axis))])]
    psum x1 -> x0, blocking collectives: 10.9 us -> none  [shards(): group_coef = lax.psum(group_term, 'sub')]
    slice x6 -> x0, local copies, waits for them, and re-layouts: 6.92 us -> none  [the longest x5 6.15 us: shards(): far_blocks[offset * far_slots:(offset + width) * far_slots]]
    all_to_all x0 -> x1, waiting for transfers between devices: none -> 6.1 us  [shards(): lax.all_to_all(planes, 'leaf', 0, 0, tiled=True, axis_index_groups=[list(...]
    unnamed x43 -> x10, local copies, waits for them, and re-layouts: 5.91 us -> 0.02 us
  transfers between devices with their start and end apart: 3 -> 10, of which waited for: 1 -> 4; matrix products, arithmetic and copies ran while one was open for 4% -> 0% of each run, Pallas kernels for 0% -> 12%
where the time goes in v1:
time: 46.6 us; the launch traced here: 46.3 us
  starting transfers between devices  21.7 us (47%)
  Pallas kernels  14.2 us (30%)
  waiting for transfers between devices  10.2 us (22%)
    pallas_call x7, Pallas kernels, call(): pl.pallas_call(kernel, out_shape=outs, in_specs=specs, out_specs=jax.tree...  14.2 us
    ppermute x7, starting transfers between devices, permuted(): lax.ppermute(x, axis, [(i, target(i)) for i in range(lax.axis_size(axis))])  9.73 us
    ppermute x2, starting transfers between devices, around(): return lax.ppermute(x, axis, [(i, (i + shift) % size) for i in range(size)])  7.72 us
    all_to_all x1, waiting for transfers between devices, shards(): lax.all_to_all(planes, 'leaf', 0, 0, tiled=True, axis_index_groups=[list(...  6.1 us
    all_to_all x1, starting transfers between devices, shards(): lax.all_to_all(planes, 'leaf', 0, 0, tiled=True, axis_index_groups=[list(...  4.26 us
    ppermute x2, waiting for transfers between devices, around(): return lax.ppermute(x, axis, [(i, (i + shift) % size) for i in range(size)])  2.41 us
    ppermute x7, waiting for transfers between devices, permuted(): lax.ppermute(x, axis, [(i, target(i)) for i in range(lax.axis_size(axis))])  1.73 us
  transfers between devices with their start and end apart: 10, of which 4 were waited for; matrix products, arithmetic and copies ran while one was open for 0% of the time, Pallas kernels for 12%

profile of v1, /device:TPU:0, one launch (start us, length us, event | category | flops | bytes accessed | tf_op | source)
XLA Modules:
  0.0 46.3 jit_solution(599763617864751531)
XLA Ops:
  0.0 0.0 copy-start
  0.0 0.0 slice-start
  0.0 3.3 %upward.1 = (f32[63,8,128]{2,1,0:T(8,128)S(1)}, f32[8,128]{1,0:T(8,128)S(1)}, f32[13,8,128]{2,1,0:T(8,128)S(1)}) custom-call(bf16[32,8,128]{2,1,0:T(8,128)(2,1)} %src_hbm.3, s32[2,4]{1,0:T(2,128)} %upper_list_hbm.1, s32[1,4]{1,0:T(1,128)} %root_list_hbm.1, bf16[32,128,128]{2,1,0:T(8,128)(2,1)} %rb_hbm.1, bf16[63,128,128]{2,1,0:T(8,128)(2,1)} %up_hbm.1, ...), custom_call_target="tpu_custom_call" | custom-call | flops 4000000000 | tf_op jit(solution)/shard_map/upward/pallas_call | solution.py:370
  3.3 0.0 copy-start.1
  3.3 0.0 copy-start.2
  3.4 1.6 %collective-permute-start = (f32[8,128]{1,0:T(8,128)S(1)}, f32[8,128]{1,0:T(8,128)S(1)}, u32[]{:S(2)}, u32[]{:S(2)}) collective-permute-start(f32[8,128]{1,0:T(8,128)S(1)} %get-tuple-element.16.g0.order), channel_id=1, source_target_pairs={{0,1},{1,2},{2,3},{3,0},{4,5},{5,6},{6,7},{7,4},{8,9},{9,10},{10,1... | collective-permute-start | bytes 12296 | tf_op jit(solution)/shard_map/ppermute | solution.py:384
  5.0 2.7 %collective-permute-start.1 = (f32[8,128]{1,0:T(8,128)S(1)}, f32[8,128]{1,0:T(8,128)S(1)}, u32[]{:S(2)}, u32[]{:S(2)}) collective-permute-start(f32[8,128]{1,0:T(8,128)S(1)} %get-tuple-element.16.g0.order), channel_id=1, source_target_pairs={{0,2},{1,3},{2,0},{3,1},{4,6},{5,7},{6,4},{7,5},{8,10},{9,11},{10,... | collective-permute-start | bytes 12296 | tf_op jit(solution)/shard_map/ppermute | solution.py:384
  7.7 1.4 %collective-permute-start.2 = (f32[8,128]{1,0:T(8,128)S(1)}, f32[8,128]{1,0:T(8,128)S(1)}, u32[]{:S(2)}, u32[]{:S(2)}) collective-permute-start(f32[8,128]{1,0:T(8,128)S(1)} %get-tuple-element.16.g0.order), channel_id=1, source_target_pairs={{0,3},{1,0},{2,1},{3,2},{4,7},{5,4},{6,5},{7,6},{8,11},{9,8},{10,9... | collective-permute-start | bytes 12296 | tf_op jit(solution)/shard_map/ppermute | solution.py:384
  9.2 0.0 copy-done
  9.2 0.0 slice-start.1
  9.2 2.4 %far.2 = (f32[60,8,128]{2,1,0:T(8,128)S(1)}, f32[60,8,128]{2,1,0:T(8,128)S(1)}, f32[60,8,128]{2,1,0:T(8,128)S(1)}) custom-call(f32[63,8,128]{2,1,0:T(8,128)S(1)} %get-tuple-element.18.coef_ref, s32[4,60]{1,0:T(4,128)} %bitcast.5, bf16[240,128,128]{2,1,0:T(8,128)(2,1)S(1)} %copy-done, f32[8,128]{1,0:T(8,128)S(1)} %get-tuple-element.16.g0.order), custom_call_target="tpu_custom_call" | custom-call | flops 4000000000 | tf_op jit(solution)/shard_map/far/pallas_call | solution.py:370
  11.6 0.0 collective-permute-done.g1
  11.6 0.0 collective-permute-done.1.g2
  11.6 0.0 collective-permute-done.2.g3
  11.6 0.0 copy-done.1
  11.6 0.0 copy-done.2
  11.7 0.1 group.1.order.p0
  11.8 0.6 %collective-permute-start.3 = (f32[17,8,128]{2,1,0:T(8,128)S(1)}, f32[17,8,128]{2,1,0:T(8,128)S(1)}, u32[]{:S(2)}, u32[]{:S(2)}) collective-permute-start(f32[17,8,128]{2,1,0:T(8,128)S(1)} %group.1.order.p0), channel_id=1, source_target_pairs={{0,1},{1,2},{2,3},{3,0},{4,5},{5,6},{6,7},{7,4},{8,9},{9,10},{10,1... | collective-permute-start | bytes 208904 | tf_op jit(solution)/shard_map/ppermute | solution.py:384
  12.4 3.2 %collective-permute-start.4 = (f32[17,8,128]{2,1,0:T(8,128)S(1)}, f32[17,8,128]{2,1,0:T(8,128)S(1)}, u32[]{:S(2)}, u32[]{:S(2)}) collective-permute-start(f32[17,8,128]{2,1,0:T(8,128)S(1)} %group.1.order.p0), channel_id=1, source_target_pairs={{0,2},{1,3},{2,0},{3,1},{4,6},{5,7},{6,4},{7,5},{8,10},{9,11},{10,... | collective-permute-start | bytes 208904 | tf_op jit(solution)/shard_map/ppermute | solution.py:384
  15.6 0.0 collective-permute-start.5
  15.6 0.0 slice-done
  15.6 0.0 slice-done.1
  15.6 2.5 %near.2 = (f32[92,8,128]{2,1,0:T(8,128)S(1)}, f32[92,8,128]{2,1,0:T(8,128)S(1)}, f32[92,8,128]{2,1,0:T(8,128)S(1)}) custom-call(bf16[32,8,128]{2,1,0:T(8,128)(2,1)} %src_hbm.3, s32[8,32]{1,0:T(8,128)} %bitcast.4, bf16[256,128,128]{2,1,0:T(8,128)(2,1)S(1)} %bitcast.3, f32[60,8,128]{2,1,0:T(8,128)S(1)} %get-tuple-element.19.far_prev, ...), custom_call_target="tpu_custom_call" | custom-call | flops 4000000000 | tf_op jit(solution)/shard_map/near/pallas_call | solution.py:370
  18.2 0.0 collective-permute-done.3.p1
  18.2 0.4 collective-permute-done.4.p2
  18.6 1.3 %collective-permute-done.5.p3 = f32[17,8,128]{2,1,0:T(8,128)S(1)} collective-permute-done((f32[17,8,128]{2,1,0:T(8,128)S(1)}, f32[17,8,128]{2,1,0:T(8,128)S(1)}, u32[]{:S(2)}, u32[]{:S(2)}) %collective-permute-start.5) | collective-permute-done | bytes 69664 | tf_op jit(solution)/shard_map/ppermute | solution.py:384
  19.9 1.3 %pack.1 = (f32[64,8,128]{2,1,0:T(8,128)S(1)}, f32[64,8,128]{2,1,0:T(8,128)S(1)}) custom-call(f32[17,8,128]{2,1,0:T(8,128)S(1)} %group.1.order.p0, f32[17,8,128]{2,1,0:T(8,128)S(1)} %collective-permute-done.3.p1, f32[17,8,128]{2,1,0:T(8,128)S(1)} %collective-permute-done.4.p2, f32[17,8,128]{2,1,0:T(8,128)S(1)} %collective-permute-done.5.p3, ...), custom_call_target="tpu_custom_call" | custom-call | tf_op jit(solution)/shard_map/pack/pallas_call | solution.py:370
  21.2 0.1 collective-permute-start.6
  21.3 0.4 collective-permute-start.7
  21.7 7.3 %collective-permute-start.8 = (f32[92,8,128]{2,1,0:T(8,128)S(1)}, f32[92,8,128]{2,1,0:T(8,128)S(1)}, u32[]{:S(2)}, u32[]{:S(2)}) collective-permute-start(f32[92,8,128]{2,1,0:T(8,128)S(1)} %get-tuple-element.26), channel_id=1, source_target_pairs={{0,127},{1,0},{2,1},{3,2},{4,3},{5,4},{6,5},{7,6},{8,7},{9,8},{10,... | collective-permute-start | bytes 1130504 | tf_op jit(solution)/shard_map/ppermute | solution.py:367
  29.0 0.0 collective-permute-done.6.core_ref
  29.0 0.7 %core.1 = f32[16,4,8,128]{3,2,1,0:T(8,128)} custom-call(f32[64,8,128]{2,1,0:T(8,128)S(1)} %get-tuple-element.23.keep_ref, f32[64,8,128]{2,1,0:T(8,128)S(1)} %collective-permute-done.6.core_ref), custom_call_target="tpu_custom_call" | custom-call | tf_op jit(solution)/shard_map/core/pallas_call | solution.py:370
  29.7 4.3 %all-to-all-start = ((f32[16,4,8,128]{3,2,1,0:T(8,128)}), f32[16,4,8,128]{3,2,1,0:T(8,128)S(1)}, u32[]{:S(2)}, u32[]{:S(2)}) async-start(f32[16,4,8,128]{3,2,1,0:T(8,128)} %core.1), calls=%async_computation | async-start | bytes 524288 | tf_op jit(solution)/shard_map/all_to_all | solution.py:428
  34.0 2.4 %collective-permute-done.7.prev = f32[92,8,128]{2,1,0:T(8,128)S(1)} collective-permute-done((f32[92,8,128]{2,1,0:T(8,128)S(1)}, f32[92,8,128]{2,1,0:T(8,128)S(1)}, u32[]{:S(2)}, u32[]{:S(2)}) %collective-permute-start.7) | collective-permute-done | bytes 376864 | tf_op jit(solution)/shard_map/ppermute | solution.py:367
  36.4 0.0 collective-permute-done.8.after
  36.4 6.1 %all-to-all-done.top = f32[16,4,8,128]{3,2,1,0:T(8,128)S(1)} async-done(((f32[16,4,8,128]{3,2,1,0:T(8,128)}), f32[16,4,8,128]{3,2,1,0:T(8,128)S(1)}, u32[]{:S(2)}, u32[]{:S(2)}) %all-to-all-start) | async-done | bytes 262176 | tf_op jit(solution)/shard_map/all_to_all | solution.py:428
  42.5 3.8 %downward.1 = f32[32,8,128]{2,1,0:T(8,128)} custom-call(f32[16,4,8,128]{3,2,1,0:T(8,128)S(1)} %all-to-all-done.top, f32[92,8,128]{2,1,0:T(8,128)S(1)} %get-tuple-element.22.order.own, f32[92,8,128]{2,1,0:T(8,128)S(1)} %collective-permute-done.7.prev, f32[92,8,128]{2,1,0:T(8,128)S(1)} %collective-permute-done.8.after, bf16[63,128,128]{2,1,0:T(8,128)(2,1)} %down_hbm.1, ...), custom_call_target="tpu_custom_call" | custom-call | tf_op jit(solution)/shard_map/downward/pallas_call | solution.py:370
  (1 shorter events, 0.0 us)
Async XLA Ops:
  0.0 9.2 %copy-start = (bf16[240,128,128]{2,1,0:T(8,128)(2,1)S(1)}, bf16[240,128,128]{2,1,0:T(8,128)(2,1)}, u32[]{:S(2)}) copy-start(bf16[240,128,128]{2,1,0:T(8,128)(2,1)} %far.3) | copy-start | bytes 23592964
  0.0 15.6 %slice-start = ((s8[8388608]{0:T(1024)(128)(4,1)}), s8[4194304]{0:T(1024)(128)(4,1)S(1)}, s32[]{:S(2)}) async-start(s8[8388608]{0:T(1024)(128)(4,1)} %bitcast.2), calls=%async_computation.1 | async-start | bytes 8388608
  3.3 8.3 %copy-start.1 = (bf16[4,128,128]{2,1,0:T(8,128)(2,1)S(1)}, bf16[4,128,128]{2,1,0:T(8,128)(2,1)}, u32[]{:S(2)}) copy-start(bf16[4,128,128]{2,1,0:T(8,128)(2,1)} %blocks.1) | copy-start | bytes 393220
  3.3 8.3 %copy-start.2 = (s32[1,4]{1,0:T(1,128)S(1)}, s32[1,4]{1,0:T(1,128)}, u32[]{:S(2)}) copy-start(s32[1,4]{1,0:T(1,128)} %group_list.1) | copy-start | bytes 52
  3.4 8.3 %collective-permute-start = (f32[8,128]{1,0:T(8,128)S(1)}, f32[8,128]{1,0:T(8,128)S(1)}, u32[]{:S(2)}, u32[]{:S(2)}) collective-permute-start(f32[8,128]{1,0:T(8,128)S(1)} %get-tuple-element.16.g0.order), channel_id=1, source_target_pairs={{0,1},{1,2},{2,3},{3,0},{4,5},{5,6},{6,7},{7,4},{8,9},{9,10},{10,1... | collective-permute-start | bytes 12296 | tf_op jit(solution)/shard_map/ppermute | solution.py:384
  5.0 6.6 %collective-permute-start.1 = (f32[8,128]{1,0:T(8,128)S(1)}, f32[8,128]{1,0:T(8,128)S(1)}, u32[]{:S(2)}, u32[]{:S(2)}) collective-permute-start(f32[8,128]{1,0:T(8,128)S(1)} %get-tuple-element.16.g0.order), channel_id=1, source_target_pairs={{0,2},{1,3},{2,0},{3,1},{4,6},{5,7},{6,4},{7,5},{8,10},{9,11},{10,... | collective-permute-start | bytes 12296 | tf_op jit(solution)/shard_map/ppermute | solution.py:384
  7.7 3.9 %collective-permute-start.2 = (f32[8,128]{1,0:T(8,128)S(1)}, f32[8,128]{1,0:T(8,128)S(1)}, u32[]{:S(2)}, u32[]{:S(2)}) collective-permute-start(f32[8,128]{1,0:T(8,128)S(1)} %get-tuple-element.16.g0.order), channel_id=1, source_target_pairs={{0,3},{1,0},{2,1},{3,2},{4,7},{5,4},{6,5},{7,6},{8,11},{9,8},{10,9... | collective-permute-start | bytes 12296 | tf_op jit(solution)/shard_map/ppermute | solution.py:384
  9.2 6.5 %slice-start.1 = ((s8[8388608]{0:T(1024)(128)(4,1)}), s8[4194304]{0:T(1024)(128)(4,1)S(1)}, s32[]{:S(2)}) async-start(s8[8388608]{0:T(1024)(128)(4,1)} %bitcast.2), calls=%async_computation.2 | async-start | bytes 8388608
  11.8 6.4 %collective-permute-start.3 = (f32[17,8,128]{2,1,0:T(8,128)S(1)}, f32[17,8,128]{2,1,0:T(8,128)S(1)}, u32[]{:S(2)}, u32[]{:S(2)}) collective-permute-start(f32[17,8,128]{2,1,0:T(8,128)S(1)} %group.1.order.p0), channel_id=1, source_target_pairs={{0,1},{1,2},{2,3},{3,0},{4,5},{5,6},{6,7},{7,4},{8,9},{9,10},{10,1... | collective-permute-start | bytes 208904 | tf_op jit(solution)/shard_map/ppermute | solution.py:384
  12.4 6.2 %collective-permute-start.4 = (f32[17,8,128]{2,1,0:T(8,128)S(1)}, f32[17,8,128]{2,1,0:T(8,128)S(1)}, u32[]{:S(2)}, u32[]{:S(2)}) collective-permute-start(f32[17,8,128]{2,1,0:T(8,128)S(1)} %group.1.order.p0), channel_id=1, source_target_pairs={{0,2},{1,3},{2,0},{3,1},{4,6},{5,7},{6,4},{7,5},{8,10},{9,11},{10,... | collective-permute-start | bytes 208904 | tf_op jit(solution)/shard_map/ppermute | solution.py:384
  15.6 4.3 %collective-permute-start.5 = (f32[17,8,128]{2,1,0:T(8,128)S(1)}, f32[17,8,128]{2,1,0:T(8,128)S(1)}, u32[]{:S(2)}, u32[]{:S(2)}) collective-permute-start(f32[17,8,128]{2,1,0:T(8,128)S(1)} %group.1.order.p0), channel_id=1, source_target_pairs={{0,3},{1,0},{2,1},{3,2},{4,7},{5,4},{6,5},{7,6},{8,11},{9,8},{10,9... | collective-permute-start | bytes 208904 | tf_op jit(solution)/shard_map/ppermute | solution.py:384
  21.2 7.8 %collective-permute-start.6 = (f32[64,8,128]{2,1,0:T(8,128)S(1)}, f32[64,8,128]{2,1,0:T(8,128)S(1)}, u32[]{:S(2)}, u32[]{:S(2)}) collective-permute-start(f32[64,8,128]{2,1,0:T(8,128)S(1)} %get-tuple-element.24), channel_id=1, source_target_pairs={{0,4},{4,0},{8,12},{12,8},{16,20},{20,16},{24,28},{28,24},{32,36},... | collective-permute-start | bytes 786440 | tf_op jit(solution)/shard_map/ppermute | solution.py:384
  21.3 15.1 %collective-permute-start.7 = (f32[92,8,128]{2,1,0:T(8,128)S(1)}, f32[92,8,128]{2,1,0:T(8,128)S(1)}, u32[]{:S(2)}, u32[]{:S(2)}) collective-permute-start(f32[92,8,128]{2,1,0:T(8,128)S(1)} %get-tuple-element.25), channel_id=1, source_target_pairs={{0,1},{1,2},{2,3},{3,4},{4,5},{5,6},{6,7},{7,8},{8,9},{9,10},{10,1... | collective-permute-start | bytes 1130504 | tf_op jit(solution)/shard_map/ppermute | solution.py:367
  21.7 14.8 %collective-permute-start.8 = (f32[92,8,128]{2,1,0:T(8,128)S(1)}, f32[92,8,128]{2,1,0:T(8,128)S(1)}, u32[]{:S(2)}, u32[]{:S(2)}) collective-permute-start(f32[92,8,128]{2,1,0:T(8,128)S(1)} %get-tuple-element.26), channel_id=1, source_target_pairs={{0,127},{1,0},{2,1},{3,2},{4,3},{5,4},{6,5},{7,6},{8,7},{9,8},{10,... | collective-permute-start | bytes 1130504 | tf_op jit(solution)/shard_map/ppermute | solution.py:367
  29.7 12.8 %all-to-all-start = ((f32[16,4,8,128]{3,2,1,0:T(8,128)}), f32[16,4,8,128]{3,2,1,0:T(8,128)S(1)}, u32[]{:S(2)}, u32[]{:S(2)}) async-start(f32[16,4,8,128]{3,2,1,0:T(8,128)} %core.1), calls=%async_computation | async-start | bytes 524288 | tf_op jit(solution)/shard_map/all_to_all | solution.py:428

commit v2 on v1

--- a/solution.py
+++ b/solution.py
@@ -173,35 +173,35 @@
 
 
 def store_totals(accs, span, refs):
-    for i, ref in enumerate(refs):
-        parts = [acc[pl.ds(i * span, span)] for acc in accs]
+    odd = lax.axis_index("sub") & 1
+    for first, ref in zip((2 - 2 * odd, 1, 2 * odd), refs):
+        parts = [acc[pl.ds(first * span, span)] for acc in accs]
         ref[0:span] = (parts[0] + parts[1]) + (parts[2] + parts[3])
 
 
 def near_kernel(
-    src_hbm, list_hbm, near, far_prev, far_own, far_next, order,
-    prev_ref, own_ref, next_ref, src_ref, near_list, a0, a1, a2, a3, sem,
+    src_ref, list_hbm, near, far_a, far_own, far_b, order,
+    a_ref, own_ref, b_ref, near_list, a0, a1, a2, a3, sem,
 ):
     leaves = src_ref.shape[0]
     slots = near_list.shape[0]
     fetch = Fetches(sem)
-    first = [fetch(list_hbm, near_list), fetch(src_hbm, src_ref)]
+    first = fetch(list_hbm, near_list)
     accs = (a0, a1, a2, a3)
     for acc in accs:
         acc[...] = jnp.zeros(acc.shape, F32)
-    for out, part in ((prev_ref, far_prev), (own_ref, far_own), (next_ref, far_next)):
+    for out, part in ((a_ref, far_a), (own_ref, far_own), (b_ref, far_b)):
         out[leaves:] = part[...]
-    for c in first:
-        c.wait()
+    first.wait()
     scatter_steps(
         lambda t: src_ref[t].astype(F32), near, lambda t, k: near_list[k, t], accs,
         slots, 0, leaves, 8, 0, leaves.bit_length() - 1, 0, leaves,
     )
-    store_totals(accs, leaves, (prev_ref, own_ref, next_ref))
+    store_totals(accs, leaves, (a_ref, own_ref, b_ref))
 
 
 def far_kernel(
-    leaves, coef_ref, list_hbm, far, order, prev_ref, own_ref, next_ref, far_list, a0, a1, a2, a3, sem,
+    leaves, coef_ref, list_hbm, far, order, a_ref, own_ref, b_ref, far_list, a0, a1, a2, a3, sem,
 ):
     levels = leaves.bit_length() - 1
     slots, nodes = far_list.shape
@@ -217,7 +217,7 @@
             lambda t: coef_ref[t], far, lambda t, k: far_list[k, t], accs,
             slots, offset, leaves >> level, min(16, leaves >> level), level, levels, offset, nodes,
         )
-    store_totals(accs, nodes, (prev_ref, own_ref, next_ref))
+    store_totals(accs, nodes, (a_ref, own_ref, b_ref))
 
 
 def group_kernel(g0, g1, g2, g3, top_ref, group_list, blocks, out_ref):
@@ -233,7 +233,7 @@
     out_ref[TERMS, 3:4, 0:4] = group_list[...].astype(F32)
 
 
-def pack_kernel(p0, p1, p2, p3, order, keep_ref, send_ref, ids, a0, a1, a2, a3, sem):
+def pack_kernel(p0, p1, p2, p3, to_a, to_b, keep_ref, send_ref, held_a, held_b, ids, a0, a1, a2, a3, sem):
     half = keep_ref.shape[0]
     parts = (p0, p1, p2, p3)
     accs = (a0, a1, a2, a3)
@@ -276,27 +276,27 @@
     send_ref[...] = total((1 - own_core) * half)
 
 
-def core_kernel(keep_ref, core_ref, out_ref):
-    out_ref[...] = (keep_ref[...] + core_ref[...]).reshape(out_ref.shape)
-
-
-def down_kernel(top, own, prev, after, down_hbm, col_hbm, out_ref, down, col, level_down, sem):
+def split_kernel(unit, *refs):
+    parts, outs = refs[:-4], refs[-4:]
+    rows = outs[0].shape[0]
+    own = (lax.axis_index("leaf") // unit) & 3
+    for digit, out in enumerate(outs):
+        part = pl.ds((own ^ digit) * rows, rows)
+        total = parts[0][part]
+        for p in parts[1:]:
+            total = total + p[part]
+        out[...] = total
+
+
+def down_kernel(t0, t1, t2, t3, own, from_a, from_b, down, col, out_ref, level_down):
     leaves = out_ref.shape[0]
     levels = leaves.bit_length() - 1
-    quarter = leaves // 4
     n, m = out_ref.shape[1:]
-    fetch = Fetches(sem)
-    rest = fetch.rows(down_hbm, down, leaves, leaves - 1)
-    down_copies = [fetch.rows(down_hbm, down, i * quarter, quarter) for i in range(4)]
-    col_copies = [fetch.rows(col_hbm, col, i * quarter, quarter) for i in range(4)]
 
     def total(i):
-        return (own[i] + prev[i]) + after[i]
-
-    fields = top[0]
-    for i in range(1, top.shape[0]):
-        fields = fields + top[i]
-    rest.wait()
+        return (own[i] + from_a[i]) + from_b[i]
+
+    fields = (t0[...] + t1[...]) + (t2[...] + t3[...])
     root = 2 * leaves - 2
     level_down[root] = rounded(fields[2] + exact_dot(exact_parts(fields[3]), down[root]))
     out = dot(level_down[root], jnp.concatenate([down[root - 2], down[root - 1]], axis=1))
@@ -306,8 +306,6 @@
         width = leaves >> level
         offset = level_offset(leaves, level)
         for t in range(0, width, 4):
-            if level == 0 and t % quarter == 0:
-                down_copies[t // quarter].wait()
             a = offset + t
             parent = offset + width + t // 2
             left = diagonal(level_down[parent], level_down[parent + 1])
@@ -316,8 +314,6 @@
             for i in range(4):
                 level_down[a + i] = rounded(total(leaves + a + i) + outs[i])
     for t in range(0, leaves, 4):
-        if t % quarter == 0:
-            col_copies[t // quarter].wait()
         span = range(t, t + 4)
         outs = quad([level_down[i] for i in span], [col[i] for i in span])
         for i, out in zip(span, outs):
@@ -336,9 +332,7 @@
     far_blocks, far_list, upper_blocks, upper_list, root_blocks, root_list, group_blocks, group_list,
 ):
     in_hbm = functools.partial(pltpu.with_memory_space_constraint, memory_space=pltpu.HBM)
-    sources, row_basis, col_basis, up_transfer, down_transfer = map(
-        in_hbm, (sources, row_basis, col_basis, up_transfer, down_transfer)
-    )
+    up_sources, row_basis, up_transfer = map(in_hbm, (sources, row_basis, up_transfer))
     near_list, far_list, upper_blocks, upper_list, root_blocks, root_list = map(
         in_hbm, (near_list.T, far_list.T, upper_blocks, upper_list, root_blocks, root_list)
     )
@@ -363,32 +357,36 @@
     def copies(count):
         return pltpu.SemaphoreType.DMA((count,))
 
-    def around(x, axis, size, shift):
-        return lax.ppermute(x, axis, [(i, (i + shift) % size) for i in range(size)])
-
-    def call(kernel, name, us, outs, operands, specs, scratch):
+    def call(kernel, name, us, outs, operands, specs, scratch, out_specs=None, **options):
         return pl.pallas_call(
             kernel,
             out_shape=outs,
             in_specs=specs,
-            out_specs=jax.tree.map(lambda _: VMEM, outs),
+            out_specs=out_specs or jax.tree.map(lambda _: VMEM, outs),
             scratch_shapes=scratch,
             compiler_params=PARAMS,
             cost_estimate=cost(us),
             name=name,
+            **options,
         )(*operands)
 
     accumulators = lambda count: [plane(3 * count + 1)] * REPLICAS
 
     def permuted(x, axis, target):
-        return lax.ppermute(x, axis, [(i, target(i)) for i in range(lax.axis_size(axis))])
+        count = lax.axis_size(axis)
+        return lax.ppermute(x, axis, [(i, target(i)) for i in range(count)])
 
     def gathered(x):
-        return [x] + [permuted(x, "sub", lambda i, s=s: (i + s) % subs) for s in range(1, subs)]
+        return [x] + [permuted(x, "sub", lambda i, s=s: i ^ s) for s in range(1, subs)]
+
+    def exchanged(parts, unit):
+        return parts[:1] + tuple(
+            permuted(x, "leaf", lambda i, s=s: i ^ (s * unit)) for s, x in enumerate(parts[1:], 1)
+        )
 
     coef, group, top = call(
         up_kernel, "upward", 4, (shape(nodes), shape(), shape(TOP_TERMS + 1)),
-        (sources, upper_list, root_list, row_basis, up_transfer, upper_blocks, root_blocks),
+        (up_sources, upper_list, root_list, row_basis, up_transfer, upper_blocks, root_blocks),
         [ANY] * 7,
         [
             pltpu.VMEM((leaves,) + row, BF16),
@@ -397,7 +395,7 @@
         ],
     )
     group_parts = gathered(group)
-    far_prev, far_own, far_next = call(
+    far_a, far_own, far_b = call(
         functools.partial(far_kernel, leaves), "far", 4, (shape(far_nodes),) * 3,
         (coef, far_list, far_blocks, group),
         [VMEM, ANY, VMEM, ANY],
@@ -408,30 +406,34 @@
         [VMEM] * 7, [],
     )
     term_parts = gathered(terms)
-    to_prev, own, to_next = call(
+    to_a, own, to_b = call(
         near_kernel, "near", 4, (shape(leaves + far_nodes),) * 3,
-        (sources, near_list, near_blocks, far_prev, far_own, far_next, terms),
-        [ANY, ANY, VMEM, VMEM, VMEM, VMEM, ANY],
-        [pltpu.VMEM((leaves,) + row, BF16), pltpu.SMEM((near_slots, leaves), jnp.int32)]
-        + accumulators(leaves) + [copies(2)],
-    )
-    from_prev = around(to_next, ("leaf", "sub"), devices, 1)
-    from_next = around(to_prev, ("leaf", "sub"), devices, -1)
-
+        (sources, near_list, near_blocks, far_a, far_own, far_b, terms),
+        [VMEM, ANY, VMEM, VMEM, VMEM, VMEM, ANY],
+        [pltpu.SMEM((near_slots, leaves), jnp.int32)] + accumulators(leaves) + [copies(1)],
+    )
     half = groups // 2 * 4
-    keep, send = call(
-        pack_kernel, "pack", 0, (shape(half), shape(half)), (*term_parts, own), [VMEM] * 4 + [ANY],
-        [pltpu.SMEM((subs,) + row, F32)] + [plane(2 * half + 1)] * 4 + [copies(subs)],
-    )
+    window = shape(leaves + far_nodes)
+    keep, send, to_a, to_b = call(
+        pack_kernel, "pack", 0, (shape(half), shape(half), window, window), (*term_parts, to_a, to_b),
+        [VMEM] * 4 + [ANY] * 2, [pltpu.SMEM((subs,) + row, F32)] + [plane(2 * half + 1)] * 4 + [copies(subs)],
+        out_specs=(VMEM, VMEM, ANY, ANY), input_output_aliases={4: 2, 5: 3},
+    )
+    everyone = ("leaf", "sub")
+    from_a = permuted(to_a, everyone, lambda i: i ^ 1)
+    from_b = permuted(to_b, everyone, lambda i: min(max(((i + 1) ^ 1) - 1, 0), devices - 1))
     from_core = permuted(send, "leaf", lambda i: i ^ 1)
-    planes = call(core_kernel, "core", 0, shape(groups // 2, 4), (keep, from_core), [VMEM] * 2, [])
-    fields = lax.all_to_all(
-        planes, "leaf", 0, 0, tiled=True, axis_index_groups=[list(range(c, groups, 2)) for c in range(2)]
+    y_unit, z_unit = groups // 4, groups // 16
+    by_y = call(
+        functools.partial(split_kernel, y_unit), "split_y", 1, (shape(half // 4),) * 4, (keep, from_core), [VMEM] * 2, []
+    )
+    by_z = call(
+        functools.partial(split_kernel, z_unit), "split_z", 0, (shape(half // 16),) * 4,
+        exchanged(by_y, y_unit), [VMEM] * 4, [],
     )
     return call(
         down_kernel, "downward", 0, shape(leaves),
-        (fields, own, from_prev, from_next, down_transfer, col_basis), [VMEM] * 4 + [ANY] * 2,
-        [buffer(nodes), buffer(leaves), plane(nodes), copies(9)],
+        (*exchanged(by_z, z_unit), own, from_a, from_b, down_transfer, col_basis), [VMEM] * 9, [plane(nodes)],
     )
 
 

time: 46.6 us -> 48.4 us (1.039)
  starting transfers between devices: 21.7 us -> 25.7 us
  Pallas kernels: 14.2 us -> 11.5 us
  waiting for transfers between devices: 10.2 us -> 11 us
    ppermute x9 -> x15, starting transfers between devices: 17.4 us -> 25.7 us  [permuted(): return lax.ppermute(x, axis, [(i, target(i)) for i in range(count)])]
    ppermute x9 -> x15, waiting for transfers between devices: 4.14 us -> 11 us  [permuted(): return lax.ppermute(x, axis, [(i, target(i)) for i in range(count)])]
    all_to_all x1 -> x0, waiting for transfers between devices: 6.1 us -> none  [shards(): lax.all_to_all(planes, 'leaf', 0, 0, tiled=True, axis_index_groups=[list(...]
    all_to_all x1 -> x0, starting transfers between devices: 4.26 us -> none  [shards(): lax.all_to_all(planes, 'leaf', 0, 0, tiled=True, axis_index_groups=[list(...]
    pallas_call x7 -> x8, Pallas kernels: 14.2 us -> 11.5 us  [call(): pl.pallas_call(kernel, out_shape=outs, in_specs=specs, out_specs=out_spec...]
  transfers between devices with their start and end apart: 10 -> 15, of which waited for: 4 -> 6; matrix products, arithmetic and copies ran while one was open for 0% -> 0% of each run, Pallas kernels for 12% -> 10%
where the time goes in v2:
time: 48.4 us; the launch traced here: 48.3 us
  starting transfers between devices  25.7 us (53%)
  Pallas kernels  11.5 us (24%)
  waiting for transfers between devices  11 us (23%)
    ppermute x15, starting transfers between devices, permuted(): return lax.ppermute(x, axis, [(i, target(i)) for i in range(count)])  25.7 us
    pallas_call x8, Pallas kernels, call(): pl.pallas_call(kernel, out_shape=outs, in_specs=specs, out_specs=out_spec...  11.5 us
    ppermute x15, waiting for transfers between devices, permuted(): return lax.ppermute(x, axis, [(i, target(i)) for i in range(count)])  11 us
  transfers between devices with their start and end apart: 15, of which 6 were waited for; matrix products, arithmetic and copies ran while one was open for 0% of the time, Pallas kernels for 10%

profile of v2, /device:TPU:0, one launch (start us, length us, event | category | flops | bytes accessed | tf_op | source)
XLA Modules:
  0.0 48.3 jit_solution(15722194758108604143)
XLA Ops:
  0.0 3.3 %upward.1 = (f32[63,8,128]{2,1,0:T(8,128)S(1)}, f32[8,128]{1,0:T(8,128)S(1)}, f32[13,8,128]{2,1,0:T(8,128)S(1)}) custom-call(bf16[32,8,128]{2,1,0:T(8,128)(2,1)} %src_ref.1, s32[2,4]{1,0:T(2,128)} %upper_list_hbm.1, s32[1,4]{1,0:T(1,128)} %root_list_hbm.1, bf16[32,128,128]{2,1,0:T(8,128)(2,1)} %rb_hbm.1, bf16[63,128,128]{2,1,0:T(8,128)(2,1)} %up_hbm.1, ...), custom_call_target="tpu_custom_call" | custom-call | flops 4000000000 | tf_op jit(solution)/shard_map/upward/pallas_call | solution.py:361
  3.3 0.0 copy-start.3
  3.3 0.0 copy-start.5
  3.4 2.9 %collective-permute-start.2 = (f32[8,128]{1,0:T(8,128)S(1)}, f32[8,128]{1,0:T(8,128)S(1)}, u32[]{:S(2)}, u32[]{:S(2)}) collective-permute-start(f32[8,128]{1,0:T(8,128)S(1)} %get-tuple-element.26.g0.order), channel_id=1, source_target_pairs={{0,3},{1,2},{2,1},{3,0},{4,7},{5,6},{6,5},{7,4},{8,11},{9,10},{10,... | collective-permute-start | bytes 12296 | tf_op jit(solution)/shard_map/ppermute | solution.py:377
  6.3 0.8 %collective-permute-start.1 = (f32[8,128]{1,0:T(8,128)S(1)}, f32[8,128]{1,0:T(8,128)S(1)}, u32[]{:S(2)}, u32[]{:S(2)}) collective-permute-start(f32[8,128]{1,0:T(8,128)S(1)} %get-tuple-element.26.g0.order), channel_id=1, source_target_pairs={{0,2},{1,3},{2,0},{3,1},{4,6},{5,7},{6,4},{7,5},{8,10},{9,11},{10,... | collective-permute-start | bytes 12296 | tf_op jit(solution)/shard_map/ppermute | solution.py:377
  7.1 0.5 collective-permute-start
  7.5 0.0 copy-done.2
  7.5 2.4 %far.2 = (f32[60,8,128]{2,1,0:T(8,128)S(1)}, f32[60,8,128]{2,1,0:T(8,128)S(1)}, f32[60,8,128]{2,1,0:T(8,128)S(1)}) custom-call(f32[63,8,128]{2,1,0:T(8,128)S(1)} %get-tuple-element.28.coef_ref, s32[4,60]{1,0:T(4,128)} %bitcast.5, bf16[240,128,128]{2,1,0:T(8,128)(2,1)S(1)} %copy-done.2, f32[8,128]{1,0:T(8,128)S(1)} %get-tuple-element.26.g0.order), custom_call_target="tpu_custom_call" | custom-call | flops 4000000000 | tf_op jit(solution)/shard_map/far/pallas_call | solution.py:361
  10.0 0.0 collective-permute-done.2.g3
  10.0 1.4 %collective-permute-done.1.g2 = f32[8,128]{1,0:T(8,128)S(1)} collective-permute-done((f32[8,128]{1,0:T(8,128)S(1)}, f32[8,128]{1,0:T(8,128)S(1)}, u32[]{:S(2)}, u32[]{:S(2)}) %collective-permute-start.1) | collective-permute-done | bytes 4128 | tf_op jit(solution)/shard_map/ppermute | solution.py:377
  11.4 0.0 collective-permute-done.g1
  11.4 0.0 copy-done.3
  11.4 0.0 copy-done.5
  11.4 0.1 group.1.order.p0
  11.5 1.5 %collective-permute-start.5 = (f32[17,8,128]{2,1,0:T(8,128)S(1)}, f32[17,8,128]{2,1,0:T(8,128)S(1)}, u32[]{:S(2)}, u32[]{:S(2)}) collective-permute-start(f32[17,8,128]{2,1,0:T(8,128)S(1)} %group.1.order.p0), channel_id=1, source_target_pairs={{0,3},{1,2},{2,1},{3,0},{4,7},{5,6},{6,5},{7,4},{8,11},{9,10},{10,... | collective-permute-start | bytes 208904 | tf_op jit(solution)/shard_map/ppermute | solution.py:377
  13.0 0.8 %collective-permute-start.4 = (f32[17,8,128]{2,1,0:T(8,128)S(1)}, f32[17,8,128]{2,1,0:T(8,128)S(1)}, u32[]{:S(2)}, u32[]{:S(2)}) collective-permute-start(f32[17,8,128]{2,1,0:T(8,128)S(1)} %group.1.order.p0), channel_id=1, source_target_pairs={{0,2},{1,3},{2,0},{3,1},{4,6},{5,7},{6,4},{7,5},{8,10},{9,11},{10,... | collective-permute-start | bytes 208904 | tf_op jit(solution)/shard_map/ppermute | solution.py:377
  13.8 1.8 %collective-permute-start.3 = (f32[17,8,128]{2,1,0:T(8,128)S(1)}, f32[17,8,128]{2,1,0:T(8,128)S(1)}, u32[]{:S(2)}, u32[]{:S(2)}) collective-permute-start(f32[17,8,128]{2,1,0:T(8,128)S(1)} %group.1.order.p0), channel_id=1, source_target_pairs={{0,1},{1,0},{2,3},{3,2},{4,5},{5,4},{6,7},{7,6},{8,9},{9,8},{10,11... | collective-permute-start | bytes 208904 | tf_op jit(solution)/shard_map/ppermute | solution.py:377
  15.6 0.0 slice-done
  15.6 0.0 slice-done.1
  15.6 0.0 copy-done.4
  15.7 0.0 copy-start
  15.7 0.0 copy-start.1
  15.7 2.6 %near.2 = (f32[92,8,128]{2,1,0:T(8,128)S(1)}, f32[92,8,128]{2,1,0:T(8,128)S(1)}, f32[92,8,128]{2,1,0:T(8,128)S(1)}) custom-call(bf16[32,8,128]{2,1,0:T(8,128)(2,1)S(1)} %copy-done.4, s32[8,32]{1,0:T(8,128)} %bitcast.4, bf16[256,128,128]{2,1,0:T(8,128)(2,1)S(1)} %bitcast.3, f32[60,8,128]{2,1,0:T(8,128)S(1)} %get-tuple-element.29.far_a, ...), custom_call_target="tpu_custom_call" | custom-call | flops 4000000000 | tf_op jit(solution)/shard_map/near/pallas_call | solution.py:361
  18.3 0.0 collective-permute-done.5.p3
  18.3 0.6 %collective-permute-done.4.p2 = f32[17,8,128]{2,1,0:T(8,128)S(1)} collective-permute-done((f32[17,8,128]{2,1,0:T(8,128)S(1)}, f32[17,8,128]{2,1,0:T(8,128)S(1)}, u32[]{:S(2)}, u32[]{:S(2)}) %collective-permute-start.4) | collective-permute-done | bytes 69664 | tf_op jit(solution)/shard_map/ppermute | solution.py:377
  18.8 0.0 collective-permute-done.3.p1
  18.8 1.3 %pack.1 = (f32[64,8,128]{2,1,0:T(8,128)S(1)}, f32[64,8,128]{2,1,0:T(8,128)S(1)}, f32[92,8,128]{2,1,0:T(8,128)S(1)}, f32[92,8,128]{2,1,0:T(8,128)S(1)}) custom-call(f32[17,8,128]{2,1,0:T(8,128)S(1)} %group.1.order.p0, f32[17,8,128]{2,1,0:T(8,128)S(1)} %collective-permute-done.3.p1, ...), custom_call_target="tpu_custom_call", output_to_operand_aliasing={{2}: (4, {}), {3}: (5, {})} | custom-call | tf_op jit(solution)/shard_map/pack/pallas_call | solution.py:361
  20.1 0.1 collective-permute-start.6
  20.2 1.2 %collective-permute-start.13 = (f32[92,8,128]{2,1,0:T(8,128)S(1)}, f32[92,8,128]{2,1,0:T(8,128)S(1)}, u32[]{:S(2)}, u32[]{:S(2)}) collective-permute-start(f32[92,8,128]{2,1,0:T(8,128)S(1)} %get-tuple-element.45), channel_id=1, source_target_pairs={{0,1},{1,0},{2,3},{3,2},{4,5},{5,4},{6,7},{7,6},{8,9},{9,8},{10,11... | collective-permute-start | bytes 1130504 | tf_op jit(solution)/shard_map/ppermute | solution.py:377
  21.4 0.7 %collective-permute-start.14 = (f32[92,8,128]{2,1,0:T(8,128)S(1)}, f32[92,8,128]{2,1,0:T(8,128)S(1)}, u32[]{:S(2)}, u32[]{:S(2)}) collective-permute-start(f32[92,8,128]{2,1,0:T(8,128)S(1)} %get-tuple-element.46), channel_id=1, source_target_pairs={{0,0},{1,2},{2,1},{3,4},{4,3},{5,6},{6,5},{7,8},{8,7},{9,10},{10,9... | collective-permute-start | bytes 1130504 | tf_op jit(solution)/shard_map/ppermute | solution.py:377
  22.1 0.0 collective-permute-done.6.refs_1_
  22.2 7.5 %collective-permute-start.7 = (f32[16,8,128]{2,1,0:T(8,128)S(1)}, f32[16,8,128]{2,1,0:T(8,128)S(1)}, u32[]{:S(2)}, u32[]{:S(2)}) collective-permute-start(f32[16,8,128]{2,1,0:T(8,128)S(1)} %get-tuple-element.37), channel_id=1, source_target_pairs={{0,32},{4,36},{8,40},{12,44},{16,48},{20,52},{24,56},{28,60},{32,0... | collective-permute-start | bytes 196616 | tf_op jit(solution)/shard_map/ppermute | solution.py:377
  29.6 3.2 %collective-permute-start.8 = (f32[16,8,128]{2,1,0:T(8,128)S(1)}, f32[16,8,128]{2,1,0:T(8,128)S(1)}, u32[]{:S(2)}, u32[]{:S(2)}) collective-permute-start(f32[16,8,128]{2,1,0:T(8,128)S(1)} %get-tuple-element.38), channel_id=1, source_target_pairs={{0,64},{4,68},{8,72},{12,76},{16,80},{20,84},{24,88},{28,92},{32,9... | collective-permute-start | bytes 196616 | tf_op jit(solution)/shard_map/ppermute | solution.py:377
  32.8 0.0 collective-permute-start.9
  32.8 0.0 collective-permute-done.7.refs_1_
  32.8 2.9 %collective-permute-done.8.refs_2_ = f32[16,8,128]{2,1,0:T(8,128)S(1)} collective-permute-done((f32[16,8,128]{2,1,0:T(8,128)S(1)}, f32[16,8,128]{2,1,0:T(8,128)S(1)}, u32[]{:S(2)}, u32[]{:S(2)}) %collective-permute-start.8) | collective-permute-done | bytes 65568 | tf_op jit(solution)/shard_map/ppermute | solution.py:377
  35.8 2.5 %collective-permute-done.9.refs_3_ = f32[16,8,128]{2,1,0:T(8,128)S(1)} collective-permute-done((f32[16,8,128]{2,1,0:T(8,128)S(1)}, f32[16,8,128]{2,1,0:T(8,128)S(1)}, u32[]{:S(2)}, u32[]{:S(2)}) %collective-permute-start.9) | collective-permute-done | bytes 65568 | tf_op jit(solution)/shard_map/ppermute | solution.py:377
  38.3 0.1 collective-permute-start.10
  38.4 3.3 %collective-permute-start.11 = (f32[4,8,128]{2,1,0:T(8,128)S(1)}, f32[4,8,128]{2,1,0:T(8,128)S(1)}, u32[]{:S(2)}, u32[]{:S(2)}) collective-permute-start(f32[4,8,128]{2,1,0:T(8,128)S(1)} %get-tuple-element.42), channel_id=1, source_target_pairs={{0,16},{4,20},{8,24},{12,28},{16,0},{20,4},{24,8},{28,12},{32,48},... | collective-permute-start | bytes 49160 | tf_op jit(solution)/shard_map/ppermute | solution.py:377
  41.7 1.4 %collective-permute-start.12 = (f32[4,8,128]{2,1,0:T(8,128)S(1)}, f32[4,8,128]{2,1,0:T(8,128)S(1)}, u32[]{:S(2)}, u32[]{:S(2)}) collective-permute-start(f32[4,8,128]{2,1,0:T(8,128)S(1)} %get-tuple-element.43), channel_id=1, source_target_pairs={{0,24},{4,28},{8,16},{12,20},{16,8},{20,12},{24,0},{28,4},{32,56},... | collective-permute-start | bytes 49160 | tf_op jit(solution)/shard_map/ppermute | solution.py:377
  43.1 0.0 collective-permute-done.10.t1
  43.1 0.6 %collective-permute-done.11.t2 = f32[4,8,128]{2,1,0:T(8,128)S(1)} collective-permute-done((f32[4,8,128]{2,1,0:T(8,128)S(1)}, f32[4,8,128]{2,1,0:T(8,128)S(1)}, u32[]{:S(2)}, u32[]{:S(2)}) %collective-permute-start.11) | collective-permute-done | bytes 16416 | tf_op jit(solution)/shard_map/ppermute | solution.py:377
  43.7 2.9 %collective-permute-done.12.t3 = f32[4,8,128]{2,1,0:T(8,128)S(1)} collective-permute-done((f32[4,8,128]{2,1,0:T(8,128)S(1)}, f32[4,8,128]{2,1,0:T(8,128)S(1)}, u32[]{:S(2)}, u32[]{:S(2)}) %collective-permute-start.12) | collective-permute-done | bytes 16416 | tf_op jit(solution)/shard_map/ppermute | solution.py:377
  46.6 0.0 collective-permute-done.13.from_a
  46.6 0.0 collective-permute-done.14.from_b
  46.6 0.0 copy-done
  46.6 0.0 copy-done.1
  46.6 1.7 %downward.1 = f32[32,8,128]{2,1,0:T(8,128)} custom-call(f32[4,8,128]{2,1,0:T(8,128)S(1)} %get-tuple-element.40.t0, f32[4,8,128]{2,1,0:T(8,128)S(1)} %collective-permute-done.10.t1, f32[4,8,128]{2,1,0:T(8,128)S(1)} %collective-permute-done.11.t2, f32[4,8,128]{2,1,0:T(8,128)S(1)} %collective-permute-done.12.t3, f32[92,8,128]{2,1,0:T(8,128)S(1)} %get-tuple-element.44.own, ...), custom_call_target="tpu_custom_call" | custom-call | tf_op jit(solution)/shard_map/downward/pallas_call | solution.py:361
  (7 shorter events, 0.1 us)
Async XLA Ops:
  0.0 7.5 %copy-start.2 = (bf16[240,128,128]{2,1,0:T(8,128)(2,1)S(1)}, bf16[240,128,128]{2,1,0:T(8,128)(2,1)}, u32[]{:S(2)}) copy-start(bf16[240,128,128]{2,1,0:T(8,128)(2,1)} %far.3) | copy-start | bytes 23592964
  0.0 15.6 %slice-start = ((s8[8388608]{0:T(1024)(128)(4,1)}), s8[4194304]{0:T(1024)(128)(4,1)S(1)}, s32[]{:S(2)}) async-start(s8[8388608]{0:T(1024)(128)(4,1)} %bitcast.2), calls=%async_computation | async-start | bytes 8388608
  3.3 8.1 %copy-start.3 = (bf16[4,128,128]{2,1,0:T(8,128)(2,1)S(1)}, bf16[4,128,128]{2,1,0:T(8,128)(2,1)}, u32[]{:S(2)}) copy-start(bf16[4,128,128]{2,1,0:T(8,128)(2,1)} %blocks.1) | copy-start | bytes 393220
  3.3 8.1 %copy-start.5 = (s32[1,4]{1,0:T(1,128)S(1)}, s32[1,4]{1,0:T(1,128)}, u32[]{:S(2)}) copy-start(s32[1,4]{1,0:T(1,128)} %group_list.1) | copy-start | bytes 52
  3.4 6.6 %collective-permute-start.2 = (f32[8,128]{1,0:T(8,128)S(1)}, f32[8,128]{1,0:T(8,128)S(1)}, u32[]{:S(2)}, u32[]{:S(2)}) collective-permute-start(f32[8,128]{1,0:T(8,128)S(1)} %get-tuple-element.26.g0.order), channel_id=1, source_target_pairs={{0,3},{1,2},{2,1},{3,0},{4,7},{5,6},{6,5},{7,4},{8,11},{9,10},{10,... | collective-permute-start | bytes 12296 | tf_op jit(solution)/shard_map/ppermute | solution.py:377
  6.3 5.1 %collective-permute-start.1 = (f32[8,128]{1,0:T(8,128)S(1)}, f32[8,128]{1,0:T(8,128)S(1)}, u32[]{:S(2)}, u32[]{:S(2)}) collective-permute-start(f32[8,128]{1,0:T(8,128)S(1)} %get-tuple-element.26.g0.order), channel_id=1, source_target_pairs={{0,2},{1,3},{2,0},{3,1},{4,6},{5,7},{6,4},{7,5},{8,10},{9,11},{10,... | collective-permute-start | bytes 12296 | tf_op jit(solution)/shard_map/ppermute | solution.py:377
  7.1 4.3 %collective-permute-start = (f32[8,128]{1,0:T(8,128)S(1)}, f32[8,128]{1,0:T(8,128)S(1)}, u32[]{:S(2)}, u32[]{:S(2)}) collective-permute-start(f32[8,128]{1,0:T(8,128)S(1)} %get-tuple-element.26.g0.order), channel_id=1, source_target_pairs={{0,1},{1,0},{2,3},{3,2},{4,5},{5,4},{6,7},{7,6},{8,9},{9,8},{10,11... | collective-permute-start | bytes 12296 | tf_op jit(solution)/shard_map/ppermute | solution.py:377
  7.5 8.1 %slice-start.1 = ((s8[8388608]{0:T(1024)(128)(4,1)}), s8[4194304]{0:T(1024)(128)(4,1)S(1)}, s32[]{:S(2)}) async-start(s8[8388608]{0:T(1024)(128)(4,1)} %bitcast.2), calls=%async_computation.1 | async-start | bytes 8388608
  7.5 8.1 %copy-start.4 = (bf16[32,8,128]{2,1,0:T(8,128)(2,1)S(1)}, bf16[32,8,128]{2,1,0:T(8,128)(2,1)}, u32[]{:S(2)}) copy-start(bf16[32,8,128]{2,1,0:T(8,128)(2,1)} %src_ref.1) | copy-start | bytes 196612
  11.5 6.7 %collective-permute-start.5 = (f32[17,8,128]{2,1,0:T(8,128)S(1)}, f32[17,8,128]{2,1,0:T(8,128)S(1)}, u32[]{:S(2)}, u32[]{:S(2)}) collective-permute-start(f32[17,8,128]{2,1,0:T(8,128)S(1)} %group.1.order.p0), channel_id=1, source_target_pairs={{0,3},{1,2},{2,1},{3,0},{4,7},{5,6},{6,5},{7,4},{8,11},{9,10},{10,... | collective-permute-start | bytes 208904 | tf_op jit(solution)/shard_map/ppermute | solution.py:377
  13.0 5.8 %collective-permute-start.4 = (f32[17,8,128]{2,1,0:T(8,128)S(1)}, f32[17,8,128]{2,1,0:T(8,128)S(1)}, u32[]{:S(2)}, u32[]{:S(2)}) collective-permute-start(f32[17,8,128]{2,1,0:T(8,128)S(1)} %group.1.order.p0), channel_id=1, source_target_pairs={{0,2},{1,3},{2,0},{3,1},{4,6},{5,7},{6,4},{7,5},{8,10},{9,11},{10,... | collective-permute-start | bytes 208904 | tf_op jit(solution)/shard_map/ppermute | solution.py:377
  13.8 5.0 %collective-permute-start.3 = (f32[17,8,128]{2,1,0:T(8,128)S(1)}, f32[17,8,128]{2,1,0:T(8,128)S(1)}, u32[]{:S(2)}, u32[]{:S(2)}) collective-permute-start(f32[17,8,128]{2,1,0:T(8,128)S(1)} %group.1.order.p0), channel_id=1, source_target_pairs={{0,1},{1,0},{2,3},{3,2},{4,5},{5,4},{6,7},{7,6},{8,9},{9,8},{10,11... | collective-permute-start | bytes 208904 | tf_op jit(solution)/shard_map/ppermute | solution.py:377
  15.7 31.0 %copy-start = (bf16[63,128,128]{2,1,0:T(8,128)(2,1)S(1)}, bf16[63,128,128]{2,1,0:T(8,128)(2,1)}, u32[]{:S(2)}) copy-start(bf16[63,128,128]{2,1,0:T(8,128)(2,1)} %down.1) | copy-start | bytes 6193156
  15.7 31.0 %copy-start.1 = (bf16[32,128,128]{2,1,0:T(8,128)(2,1)S(1)}, bf16[32,128,128]{2,1,0:T(8,128)(2,1)}, u32[]{:S(2)}) copy-start(bf16[32,128,128]{2,1,0:T(8,128)(2,1)} %col.1) | copy-start | bytes 3145732
  20.1 2.0 %collective-permute-start.6 = (f32[64,8,128]{2,1,0:T(8,128)S(1)}, f32[64,8,128]{2,1,0:T(8,128)S(1)}, u32[]{:S(2)}, u32[]{:S(2)}) collective-permute-start(f32[64,8,128]{2,1,0:T(8,128)S(1)} %get-tuple-element.35), channel_id=1, source_target_pairs={{0,4},{4,0},{8,12},{12,8},{16,20},{20,16},{24,28},{28,24},{32,36},... | collective-permute-start | bytes 786440 | tf_op jit(solution)/shard_map/ppermute | solution.py:377
  20.2 26.4 %collective-permute-start.13 = (f32[92,8,128]{2,1,0:T(8,128)S(1)}, f32[92,8,128]{2,1,0:T(8,128)S(1)}, u32[]{:S(2)}, u32[]{:S(2)}) collective-permute-start(f32[92,8,128]{2,1,0:T(8,128)S(1)} %get-tuple-element.45), channel_id=1, source_target_pairs={{0,1},{1,0},{2,3},{3,2},{4,5},{5,4},{6,7},{7,6},{8,9},{9,8},{10,11... | collective-permute-start | bytes 1130504 | tf_op jit(solution)/shard_map/ppermute | solution.py:377
  21.4 25.2 %collective-permute-start.14 = (f32[92,8,128]{2,1,0:T(8,128)S(1)}, f32[92,8,128]{2,1,0:T(8,128)S(1)}, u32[]{:S(2)}, u32[]{:S(2)}) collective-permute-start(f32[92,8,128]{2,1,0:T(8,128)S(1)} %get-tuple-element.46), channel_id=1, source_target_pairs={{0,0},{1,2},{2,1},{3,4},{4,3},{5,6},{6,5},{7,8},{8,7},{9,10},{10,9... | collective-permute-start | bytes 1130504 | tf_op jit(solution)/shard_map/ppermute | solution.py:377
  22.2 10.7 %collective-permute-start.7 = (f32[16,8,128]{2,1,0:T(8,128)S(1)}, f32[16,8,128]{2,1,0:T(8,128)S(1)}, u32[]{:S(2)}, u32[]{:S(2)}) collective-permute-start(f32[16,8,128]{2,1,0:T(8,128)S(1)} %get-tuple-element.37), channel_id=1, source_target_pairs={{0,32},{4,36},{8,40},{12,44},{16,48},{20,52},{24,56},{28,60},{32,0... | collective-permute-start | bytes 196616 | tf_op jit(solution)/shard_map/ppermute | solution.py:377
  29.6 6.1 %collective-permute-start.8 = (f32[16,8,128]{2,1,0:T(8,128)S(1)}, f32[16,8,128]{2,1,0:T(8,128)S(1)}, u32[]{:S(2)}, u32[]{:S(2)}) collective-permute-start(f32[16,8,128]{2,1,0:T(8,128)S(1)} %get-tuple-element.38), channel_id=1, source_target_pairs={{0,64},{4,68},{8,72},{12,76},{16,80},{20,84},{24,88},{28,92},{32,9... | collective-permute-start | bytes 196616 | tf_op jit(solution)/shard_map/ppermute | solution.py:377
  32.8 5.5 %collective-permute-start.9 = (f32[16,8,128]{2,1,0:T(8,128)S(1)}, f32[16,8,128]{2,1,0:T(8,128)S(1)}, u32[]{:S(2)}, u32[]{:S(2)}) collective-permute-start(f32[16,8,128]{2,1,0:T(8,128)S(1)} %get-tuple-element.39), channel_id=1, source_target_pairs={{0,96},{4,100},{8,104},{12,108},{16,112},{20,116},{24,120},{28,124... | collective-permute-start | bytes 196616 | tf_op jit(solution)/shard_map/ppermute | solution.py:377
  38.3 4.8 %collective-permute-start.10 = (f32[4,8,128]{2,1,0:T(8,128)S(1)}, f32[4,8,128]{2,1,0:T(8,128)S(1)}, u32[]{:S(2)}, u32[]{:S(2)}) collective-permute-start(f32[4,8,128]{2,1,0:T(8,128)S(1)} %get-tuple-element.41), channel_id=1, source_target_pairs={{0,8},{4,12},{8,0},{12,4},{16,24},{20,28},{24,16},{28,20},{32,40},... | collective-permute-start | bytes 49160 | tf_op jit(solution)/shard_map/ppermute | solution.py:377
  38.4 5.3 %collective-permute-start.11 = (f32[4,8,128]{2,1,0:T(8,128)S(1)}, f32[4,8,128]{2,1,0:T(8,128)S(1)}, u32[]{:S(2)}, u32[]{:S(2)}) collective-permute-start(f32[4,8,128]{2,1,0:T(8,128)S(1)} %get-tuple-element.42), channel_id=1, source_target_pairs={{0,16},{4,20},{8,24},{12,28},{16,0},{20,4},{24,8},{28,12},{32,48},... | collective-permute-start | bytes 49160 | tf_op jit(solution)/shard_map/ppermute | solution.py:377
  41.7 4.9 %collective-permute-start.12 = (f32[4,8,128]{2,1,0:T(8,128)S(1)}, f32[4,8,128]{2,1,0:T(8,128)S(1)}, u32[]{:S(2)}, u32[]{:S(2)}) collective-permute-start(f32[4,8,128]{2,1,0:T(8,128)S(1)} %get-tuple-element.43), channel_id=1, source_target_pairs={{0,24},{4,28},{8,16},{12,20},{16,8},{20,12},{24,0},{28,4},{32,56},... | collective-permute-start | bytes 49160 | tf_op jit(solution)/shard_map/ppermute | solution.py:377

commit v3 on v1

--- a/solution.py
+++ b/solution.py
@@ -179,20 +179,19 @@
 
 
 def near_kernel(
-    src_hbm, list_hbm, near, far_prev, far_own, far_next, order,
-    prev_ref, own_ref, next_ref, src_ref, near_list, a0, a1, a2, a3, sem,
+    src_ref, list_hbm, near, far_prev, far_own, far_next, order,
+    prev_ref, own_ref, next_ref, near_list, a0, a1, a2, a3, sem,
 ):
     leaves = src_ref.shape[0]
     slots = near_list.shape[0]
     fetch = Fetches(sem)
-    first = [fetch(list_hbm, near_list), fetch(src_hbm, src_ref)]
+    first = fetch(list_hbm, near_list)
     accs = (a0, a1, a2, a3)
     for acc in accs:
         acc[...] = jnp.zeros(acc.shape, F32)
     for out, part in ((prev_ref, far_prev), (own_ref, far_own), (next_ref, far_next)):
         out[leaves:] = part[...]
-    for c in first:
-        c.wait()
+    first.wait()
     scatter_steps(
         lambda t: src_ref[t].astype(F32), near, lambda t, k: near_list[k, t], accs,
         slots, 0, leaves, 8, 0, leaves.bit_length() - 1, 0, leaves,
@@ -280,23 +279,21 @@
     out_ref[...] = (keep_ref[...] + core_ref[...]).reshape(out_ref.shape)
 
 
-def down_kernel(top, own, prev, after, down_hbm, col_hbm, out_ref, down, col, level_down, sem):
+def merge_kernel(own_ref, prev_ref, next_ref, out_ref):
+    out_ref[...] = (own_ref[...] + prev_ref[...]) + next_ref[...]
+
+
+def down_kernel(top, total, down, col_hbm, out_ref, col, level_down, sem):
     leaves = out_ref.shape[0]
     levels = leaves.bit_length() - 1
     quarter = leaves // 4
     n, m = out_ref.shape[1:]
     fetch = Fetches(sem)
-    rest = fetch.rows(down_hbm, down, leaves, leaves - 1)
-    down_copies = [fetch.rows(down_hbm, down, i * quarter, quarter) for i in range(4)]
     col_copies = [fetch.rows(col_hbm, col, i * quarter, quarter) for i in range(4)]
-
-    def total(i):
-        return (own[i] + prev[i]) + after[i]
 
     fields = top[0]
     for i in range(1, top.shape[0]):
         fields = fields + top[i]
-    rest.wait()
     root = 2 * leaves - 2
     level_down[root] = rounded(fields[2] + exact_dot(exact_parts(fields[3]), down[root]))
     out = dot(level_down[root], jnp.concatenate([down[root - 2], down[root - 1]], axis=1))
@@ -306,22 +303,20 @@
         width = leaves >> level
         offset = level_offset(leaves, level)
         for t in range(0, width, 4):
-            if level == 0 and t % quarter == 0:
-                down_copies[t // quarter].wait()
             a = offset + t
             parent = offset + width + t // 2
             left = diagonal(level_down[parent], level_down[parent + 1])
             out = dot(left, square(down[a], down[a + 1], down[a + 2], down[a + 3]))
             outs = (out[:n, :m], out[:n, m:], out[n:, :m], out[n:, m:])
             for i in range(4):
-                level_down[a + i] = rounded(total(leaves + a + i) + outs[i])
+                level_down[a + i] = rounded(total[leaves + a + i] + outs[i])
     for t in range(0, leaves, 4):
         if t % quarter == 0:
             col_copies[t // quarter].wait()
         span = range(t, t + 4)
         outs = quad([level_down[i] for i in span], [col[i] for i in span])
         for i, out in zip(span, outs):
-            out_ref[i] = total(i) + out
+            out_ref[i] = total[i] + out
 
 
 PARAMS = pltpu.CompilerParams(vmem_limit_bytes=24 * 1024 * 1024)
@@ -336,9 +331,7 @@
     far_blocks, far_list, upper_blocks, upper_list, root_blocks, root_list, group_blocks, group_list,
 ):
     in_hbm = functools.partial(pltpu.with_memory_space_constraint, memory_space=pltpu.HBM)
-    sources, row_basis, col_basis, up_transfer, down_transfer = map(
-        in_hbm, (sources, row_basis, col_basis, up_transfer, down_transfer)
-    )
+    up_sources, row_basis, up_transfer, col_basis = map(in_hbm, (sources, row_basis, up_transfer, col_basis))
     near_list, far_list, upper_blocks, upper_list, root_blocks, root_list = map(
         in_hbm, (near_list.T, far_list.T, upper_blocks, upper_list, root_blocks, root_list)
     )
@@ -363,32 +356,31 @@
     def copies(count):
         return pltpu.SemaphoreType.DMA((count,))
 
-    def around(x, axis, size, shift):
-        return lax.ppermute(x, axis, [(i, (i + shift) % size) for i in range(size)])
-
-    def call(kernel, name, us, outs, operands, specs, scratch):
+    def call(kernel, name, us, outs, operands, specs, scratch, out_specs=None, **options):
         return pl.pallas_call(
             kernel,
             out_shape=outs,
             in_specs=specs,
-            out_specs=jax.tree.map(lambda _: VMEM, outs),
+            out_specs=out_specs or jax.tree.map(lambda _: VMEM, outs),
             scratch_shapes=scratch,
             compiler_params=PARAMS,
             cost_estimate=cost(us),
             name=name,
+            **options,
         )(*operands)
 
     accumulators = lambda count: [plane(3 * count + 1)] * REPLICAS
 
     def permuted(x, axis, target):
-        return lax.ppermute(x, axis, [(i, target(i)) for i in range(lax.axis_size(axis))])
+        count = lax.axis_size(axis)
+        return lax.ppermute(x, axis, [(i, target(i)) for i in range(count)])
 
     def gathered(x):
-        return [x] + [permuted(x, "sub", lambda i, s=s: (i + s) % subs) for s in range(1, subs)]
+        return [x] + [permuted(x, "sub", lambda i, s=s: i ^ s) for s in range(1, subs)]
 
     coef, group, top = call(
         up_kernel, "upward", 4, (shape(nodes), shape(), shape(TOP_TERMS + 1)),
-        (sources, upper_list, root_list, row_basis, up_transfer, upper_blocks, root_blocks),
+        (up_sources, upper_list, root_list, row_basis, up_transfer, upper_blocks, root_blocks),
         [ANY] * 7,
         [
             pltpu.VMEM((leaves,) + row, BF16),
@@ -411,14 +403,16 @@
     to_prev, own, to_next = call(
         near_kernel, "near", 4, (shape(leaves + far_nodes),) * 3,
         (sources, near_list, near_blocks, far_prev, far_own, far_next, terms),
-        [ANY, ANY, VMEM, VMEM, VMEM, VMEM, ANY],
-        [pltpu.VMEM((leaves,) + row, BF16), pltpu.SMEM((near_slots, leaves), jnp.int32)]
-        + accumulators(leaves) + [copies(2)],
-    )
-    from_prev = around(to_next, ("leaf", "sub"), devices, 1)
-    from_next = around(to_prev, ("leaf", "sub"), devices, -1)
-
+        [VMEM, ANY, VMEM, VMEM, VMEM, VMEM, ANY],
+        [pltpu.SMEM((near_slots, leaves), jnp.int32)] + accumulators(leaves) + [copies(1)],
+    )
     half = groups // 2 * 4
+    everyone = ("leaf", "sub")
+    window = shape(leaves + far_nodes)
+    from_prev = permuted(to_next, everyone, lambda i: (i + 1) % devices)
+    from_next = permuted(to_prev, everyone, lambda i: (i - 1) % devices)
+    total = call(merge_kernel, "merge", 20, window, (own, from_prev, from_next), [VMEM] * 3, [])
+
     keep, send = call(
         pack_kernel, "pack", 0, (shape(half), shape(half)), (*term_parts, own), [VMEM] * 4 + [ANY],
         [pltpu.SMEM((subs,) + row, F32)] + [plane(2 * half + 1)] * 4 + [copies(subs)],
@@ -429,9 +423,8 @@
         planes, "leaf", 0, 0, tiled=True, axis_index_groups=[list(range(c, groups, 2)) for c in range(2)]
     )
     return call(
-        down_kernel, "downward", 0, shape(leaves),
-        (fields, own, from_prev, from_next, down_transfer, col_basis), [VMEM] * 4 + [ANY] * 2,
-        [buffer(nodes), buffer(leaves), plane(nodes), copies(9)],
+        down_kernel, "downward", 0, shape(leaves), (fields, total, down_transfer, col_basis), [VMEM] * 3 + [ANY],
+        [buffer(leaves), plane(nodes), copies(4)],
     )
 
 

time: 46.6 us -> 53.5 us (1.15); the launches traced: 46.3 us -> 52.4 us
  waiting for transfers between devices: 10.2 us -> 13.4 us
  starting transfers between devices: 21.7 us -> 24.3 us
    all_to_all x1, starting transfers between devices: 4.26 us -> 7.47 us  [shards(): lax.all_to_all(planes, 'leaf', 0, 0, tiled=True, axis_index_groups=[list(...]
    ppermute x9, waiting for transfers between devices: 4.14 us -> 5.78 us  [permuted(): return lax.ppermute(x, axis, [(i, target(i)) for i in range(count)])]
    all_to_all x1, waiting for transfers between devices: 6.1 us -> 7.58 us  [shards(): lax.all_to_all(planes, 'leaf', 0, 0, tiled=True, axis_index_groups=[list(...]
    ppermute x9, starting transfers between devices: 17.4 us -> 16.8 us  [permuted(): return lax.ppermute(x, axis, [(i, target(i)) for i in range(count)])]
    pallas_call x7 -> x8, Pallas kernels: 14.2 us -> 14.6 us  [call(): pl.pallas_call(kernel, out_shape=outs, in_specs=specs, out_specs=out_spec...]
  transfers between devices with their start and end apart: 10 -> 10, of which waited for: 4 -> 5; matrix products, arithmetic and copies ran while one was open for 0% -> 0% of each run, Pallas kernels for 12% -> 11%
where the time goes in v3:
time: 53.5 us; the launch traced here: 52.4 us
  starting transfers between devices  24.3 us (45%)
  Pallas kernels  14.6 us (27%)
  waiting for transfers between devices  13.4 us (25%)
    ppermute x9, starting transfers between devices, permuted(): return lax.ppermute(x, axis, [(i, target(i)) for i in range(count)])  16.8 us
    pallas_call x8, Pallas kernels, call(): pl.pallas_call(kernel, out_shape=outs, in_specs=specs, out_specs=out_spec...  14.6 us
    all_to_all x1, waiting for transfers between devices, shards(): lax.all_to_all(planes, 'leaf', 0, 0, tiled=True, axis_index_groups=[list(...  7.58 us
    all_to_all x1, starting transfers between devices, shards(): lax.all_to_all(planes, 'leaf', 0, 0, tiled=True, axis_index_groups=[list(...  7.47 us
    ppermute x9, waiting for transfers between devices, permuted(): return lax.ppermute(x, axis, [(i, target(i)) for i in range(count)])  5.78 us
  transfers between devices with their start and end apart: 10, of which 5 were waited for; matrix products, arithmetic and copies ran while one was open for 0% of the time, Pallas kernels for 11%

profile of v3, /device:TPU:0, one launch (start us, length us, event | category | flops | bytes accessed | tf_op | source)
XLA Modules:
  0.0 52.4 jit_solution(74381065149511807)
XLA Ops:
  0.0 0.0 copy-start.1
  0.0 0.0 slice-start
  0.0 3.3 %upward.1 = (f32[63,8,128]{2,1,0:T(8,128)S(1)}, f32[8,128]{1,0:T(8,128)S(1)}, f32[13,8,128]{2,1,0:T(8,128)S(1)}) custom-call(bf16[32,8,128]{2,1,0:T(8,128)(2,1)} %src_ref.1, s32[2,4]{1,0:T(2,128)} %upper_list_hbm.1, s32[1,4]{1,0:T(1,128)} %root_list_hbm.1, bf16[32,128,128]{2,1,0:T(8,128)(2,1)} %rb_hbm.1, bf16[63,128,128]{2,1,0:T(8,128)(2,1)} %up_hbm.1, ...), custom_call_target="tpu_custom_call" | custom-call | flops 4000000000 | tf_op jit(solution)/shard_map/upward/pallas_call | solution.py:360
  3.3 0.0 copy-start.2
  3.3 0.0 copy-start.4
  3.4 1.7 %collective-permute-start = (f32[8,128]{1,0:T(8,128)S(1)}, f32[8,128]{1,0:T(8,128)S(1)}, u32[]{:S(2)}, u32[]{:S(2)}) collective-permute-start(f32[8,128]{1,0:T(8,128)S(1)} %get-tuple-element.16.g0.order), channel_id=1, source_target_pairs={{0,1},{1,0},{2,3},{3,2},{4,5},{5,4},{6,7},{7,6},{8,9},{9,8},{10,11... | collective-permute-start | bytes 12296 | tf_op jit(solution)/shard_map/ppermute | solution.py:376
  5.0 2.7 %collective-permute-start.1 = (f32[8,128]{1,0:T(8,128)S(1)}, f32[8,128]{1,0:T(8,128)S(1)}, u32[]{:S(2)}, u32[]{:S(2)}) collective-permute-start(f32[8,128]{1,0:T(8,128)S(1)} %get-tuple-element.16.g0.order), channel_id=1, source_target_pairs={{0,2},{1,3},{2,0},{3,1},{4,6},{5,7},{6,4},{7,5},{8,10},{9,11},{10,... | collective-permute-start | bytes 12296 | tf_op jit(solution)/shard_map/ppermute | solution.py:376
  7.7 0.4 collective-permute-start.2
  8.1 0.0 copy-done.1
  8.1 0.0 slice-start.1
  8.1 0.0 copy-start.3
  8.1 2.4 %far.2 = (f32[60,8,128]{2,1,0:T(8,128)S(1)}, f32[60,8,128]{2,1,0:T(8,128)S(1)}, f32[60,8,128]{2,1,0:T(8,128)S(1)}) custom-call(f32[63,8,128]{2,1,0:T(8,128)S(1)} %get-tuple-element.18.coef_ref, s32[4,60]{1,0:T(4,128)} %bitcast.5, bf16[240,128,128]{2,1,0:T(8,128)(2,1)S(1)} %copy-done.1, f32[8,128]{1,0:T(8,128)S(1)} %get-tuple-element.16.g0.order), custom_call_target="tpu_custom_call" | custom-call | flops 4000000000 | tf_op jit(solution)/shard_map/far/pallas_call | solution.py:360
  10.6 0.0 collective-permute-done.g1
  10.6 0.0 collective-permute-done.1.g2
  10.6 2.0 %collective-permute-done.2.g3 = f32[8,128]{1,0:T(8,128)S(1)} collective-permute-done((f32[8,128]{1,0:T(8,128)S(1)}, f32[8,128]{1,0:T(8,128)S(1)}, u32[]{:S(2)}, u32[]{:S(2)}) %collective-permute-start.2) | collective-permute-done | bytes 4128 | tf_op jit(solution)/shard_map/ppermute | solution.py:376
  12.6 0.0 copy-done.2
  12.6 0.0 copy-done.4
  12.6 0.1 group.1.order.p0
  12.7 0.0 slice-done
  12.7 0.0 slice-done.1
  12.7 0.0 copy-done.3
  12.7 3.1 %near.2 = (f32[92,8,128]{2,1,0:T(8,128)S(1)}, f32[92,8,128]{2,1,0:T(8,128)S(1)}, f32[92,8,128]{2,1,0:T(8,128)}) custom-call(bf16[32,8,128]{2,1,0:T(8,128)(2,1)S(1)} %copy-done.3, s32[8,32]{1,0:T(8,128)} %bitcast.4, bf16[256,128,128]{2,1,0:T(8,128)(2,1)S(1)} %bitcast.3, f32[60,8,128]{2,1,0:T(8,128)S(1)} %get-tuple-element.19.far_prev, ...), custom_call_target="tpu_custom_call" | custom-call | flops 4000000000 | tf_op jit(solution)/shard_map/near/pallas_call | solution.py:360
  15.9 0.1 collective-permute-start.7
  16.0 7.2 %collective-permute-start.8 = (f32[92,8,128]{2,1,0:T(8,128)S(1)}, f32[92,8,128]{2,1,0:T(8,128)}, u32[]{:S(2)}, u32[]{:S(2)}) collective-permute-start(f32[92,8,128]{2,1,0:T(8,128)S(1)} %get-tuple-element.26), channel_id=1, source_target_pairs={{0,127},{1,0},{2,1},{3,2},{4,3},{5,4},{6,5},{7,6},{8,7},{9,8},{10,... | collective-permute-start | bytes 1130504 | tf_op jit(solution)/shard_map/ppermute | solution.py:376
  23.1 0.0 collective-permute-start.3
  23.1 0.0 collective-permute-start.4
  23.1 4.7 %collective-permute-start.5 = (f32[17,8,128]{2,1,0:T(8,128)S(1)}, f32[17,8,128]{2,1,0:T(8,128)S(1)}, u32[]{:S(2)}, u32[]{:S(2)}) collective-permute-start(f32[17,8,128]{2,1,0:T(8,128)S(1)} %group.1.order.p0), channel_id=1, source_target_pairs={{0,3},{1,2},{2,1},{3,0},{4,7},{5,6},{6,5},{7,4},{8,11},{9,10},{10,... | collective-permute-start | bytes 208904 | tf_op jit(solution)/shard_map/ppermute | solution.py:376
  27.8 0.0 collective-permute-done.3.p1
  27.8 1.3 %collective-permute-done.4.p2 = f32[17,8,128]{2,1,0:T(8,128)S(1)} collective-permute-done((f32[17,8,128]{2,1,0:T(8,128)S(1)}, f32[17,8,128]{2,1,0:T(8,128)S(1)}, u32[]{:S(2)}, u32[]{:S(2)}) %collective-permute-start.4) | collective-permute-done | bytes 69664 | tf_op jit(solution)/shard_map/ppermute | solution.py:376
  29.1 1.0 %collective-permute-done.5.p3 = f32[17,8,128]{2,1,0:T(8,128)S(1)} collective-permute-done((f32[17,8,128]{2,1,0:T(8,128)S(1)}, f32[17,8,128]{2,1,0:T(8,128)S(1)}, u32[]{:S(2)}, u32[]{:S(2)}) %collective-permute-start.5) | collective-permute-done | bytes 69664 | tf_op jit(solution)/shard_map/ppermute | solution.py:376
  30.1 1.3 %pack.1 = (f32[64,8,128]{2,1,0:T(8,128)S(1)}, f32[64,8,128]{2,1,0:T(8,128)S(1)}) custom-call(f32[17,8,128]{2,1,0:T(8,128)S(1)} %group.1.order.p0, f32[17,8,128]{2,1,0:T(8,128)S(1)} %collective-permute-done.3.p1, f32[17,8,128]{2,1,0:T(8,128)S(1)} %collective-permute-done.4.p2, f32[17,8,128]{2,1,0:T(8,128)S(1)} %collective-permute-done.5.p3, ...), custom_call_target="tpu_custom_call" | custom-call | tf_op jit(solution)/shard_map/pack/pallas_call | solution.py:360
  31.4 0.1 collective-permute-start.6
  31.5 1.5 %collective-permute-done.6.core_ref = f32[64,8,128]{2,1,0:T(8,128)S(1)} collective-permute-done((f32[64,8,128]{2,1,0:T(8,128)S(1)}, f32[64,8,128]{2,1,0:T(8,128)S(1)}, u32[]{:S(2)}, u32[]{:S(2)}) %collective-permute-start.6) | collective-permute-done | bytes 262176 | tf_op jit(solution)/shard_map/ppermute | solution.py:376
  33.0 0.7 %core.1 = f32[16,4,8,128]{3,2,1,0:T(8,128)} custom-call(f32[64,8,128]{2,1,0:T(8,128)S(1)} %get-tuple-element.23.keep_ref, f32[64,8,128]{2,1,0:T(8,128)S(1)} %collective-permute-done.6.core_ref), custom_call_target="tpu_custom_call" | custom-call | tf_op jit(solution)/shard_map/core/pallas_call | solution.py:360
  33.7 7.5 %all-to-all-start = ((f32[16,4,8,128]{3,2,1,0:T(8,128)}), f32[16,4,8,128]{3,2,1,0:T(8,128)S(1)}, u32[]{:S(2)}, u32[]{:S(2)}) async-start(f32[16,4,8,128]{3,2,1,0:T(8,128)} %core.1), calls=%async_computation | async-start | bytes 524288 | tf_op jit(solution)/shard_map/all_to_all | solution.py:422
  41.2 0.0 copy-start
  41.2 0.0 collective-permute-done.7.prev_ref
  41.2 0.0 collective-permute-done.8.next_ref
  41.2 1.2 %merge.1.total = f32[92,8,128]{2,1,0:T(8,128)S(1)} custom-call(f32[92,8,128]{2,1,0:T(8,128)S(1)} %get-tuple-element.22.order.own_ref, f32[92,8,128]{2,1,0:T(8,128)S(1)} %collective-permute-done.7.prev_ref, f32[92,8,128]{2,1,0:T(8,128)} %collective-permute-done.8.next_ref), custom_call_target="tpu_custom_call" | custom-call | flops 20000000000 | tf_op jit(solution)/shard_map/merge/pallas_call | solution.py:360
  42.4 7.6 %all-to-all-done.top = f32[16,4,8,128]{3,2,1,0:T(8,128)S(1)} async-done(((f32[16,4,8,128]{3,2,1,0:T(8,128)}), f32[16,4,8,128]{3,2,1,0:T(8,128)S(1)}, u32[]{:S(2)}, u32[]{:S(2)}) %all-to-all-start) | async-done | bytes 262176 | tf_op jit(solution)/shard_map/all_to_all | solution.py:422
  50.0 0.0 copy-done
  50.0 2.4 %downward.1 = f32[32,8,128]{2,1,0:T(8,128)} custom-call(f32[16,4,8,128]{3,2,1,0:T(8,128)S(1)} %all-to-all-done.top, f32[92,8,128]{2,1,0:T(8,128)S(1)} %merge.1.total, bf16[63,128,128]{2,1,0:T(8,128)(2,1)S(1)} %copy-done, bf16[32,128,128]{2,1,0:T(8,128)(2,1)} %col_hbm.1), custom_call_target="tpu_custom_call" | custom-call | tf_op jit(solution)/shard_map/downward/pallas_call | solution.py:360
  (1 shorter events, 0.0 us)
Async XLA Ops:
  0.0 8.1 %copy-start.1 = (bf16[240,128,128]{2,1,0:T(8,128)(2,1)S(1)}, bf16[240,128,128]{2,1,0:T(8,128)(2,1)}, u32[]{:S(2)}) copy-start(bf16[240,128,128]{2,1,0:T(8,128)(2,1)} %far.3) | copy-start | bytes 23592964
  0.0 12.7 %slice-start = ((s8[8388608]{0:T(1024)(128)(4,1)}), s8[4194304]{0:T(1024)(128)(4,1)S(1)}, s32[]{:S(2)}) async-start(s8[8388608]{0:T(1024)(128)(4,1)} %bitcast.2), calls=%async_computation.1 | async-start | bytes 8388608
  3.3 9.2 %copy-start.2 = (bf16[4,128,128]{2,1,0:T(8,128)(2,1)S(1)}, bf16[4,128,128]{2,1,0:T(8,128)(2,1)}, u32[]{:S(2)}) copy-start(bf16[4,128,128]{2,1,0:T(8,128)(2,1)} %blocks.1) | copy-start | bytes 393220
  3.3 9.2 %copy-start.4 = (s32[1,4]{1,0:T(1,128)S(1)}, s32[1,4]{1,0:T(1,128)}, u32[]{:S(2)}) copy-start(s32[1,4]{1,0:T(1,128)} %group_list.1) | copy-start | bytes 52
  3.4 7.2 %collective-permute-start = (f32[8,128]{1,0:T(8,128)S(1)}, f32[8,128]{1,0:T(8,128)S(1)}, u32[]{:S(2)}, u32[]{:S(2)}) collective-permute-start(f32[8,128]{1,0:T(8,128)S(1)} %get-tuple-element.16.g0.order), channel_id=1, source_target_pairs={{0,1},{1,0},{2,3},{3,2},{4,5},{5,4},{6,7},{7,6},{8,9},{9,8},{10,11... | collective-permute-start | bytes 12296 | tf_op jit(solution)/shard_map/ppermute | solution.py:376
  5.0 5.6 %collective-permute-start.1 = (f32[8,128]{1,0:T(8,128)S(1)}, f32[8,128]{1,0:T(8,128)S(1)}, u32[]{:S(2)}, u32[]{:S(2)}) collective-permute-start(f32[8,128]{1,0:T(8,128)S(1)} %get-tuple-element.16.g0.order), channel_id=1, source_target_pairs={{0,2},{1,3},{2,0},{3,1},{4,6},{5,7},{6,4},{7,5},{8,10},{9,11},{10,... | collective-permute-start | bytes 12296 | tf_op jit(solution)/shard_map/ppermute | solution.py:376
  7.7 4.8 %collective-permute-start.2 = (f32[8,128]{1,0:T(8,128)S(1)}, f32[8,128]{1,0:T(8,128)S(1)}, u32[]{:S(2)}, u32[]{:S(2)}) collective-permute-start(f32[8,128]{1,0:T(8,128)S(1)} %get-tuple-element.16.g0.order), channel_id=1, source_target_pairs={{0,3},{1,2},{2,1},{3,0},{4,7},{5,6},{6,5},{7,4},{8,11},{9,10},{10,... | collective-permute-start | bytes 12296 | tf_op jit(solution)/shard_map/ppermute | solution.py:376
  8.1 4.6 %slice-start.1 = ((s8[8388608]{0:T(1024)(128)(4,1)}), s8[4194304]{0:T(1024)(128)(4,1)S(1)}, s32[]{:S(2)}) async-start(s8[8388608]{0:T(1024)(128)(4,1)} %bitcast.2), calls=%async_computation.2 | async-start | bytes 8388608
  8.1 4.6 %copy-start.3 = (bf16[32,8,128]{2,1,0:T(8,128)(2,1)S(1)}, bf16[32,8,128]{2,1,0:T(8,128)(2,1)}, u32[]{:S(2)}) copy-start(bf16[32,8,128]{2,1,0:T(8,128)(2,1)} %src_ref.1) | copy-start | bytes 196612
  15.9 25.4 %collective-permute-start.7 = (f32[92,8,128]{2,1,0:T(8,128)}, f32[92,8,128]{2,1,0:T(8,128)S(1)}, u32[]{:S(2)}, u32[]{:S(2)}) collective-permute-start(f32[92,8,128]{2,1,0:T(8,128)} %get-tuple-element.25), channel_id=1, source_target_pairs={{0,1},{1,2},{2,3},{3,4},{4,5},{5,6},{6,7},{7,8},{8,9},{9,10},{10,1... | collective-permute-start | bytes 1130504 | tf_op jit(solution)/shard_map/ppermute | solution.py:376
  16.0 25.3 %collective-permute-start.8 = (f32[92,8,128]{2,1,0:T(8,128)S(1)}, f32[92,8,128]{2,1,0:T(8,128)}, u32[]{:S(2)}, u32[]{:S(2)}) collective-permute-start(f32[92,8,128]{2,1,0:T(8,128)S(1)} %get-tuple-element.26), channel_id=1, source_target_pairs={{0,127},{1,0},{2,1},{3,2},{4,3},{5,4},{6,5},{7,6},{8,7},{9,8},{10,... | collective-permute-start | bytes 1130504 | tf_op jit(solution)/shard_map/ppermute | solution.py:376
  23.1 4.7 %collective-permute-start.3 = (f32[17,8,128]{2,1,0:T(8,128)S(1)}, f32[17,8,128]{2,1,0:T(8,128)S(1)}, u32[]{:S(2)}, u32[]{:S(2)}) collective-permute-start(f32[17,8,128]{2,1,0:T(8,128)S(1)} %group.1.order.p0), channel_id=1, source_target_pairs={{0,1},{1,0},{2,3},{3,2},{4,5},{5,4},{6,7},{7,6},{8,9},{9,8},{10,11... | collective-permute-start | bytes 208904 | tf_op jit(solution)/shard_map/ppermute | solution.py:376
  23.1 6.0 %collective-permute-start.4 = (f32[17,8,128]{2,1,0:T(8,128)S(1)}, f32[17,8,128]{2,1,0:T(8,128)S(1)}, u32[]{:S(2)}, u32[]{:S(2)}) collective-permute-start(f32[17,8,128]{2,1,0:T(8,128)S(1)} %group.1.order.p0), channel_id=1, source_target_pairs={{0,2},{1,3},{2,0},{3,1},{4,6},{5,7},{6,4},{7,5},{8,10},{9,11},{10,... | collective-permute-start | bytes 208904 | tf_op jit(solution)/shard_map/ppermute | solution.py:376
  23.1 7.0 %collective-permute-start.5 = (f32[17,8,128]{2,1,0:T(8,128)S(1)}, f32[17,8,128]{2,1,0:T(8,128)S(1)}, u32[]{:S(2)}, u32[]{:S(2)}) collective-permute-start(f32[17,8,128]{2,1,0:T(8,128)S(1)} %group.1.order.p0), channel_id=1, source_target_pairs={{0,3},{1,2},{2,1},{3,0},{4,7},{5,6},{6,5},{7,4},{8,11},{9,10},{10,... | collective-permute-start | bytes 208904 | tf_op jit(solution)/shard_map/ppermute | solution.py:376
  31.4 1.6 %collective-permute-start.6 = (f32[64,8,128]{2,1,0:T(8,128)S(1)}, f32[64,8,128]{2,1,0:T(8,128)S(1)}, u32[]{:S(2)}, u32[]{:S(2)}) collective-permute-start(f32[64,8,128]{2,1,0:T(8,128)S(1)} %get-tuple-element.24), channel_id=1, source_target_pairs={{0,4},{4,0},{8,12},{12,8},{16,20},{20,16},{24,28},{28,24},{32,36},... | collective-permute-start | bytes 786440 | tf_op jit(solution)/shard_map/ppermute | solution.py:376
  33.7 16.3 %all-to-all-start = ((f32[16,4,8,128]{3,2,1,0:T(8,128)}), f32[16,4,8,128]{3,2,1,0:T(8,128)S(1)}, u32[]{:S(2)}, u32[]{:S(2)}) async-start(f32[16,4,8,128]{3,2,1,0:T(8,128)} %core.1), calls=%async_computation | async-start | bytes 524288 | tf_op jit(solution)/shard_map/all_to_all | solution.py:422
  41.2 8.8 %copy-start = (bf16[63,128,128]{2,1,0:T(8,128)(2,1)S(1)}, bf16[63,128,128]{2,1,0:T(8,128)(2,1)}, u32[]{:S(2)}) copy-start(bf16[63,128,128]{2,1,0:T(8,128)(2,1)} %down.1) | copy-start | bytes 6193156

commit v4 on v3

--- a/solution.py
+++ b/solution.py
@@ -279,17 +279,16 @@
     out_ref[...] = (keep_ref[...] + core_ref[...]).reshape(out_ref.shape)
 
 
-def merge_kernel(own_ref, prev_ref, next_ref, out_ref):
-    out_ref[...] = (own_ref[...] + prev_ref[...]) + next_ref[...]
-
-
-def down_kernel(top, total, down, col_hbm, out_ref, col, level_down, sem):
+def down_kernel(top, own, from_prev, from_next, down, col_hbm, out_ref, col, level_down, sem):
     leaves = out_ref.shape[0]
     levels = leaves.bit_length() - 1
     quarter = leaves // 4
     n, m = out_ref.shape[1:]
     fetch = Fetches(sem)
     col_copies = [fetch.rows(col_hbm, col, i * quarter, quarter) for i in range(4)]
+
+    def total(i):
+        return (own[i] + from_prev[i]) + from_next[i]
 
     fields = top[0]
     for i in range(1, top.shape[0]):
@@ -309,14 +308,14 @@
             out = dot(left, square(down[a], down[a + 1], down[a + 2], down[a + 3]))
             outs = (out[:n, :m], out[:n, m:], out[n:, :m], out[n:, m:])
             for i in range(4):
-                level_down[a + i] = rounded(total[leaves + a + i] + outs[i])
+                level_down[a + i] = rounded(total(leaves + a + i) + outs[i])
     for t in range(0, leaves, 4):
         if t % quarter == 0:
             col_copies[t // quarter].wait()
         span = range(t, t + 4)
         outs = quad([level_down[i] for i in span], [col[i] for i in span])
         for i, out in zip(span, outs):
-            out_ref[i] = total[i] + out
+            out_ref[i] = total(i) + out
 
 
 PARAMS = pltpu.CompilerParams(vmem_limit_bytes=24 * 1024 * 1024)
@@ -376,7 +375,7 @@
         return lax.ppermute(x, axis, [(i, target(i)) for i in range(count)])
 
     def gathered(x):
-        return [x] + [permuted(x, "sub", lambda i, s=s: i ^ s) for s in range(1, subs)]
+        return [x] + [permuted(x, "sub", lambda i, s=s: i ^ s) for s in (2, 1, 3)]
 
     coef, group, top = call(
         up_kernel, "upward", 4, (shape(nodes), shape(), shape(TOP_TERMS + 1)),
@@ -408,10 +407,8 @@
     )
     half = groups // 2 * 4
     everyone = ("leaf", "sub")
-    window = shape(leaves + far_nodes)
     from_prev = permuted(to_next, everyone, lambda i: (i + 1) % devices)
     from_next = permuted(to_prev, everyone, lambda i: (i - 1) % devices)
-    total = call(merge_kernel, "merge", 20, window, (own, from_prev, from_next), [VMEM] * 3, [])
 
     keep, send = call(
         pack_kernel, "pack", 0, (shape(half), shape(half)), (*term_parts, own), [VMEM] * 4 + [ANY],
@@ -423,7 +420,7 @@
         planes, "leaf", 0, 0, tiled=True, axis_index_groups=[list(range(c, groups, 2)) for c in range(2)]
     )
     return call(
-        down_kernel, "downward", 0, shape(leaves), (fields, total, down_transfer, col_basis), [VMEM] * 3 + [ANY],
+        down_kernel, "downward", 0, shape(leaves), (fields, own, from_prev, from_next, down_transfer, col_basis), [VMEM] * 5 + [ANY],
         [buffer(leaves), plane(nodes), copies(4)],
     )
 

time: 53.5 us -> 44.9 us (0.84); the launches traced: 52.4 us -> 44.7 us
  starting transfers between devices: 24.3 us -> 20.5 us
  waiting for transfers between devices: 13.4 us -> 10.3 us
  Pallas kernels: 14.6 us -> 13.7 us
    all_to_all x1, starting transfers between devices: 7.47 us -> 3.87 us  [shards(): lax.all_to_all(planes, 'leaf', 0, 0, tiled=True, axis_index_groups=[list(...]
    all_to_all x1, waiting for transfers between devices: 7.58 us -> 5.1 us  [shards(): lax.all_to_all(planes, 'leaf', 0, 0, tiled=True, axis_index_groups=[list(...]
    pallas_call x8 -> x7, Pallas kernels: 14.6 us -> 13.7 us  [call(): pl.pallas_call(kernel, out_shape=outs, in_specs=specs, out_specs=out_spec...]
    ppermute x9, waiting for transfers between devices: 5.78 us -> 5.24 us  [permuted(): return lax.ppermute(x, axis, [(i, target(i)) for i in range(count)])]
  transfers between devices with their start and end apart: 10 -> 10, of which waited for: 5 -> 3; matrix products, arithmetic and copies ran while one was open for 0% -> 0% of each run, Pallas kernels for 11% -> 15%
where the time goes in v4:
time: 44.9 us; the launch traced here: 44.7 us
  starting transfers between devices  20.5 us (46%)
  Pallas kernels  13.7 us (31%)
  waiting for transfers between devices  10.3 us (23%)
    ppermute x9, starting transfers between devices, permuted(): return lax.ppermute(x, axis, [(i, target(i)) for i in range(count)])  16.6 us
    pallas_call x7, Pallas kernels, call(): pl.pallas_call(kernel, out_shape=outs, in_specs=specs, out_specs=out_spec...  13.7 us
    ppermute x9, waiting for transfers between devices, permuted(): return lax.ppermute(x, axis, [(i, target(i)) for i in range(count)])  5.24 us
    all_to_all x1, waiting for transfers between devices, shards(): lax.all_to_all(planes, 'leaf', 0, 0, tiled=True, axis_index_groups=[list(...  5.1 us
    all_to_all x1, starting transfers between devices, shards(): lax.all_to_all(planes, 'leaf', 0, 0, tiled=True, axis_index_groups=[list(...  3.87 us
  transfers between devices with their start and end apart: 10, of which 3 were waited for; matrix products, arithmetic and copies ran while one was open for 0% of the time, Pallas kernels for 15%

profile of v4, /device:TPU:0, one launch (start us, length us, event | category | flops | bytes accessed | tf_op | source)
XLA Modules:
  0.0 44.7 jit_solution(10076277077600855815)
XLA Ops:
  0.0 0.0 copy-start.1
  0.0 0.0 slice-start
  0.0 3.3 %upward.1 = (f32[63,8,128]{2,1,0:T(8,128)S(1)}, f32[8,128]{1,0:T(8,128)S(1)}, f32[13,8,128]{2,1,0:T(8,128)S(1)}) custom-call(bf16[32,8,128]{2,1,0:T(8,128)(2,1)} %src_ref.1, s32[2,4]{1,0:T(2,128)} %upper_list_hbm.1, s32[1,4]{1,0:T(1,128)} %root_list_hbm.1, bf16[32,128,128]{2,1,0:T(8,128)(2,1)} %rb_hbm.1, bf16[63,128,128]{2,1,0:T(8,128)(2,1)} %up_hbm.1, ...), custom_call_target="tpu_custom_call" | custom-call | flops 4000000000 | tf_op jit(solution)/shard_map/upward/pallas_call | solution.py:359
  3.3 0.0 copy-start.2
  3.3 0.0 copy-start.4
  3.4 3.2 %collective-permute-start = (f32[8,128]{1,0:T(8,128)S(1)}, f32[8,128]{1,0:T(8,128)S(1)}, u32[]{:S(2)}, u32[]{:S(2)}) collective-permute-start(f32[8,128]{1,0:T(8,128)S(1)} %get-tuple-element.16.g0.order), channel_id=1, source_target_pairs={{0,2},{1,3},{2,0},{3,1},{4,6},{5,7},{6,4},{7,5},{8,10},{9,11},{10,... | collective-permute-start | bytes 12296 | tf_op jit(solution)/shard_map/ppermute | solution.py:375
  6.5 0.6 %collective-permute-start.1 = (f32[8,128]{1,0:T(8,128)S(1)}, f32[8,128]{1,0:T(8,128)S(1)}, u32[]{:S(2)}, u32[]{:S(2)}) collective-permute-start(f32[8,128]{1,0:T(8,128)S(1)} %get-tuple-element.16.g0.order), channel_id=1, source_target_pairs={{0,1},{1,0},{2,3},{3,2},{4,5},{5,4},{6,7},{7,6},{8,9},{9,8},{10,11... | collective-permute-start | bytes 12296 | tf_op jit(solution)/shard_map/ppermute | solution.py:375
  7.1 0.6 %collective-permute-start.2 = (f32[8,128]{1,0:T(8,128)S(1)}, f32[8,128]{1,0:T(8,128)S(1)}, u32[]{:S(2)}, u32[]{:S(2)}) collective-permute-start(f32[8,128]{1,0:T(8,128)S(1)} %get-tuple-element.16.g0.order), channel_id=1, source_target_pairs={{0,3},{1,2},{2,1},{3,0},{4,7},{5,6},{6,5},{7,4},{8,11},{9,10},{10,... | collective-permute-start | bytes 12296 | tf_op jit(solution)/shard_map/ppermute | solution.py:375
  7.7 0.0 copy-done.1
  7.7 0.0 slice-start.1
  7.7 0.0 copy-start.3
  7.7 2.4 %far.2 = (f32[60,8,128]{2,1,0:T(8,128)S(1)}, f32[60,8,128]{2,1,0:T(8,128)S(1)}, f32[60,8,128]{2,1,0:T(8,128)S(1)}) custom-call(f32[63,8,128]{2,1,0:T(8,128)S(1)} %get-tuple-element.18.coef_ref, s32[4,60]{1,0:T(4,128)} %bitcast.5, bf16[240,128,128]{2,1,0:T(8,128)(2,1)S(1)} %copy-done.1, f32[8,128]{1,0:T(8,128)S(1)} %get-tuple-element.16.g0.order), custom_call_target="tpu_custom_call" | custom-call | flops 4000000000 | tf_op jit(solution)/shard_map/far/pallas_call | solution.py:359
  10.1 0.0 collective-permute-done.g1
  10.1 0.0 collective-permute-done.1.g2
  10.2 1.8 %collective-permute-done.2.g3 = f32[8,128]{1,0:T(8,128)S(1)} collective-permute-done((f32[8,128]{1,0:T(8,128)S(1)}, f32[8,128]{1,0:T(8,128)S(1)}, u32[]{:S(2)}, u32[]{:S(2)}) %collective-permute-start.2) | collective-permute-done | bytes 4128 | tf_op jit(solution)/shard_map/ppermute | solution.py:375
  12.0 0.0 copy-done.2
  12.0 0.0 copy-done.4
  12.0 0.1 group.1.order.p0
  12.1 1.2 %collective-permute-start.3 = (f32[17,8,128]{2,1,0:T(8,128)S(1)}, f32[17,8,128]{2,1,0:T(8,128)S(1)}, u32[]{:S(2)}, u32[]{:S(2)}) collective-permute-start(f32[17,8,128]{2,1,0:T(8,128)S(1)} %group.1.order.p0), channel_id=1, source_target_pairs={{0,2},{1,3},{2,0},{3,1},{4,6},{5,7},{6,4},{7,5},{8,10},{9,11},{10,... | collective-permute-start | bytes 208904 | tf_op jit(solution)/shard_map/ppermute | solution.py:375
  13.3 0.6 %collective-permute-start.4 = (f32[17,8,128]{2,1,0:T(8,128)S(1)}, f32[17,8,128]{2,1,0:T(8,128)S(1)}, u32[]{:S(2)}, u32[]{:S(2)}) collective-permute-start(f32[17,8,128]{2,1,0:T(8,128)S(1)} %group.1.order.p0), channel_id=1, source_target_pairs={{0,1},{1,0},{2,3},{3,2},{4,5},{5,4},{6,7},{7,6},{8,9},{9,8},{10,11... | collective-permute-start | bytes 208904 | tf_op jit(solution)/shard_map/ppermute | solution.py:375
  13.9 2.3 %collective-permute-start.5 = (f32[17,8,128]{2,1,0:T(8,128)S(1)}, f32[17,8,128]{2,1,0:T(8,128)S(1)}, u32[]{:S(2)}, u32[]{:S(2)}) collective-permute-start(f32[17,8,128]{2,1,0:T(8,128)S(1)} %group.1.order.p0), channel_id=1, source_target_pairs={{0,3},{1,2},{2,1},{3,0},{4,7},{5,6},{6,5},{7,4},{8,11},{9,10},{10,... | collective-permute-start | bytes 208904 | tf_op jit(solution)/shard_map/ppermute | solution.py:375
  16.2 0.0 slice-done
  16.2 0.0 slice-done.1
  16.2 0.0 copy-done.3
  16.2 0.0 copy-start
  16.2 3.4 %near.2 = (f32[92,8,128]{2,1,0:T(8,128)}, f32[92,8,128]{2,1,0:T(8,128)S(1)}, f32[92,8,128]{2,1,0:T(8,128)}) custom-call(bf16[32,8,128]{2,1,0:T(8,128)(2,1)S(1)} %copy-done.3, s32[8,32]{1,0:T(8,128)} %bitcast.4, bf16[256,128,128]{2,1,0:T(8,128)(2,1)S(1)} %bitcast.3, f32[60,8,128]{2,1,0:T(8,128)S(1)} %get-tuple-element.19.far_prev, ...), custom_call_target="tpu_custom_call" | custom-call | flops 4000000000 | tf_op jit(solution)/shard_map/near/pallas_call | solution.py:359
  19.6 0.0 collective-permute-done.3.p1
  19.6 0.0 collective-permute-done.4.p2
  19.6 0.0 collective-permute-done.5.p3
  19.6 1.3 %pack.1 = (f32[64,8,128]{2,1,0:T(8,128)S(1)}, f32[64,8,128]{2,1,0:T(8,128)S(1)}) custom-call(f32[17,8,128]{2,1,0:T(8,128)S(1)} %group.1.order.p0, f32[17,8,128]{2,1,0:T(8,128)S(1)} %collective-permute-done.3.p1, f32[17,8,128]{2,1,0:T(8,128)S(1)} %collective-permute-done.4.p2, f32[17,8,128]{2,1,0:T(8,128)S(1)} %collective-permute-done.5.p3, ...), custom_call_target="tpu_custom_call" | custom-call | tf_op jit(solution)/shard_map/pack/pallas_call | solution.py:359
  20.9 0.1 collective-permute-start.6
  21.0 0.3 collective-permute-start.7
  21.3 7.8 %collective-permute-start.8 = (f32[92,8,128]{2,1,0:T(8,128)}, f32[92,8,128]{2,1,0:T(8,128)S(1)}, u32[]{:S(2)}, u32[]{:S(2)}) collective-permute-start(f32[92,8,128]{2,1,0:T(8,128)} %get-tuple-element.26), channel_id=1, source_target_pairs={{0,127},{1,0},{2,1},{3,2},{4,3},{5,4},{6,5},{7,6},{8,7},{9,8},{10,... | collective-permute-start | bytes 1130504 | tf_op jit(solution)/shard_map/ppermute | solution.py:375
  29.1 0.0 collective-permute-done.6.core_ref
  29.1 0.7 %core.1 = f32[16,4,8,128]{3,2,1,0:T(8,128)} custom-call(f32[64,8,128]{2,1,0:T(8,128)S(1)} %get-tuple-element.23.keep_ref, f32[64,8,128]{2,1,0:T(8,128)S(1)} %collective-permute-done.6.core_ref), custom_call_target="tpu_custom_call" | custom-call | tf_op jit(solution)/shard_map/core/pallas_call | solution.py:359
  29.9 3.9 %all-to-all-start = ((f32[16,4,8,128]{3,2,1,0:T(8,128)}), f32[16,4,8,128]{3,2,1,0:T(8,128)S(1)}, u32[]{:S(2)}, u32[]{:S(2)}) async-start(f32[16,4,8,128]{3,2,1,0:T(8,128)} %core.1), calls=%async_computation | async-start | bytes 524288 | tf_op jit(solution)/shard_map/all_to_all | solution.py:419
  33.7 3.4 %collective-permute-done.7.from_prev = f32[92,8,128]{2,1,0:T(8,128)S(1)} collective-permute-done((f32[92,8,128]{2,1,0:T(8,128)}, f32[92,8,128]{2,1,0:T(8,128)S(1)}, u32[]{:S(2)}, u32[]{:S(2)}) %collective-permute-start.7) | collective-permute-done | bytes 376864 | tf_op jit(solution)/shard_map/ppermute | solution.py:375
  37.2 0.0 collective-permute-done.8.from_next
  37.2 5.1 %all-to-all-done.top = f32[16,4,8,128]{3,2,1,0:T(8,128)S(1)} async-done(((f32[16,4,8,128]{3,2,1,0:T(8,128)}), f32[16,4,8,128]{3,2,1,0:T(8,128)S(1)}, u32[]{:S(2)}, u32[]{:S(2)}) %all-to-all-start) | async-done | bytes 262176 | tf_op jit(solution)/shard_map/all_to_all | solution.py:419
  42.3 0.0 copy-done
  42.3 2.4 %downward.1 = f32[32,8,128]{2,1,0:T(8,128)} custom-call(f32[16,4,8,128]{3,2,1,0:T(8,128)S(1)} %all-to-all-done.top, f32[92,8,128]{2,1,0:T(8,128)S(1)} %get-tuple-element.22.order.own, f32[92,8,128]{2,1,0:T(8,128)S(1)} %collective-permute-done.7.from_prev, f32[92,8,128]{2,1,0:T(8,128)S(1)} %collective-permute-done.8.from_next, ...), custom_call_target="tpu_custom_call" | custom-call | tf_op jit(solution)/shard_map/downward/pallas_call | solution.py:359
  (1 shorter events, 0.0 us)
Async XLA Ops:
  0.0 7.7 %copy-start.1 = (bf16[240,128,128]{2,1,0:T(8,128)(2,1)S(1)}, bf16[240,128,128]{2,1,0:T(8,128)(2,1)}, u32[]{:S(2)}) copy-start(bf16[240,128,128]{2,1,0:T(8,128)(2,1)} %far.3) | copy-start | bytes 23592964
  0.0 16.2 %slice-start = ((s8[8388608]{0:T(1024)(128)(4,1)}), s8[4194304]{0:T(1024)(128)(4,1)S(1)}, s32[]{:S(2)}) async-start(s8[8388608]{0:T(1024)(128)(4,1)} %bitcast.2), calls=%async_computation.1 | async-start | bytes 8388608
  3.3 8.6 %copy-start.2 = (bf16[4,128,128]{2,1,0:T(8,128)(2,1)S(1)}, bf16[4,128,128]{2,1,0:T(8,128)(2,1)}, u32[]{:S(2)}) copy-start(bf16[4,128,128]{2,1,0:T(8,128)(2,1)} %blocks.1) | copy-start | bytes 393220
  3.3 8.6 %copy-start.4 = (s32[1,4]{1,0:T(1,128)S(1)}, s32[1,4]{1,0:T(1,128)}, u32[]{:S(2)}) copy-start(s32[1,4]{1,0:T(1,128)} %group_list.1) | copy-start | bytes 52
  3.4 6.8 %collective-permute-start = (f32[8,128]{1,0:T(8,128)S(1)}, f32[8,128]{1,0:T(8,128)S(1)}, u32[]{:S(2)}, u32[]{:S(2)}) collective-permute-start(f32[8,128]{1,0:T(8,128)S(1)} %get-tuple-element.16.g0.order), channel_id=1, source_target_pairs={{0,2},{1,3},{2,0},{3,1},{4,6},{5,7},{6,4},{7,5},{8,10},{9,11},{10,... | collective-permute-start | bytes 12296 | tf_op jit(solution)/shard_map/ppermute | solution.py:375
  6.5 3.6 %collective-permute-start.1 = (f32[8,128]{1,0:T(8,128)S(1)}, f32[8,128]{1,0:T(8,128)S(1)}, u32[]{:S(2)}, u32[]{:S(2)}) collective-permute-start(f32[8,128]{1,0:T(8,128)S(1)} %get-tuple-element.16.g0.order), channel_id=1, source_target_pairs={{0,1},{1,0},{2,3},{3,2},{4,5},{5,4},{6,7},{7,6},{8,9},{9,8},{10,11... | collective-permute-start | bytes 12296 | tf_op jit(solution)/shard_map/ppermute | solution.py:375
  7.1 4.8 %collective-permute-start.2 = (f32[8,128]{1,0:T(8,128)S(1)}, f32[8,128]{1,0:T(8,128)S(1)}, u32[]{:S(2)}, u32[]{:S(2)}) collective-permute-start(f32[8,128]{1,0:T(8,128)S(1)} %get-tuple-element.16.g0.order), channel_id=1, source_target_pairs={{0,3},{1,2},{2,1},{3,0},{4,7},{5,6},{6,5},{7,4},{8,11},{9,10},{10,... | collective-permute-start | bytes 12296 | tf_op jit(solution)/shard_map/ppermute | solution.py:375
  7.7 8.5 %slice-start.1 = ((s8[8388608]{0:T(1024)(128)(4,1)}), s8[4194304]{0:T(1024)(128)(4,1)S(1)}, s32[]{:S(2)}) async-start(s8[8388608]{0:T(1024)(128)(4,1)} %bitcast.2), calls=%async_computation.2 | async-start | bytes 8388608
  7.7 8.5 %copy-start.3 = (bf16[32,8,128]{2,1,0:T(8,128)(2,1)S(1)}, bf16[32,8,128]{2,1,0:T(8,128)(2,1)}, u32[]{:S(2)}) copy-start(bf16[32,8,128]{2,1,0:T(8,128)(2,1)} %src_ref.1) | copy-start | bytes 196612
  12.1 7.5 %collective-permute-start.3 = (f32[17,8,128]{2,1,0:T(8,128)S(1)}, f32[17,8,128]{2,1,0:T(8,128)S(1)}, u32[]{:S(2)}, u32[]{:S(2)}) collective-permute-start(f32[17,8,128]{2,1,0:T(8,128)S(1)} %group.1.order.p0), channel_id=1, source_target_pairs={{0,2},{1,3},{2,0},{3,1},{4,6},{5,7},{6,4},{7,5},{8,10},{9,11},{10,... | collective-permute-start | bytes 208904 | tf_op jit(solution)/shard_map/ppermute | solution.py:375
  13.3 6.3 %collective-permute-start.4 = (f32[17,8,128]{2,1,0:T(8,128)S(1)}, f32[17,8,128]{2,1,0:T(8,128)S(1)}, u32[]{:S(2)}, u32[]{:S(2)}) collective-permute-start(f32[17,8,128]{2,1,0:T(8,128)S(1)} %group.1.order.p0), channel_id=1, source_target_pairs={{0,1},{1,0},{2,3},{3,2},{4,5},{5,4},{6,7},{7,6},{8,9},{9,8},{10,11... | collective-permute-start | bytes 208904 | tf_op jit(solution)/shard_map/ppermute | solution.py:375
  13.9 5.8 %collective-permute-start.5 = (f32[17,8,128]{2,1,0:T(8,128)S(1)}, f32[17,8,128]{2,1,0:T(8,128)S(1)}, u32[]{:S(2)}, u32[]{:S(2)}) collective-permute-start(f32[17,8,128]{2,1,0:T(8,128)S(1)} %group.1.order.p0), channel_id=1, source_target_pairs={{0,3},{1,2},{2,1},{3,0},{4,7},{5,6},{6,5},{7,4},{8,11},{9,10},{10,... | collective-permute-start | bytes 208904 | tf_op jit(solution)/shard_map/ppermute | solution.py:375
  16.2 26.0 %copy-start = (bf16[63,128,128]{2,1,0:T(8,128)(2,1)S(1)}, bf16[63,128,128]{2,1,0:T(8,128)(2,1)}, u32[]{:S(2)}) copy-start(bf16[63,128,128]{2,1,0:T(8,128)(2,1)} %down.1) | copy-start | bytes 6193156
  20.9 8.2 %collective-permute-start.6 = (f32[64,8,128]{2,1,0:T(8,128)S(1)}, f32[64,8,128]{2,1,0:T(8,128)S(1)}, u32[]{:S(2)}, u32[]{:S(2)}) collective-permute-start(f32[64,8,128]{2,1,0:T(8,128)S(1)} %get-tuple-element.24), channel_id=1, source_target_pairs={{0,4},{4,0},{8,12},{12,8},{16,20},{20,16},{24,28},{28,24},{32,36},... | collective-permute-start | bytes 786440 | tf_op jit(solution)/shard_map/ppermute | solution.py:375
  21.0 16.1 %collective-permute-start.7 = (f32[92,8,128]{2,1,0:T(8,128)}, f32[92,8,128]{2,1,0:T(8,128)S(1)}, u32[]{:S(2)}, u32[]{:S(2)}) collective-permute-start(f32[92,8,128]{2,1,0:T(8,128)} %get-tuple-element.25), channel_id=1, source_target_pairs={{0,1},{1,2},{2,3},{3,4},{4,5},{5,6},{6,7},{7,8},{8,9},{9,10},{10,1... | collective-permute-start | bytes 1130504 | tf_op jit(solution)/shard_map/ppermute | solution.py:375
  21.3 15.8 %collective-permute-start.8 = (f32[92,8,128]{2,1,0:T(8,128)}, f32[92,8,128]{2,1,0:T(8,128)S(1)}, u32[]{:S(2)}, u32[]{:S(2)}) collective-permute-start(f32[92,8,128]{2,1,0:T(8,128)} %get-tuple-element.26), channel_id=1, source_target_pairs={{0,127},{1,0},{2,1},{3,2},{4,3},{5,4},{6,5},{7,6},{8,7},{9,8},{10,... | collective-permute-start | bytes 1130504 | tf_op jit(solution)/shard_map/ppermute | solution.py:375
  29.9 12.4 %all-to-all-start = ((f32[16,4,8,128]{3,2,1,0:T(8,128)}), f32[16,4,8,128]{3,2,1,0:T(8,128)S(1)}, u32[]{:S(2)}, u32[]{:S(2)}) async-start(f32[16,4,8,128]{3,2,1,0:T(8,128)} %core.1), calls=%async_computation | async-start | bytes 524288 | tf_op jit(solution)/shard_map/all_to_all | solution.py:419

commit v5 on v4

--- a/solution.py
+++ b/solution.py
@@ -12,6 +12,7 @@
 ANY = pl.BlockSpec(memory_space=pl.ANY)
 VMEM = pl.BlockSpec(memory_space=pltpu.VMEM)
 REPLICAS = 4
+SUB_ORDER, PLANE_ORDER = (3, 1, 2), (2, 1, 3)
 UPPER_TERMS, ROOT_TERMS, GROUP_TERMS = 8, 4, 4
 TOP_TERMS = UPPER_TERMS + ROOT_TERMS
 TERMS = TOP_TERMS + GROUP_TERMS
@@ -275,24 +276,32 @@
     send_ref[...] = total((1 - own_core) * half)
 
 
-def core_kernel(keep_ref, core_ref, out_ref):
-    out_ref[...] = (keep_ref[...] + core_ref[...]).reshape(out_ref.shape)
-
-
-def down_kernel(top, own, from_prev, from_next, down, col_hbm, out_ref, col, level_down, sem):
+def merge_kernel(own_ref, prev_ref, out_ref):
+    out_ref[...] = own_ref[...] + prev_ref[...]
+
+
+def split_kernel(unit, held, *refs):
+    refs = refs[: len(refs) - held]
+    parts, outs = refs[: -4 - held], refs[-4:]
+    rows = outs[0].shape[0]
+    own = (lax.axis_index("leaf") // unit) & 3
+    for digit, out in enumerate(outs):
+        part = pl.ds((own ^ digit) * rows, rows)
+        total = parts[0][part]
+        for p in parts[1:]:
+            total = total + p[part]
+        out[...] = total
+
+
+def down_kernel(t0, t1, t2, t3, own, from_next, down, col, out_ref, level_down):
     leaves = out_ref.shape[0]
     levels = leaves.bit_length() - 1
-    quarter = leaves // 4
     n, m = out_ref.shape[1:]
-    fetch = Fetches(sem)
-    col_copies = [fetch.rows(col_hbm, col, i * quarter, quarter) for i in range(4)]
 
     def total(i):
-        return (own[i] + from_prev[i]) + from_next[i]
-
-    fields = top[0]
-    for i in range(1, top.shape[0]):
-        fields = fields + top[i]
+        return own[i] + from_next[i]
+
+    fields = (t0[...] + t1[...]) + (t2[...] + t3[...])
     root = 2 * leaves - 2
     level_down[root] = rounded(fields[2] + exact_dot(exact_parts(fields[3]), down[root]))
     out = dot(level_down[root], jnp.concatenate([down[root - 2], down[root - 1]], axis=1))
@@ -310,8 +319,6 @@
             for i in range(4):
                 level_down[a + i] = rounded(total(leaves + a + i) + outs[i])
     for t in range(0, leaves, 4):
-        if t % quarter == 0:
-            col_copies[t // quarter].wait()
         span = range(t, t + 4)
         outs = quad([level_down[i] for i in span], [col[i] for i in span])
         for i, out in zip(span, outs):
@@ -330,10 +337,11 @@
     far_blocks, far_list, upper_blocks, upper_list, root_blocks, root_list, group_blocks, group_list,
 ):
     in_hbm = functools.partial(pltpu.with_memory_space_constraint, memory_space=pltpu.HBM)
-    up_sources, row_basis, up_transfer, col_basis = map(in_hbm, (sources, row_basis, up_transfer, col_basis))
-    near_list, far_list, upper_blocks, upper_list, root_blocks, root_list = map(
-        in_hbm, (near_list.T, far_list.T, upper_blocks, upper_list, root_blocks, root_list)
-    )
+    up_sources, row_basis, up_transfer = map(in_hbm, (sources, row_basis, up_transfer))
+    upper_blocks, upper_list, root_blocks, root_list = map(
+        in_hbm, (upper_blocks, upper_list, root_blocks, root_list)
+    )
+    near_list, far_list = near_list.T, far_list.T
     leaves, columns, size = sources.shape
     nodes = up_transfer.shape[0]
     far_slots, far_nodes = far_list.shape
@@ -375,7 +383,10 @@
         return lax.ppermute(x, axis, [(i, target(i)) for i in range(count)])
 
     def gathered(x):
-        return [x] + [permuted(x, "sub", lambda i, s=s: i ^ s) for s in (2, 1, 3)]
+        return [x] + [permuted(x, "sub", lambda i, s=s: i ^ s) for s in SUB_ORDER]
+
+    def exchanged(parts, unit):
+        return (parts[0],) + tuple(permuted(parts[s], "leaf", lambda i, s=s: i ^ (s * unit)) for s in PLANE_ORDER)
 
     coef, group, top = call(
         up_kernel, "upward", 4, (shape(nodes), shape(), shape(TOP_TERMS + 1)),
@@ -406,22 +417,29 @@
         [pltpu.SMEM((near_slots, leaves), jnp.int32)] + accumulators(leaves) + [copies(1)],
     )
     half = groups // 2 * 4
+    window = shape(leaves + far_nodes)
     everyone = ("leaf", "sub")
     from_prev = permuted(to_next, everyone, lambda i: (i + 1) % devices)
-    from_next = permuted(to_prev, everyone, lambda i: (i - 1) % devices)
-
+    total = call(merge_kernel, "merge", 4, window, (own, from_prev), [VMEM] * 2, [])
     keep, send = call(
         pack_kernel, "pack", 0, (shape(half), shape(half)), (*term_parts, own), [VMEM] * 4 + [ANY],
         [pltpu.SMEM((subs,) + row, F32)] + [plane(2 * half + 1)] * 4 + [copies(subs)],
     )
     from_core = permuted(send, "leaf", lambda i: i ^ 1)
-    planes = call(core_kernel, "core", 0, shape(groups // 2, 4), (keep, from_core), [VMEM] * 2, [])
-    fields = lax.all_to_all(
-        planes, "leaf", 0, 0, tiled=True, axis_index_groups=[list(range(c, groups, 2)) for c in range(2)]
+    y_unit, z_unit = groups // 4, groups // 16
+    *by_y, to_prev = call(
+        functools.partial(split_kernel, y_unit, 1), "split_y", 1, (shape(half // 4),) * 4 + (window,),
+        (keep, from_core, to_prev), [VMEM] * 2 + [ANY], [],
+        out_specs=(VMEM,) * 4 + (ANY,), input_output_aliases={2: 4},
+    )
+    from_next = permuted(to_prev, everyone, lambda i: (i - 1) % devices)
+    by_z = call(
+        functools.partial(split_kernel, z_unit, 0), "split_z", 1, (shape(half // 16),) * 4,
+        exchanged(by_y, y_unit), [VMEM] * 4, [],
     )
     return call(
-        down_kernel, "downward", 0, shape(leaves), (fields, own, from_prev, from_next, down_transfer, col_basis), [VMEM] * 5 + [ANY],
-        [buffer(leaves), plane(nodes), copies(4)],
+        down_kernel, "downward", 0, shape(leaves),
+        (*exchanged(by_z, z_unit), total, from_next, down_transfer, col_basis), [VMEM] * 8, [plane(nodes)],
     )
 
 

time: 44.9 us -> 45.3 us (level)
  starting transfers between devices: 20.5 us -> 27.1 us
  waiting for transfers between devices: 10.3 us -> 6.85 us
  Pallas kernels: 13.7 us -> 11 us
    ppermute x9 -> x15, starting transfers between devices: 16.6 us -> 27.1 us  [permuted(): return lax.ppermute(x, axis, [(i, target(i)) for i in range(count)])]
    all_to_all x1 -> x0, waiting for transfers between devices: 5.1 us -> none  [shards(): lax.all_to_all(planes, 'leaf', 0, 0, tiled=True, axis_index_groups=[list(...]
    all_to_all x1 -> x0, starting transfers between devices: 3.87 us -> none  [shards(): lax.all_to_all(planes, 'leaf', 0, 0, tiled=True, axis_index_groups=[list(...]
    pallas_call x7 -> x9, Pallas kernels: 13.7 us -> 11 us  [call(): pl.pallas_call(kernel, out_shape=outs, in_specs=specs, out_specs=out_spec...]
    ppermute x9 -> x15, waiting for transfers between devices: 5.24 us -> 6.85 us  [permuted(): return lax.ppermute(x, axis, [(i, target(i)) for i in range(count)])]
  transfers between devices with their start and end apart: 10 -> 15, of which waited for: 3 -> 5; matrix products, arithmetic and copies ran while one was open for 0% -> 0% of each run, Pallas kernels for 15% -> 10%
where the time goes in v5:
time: 45.3 us; the launch traced here: 45.2 us
  starting transfers between devices  27.1 us (60%)
  Pallas kernels  11 us (24%)
  waiting for transfers between devices  6.85 us (15%)
    ppermute x15, starting transfers between devices, permuted(): return lax.ppermute(x, axis, [(i, target(i)) for i in range(count)])  27.1 us
    pallas_call x9, Pallas kernels, call(): pl.pallas_call(kernel, out_shape=outs, in_specs=specs, out_specs=out_spec...  11 us
    ppermute x15, waiting for transfers between devices, permuted(): return lax.ppermute(x, axis, [(i, target(i)) for i in range(count)])  6.85 us
  transfers between devices with their start and end apart: 15, of which 5 were waited for; matrix products, arithmetic and copies ran while one was open for 0% of the time, Pallas kernels for 10%

profile of v5, /device:TPU:0, one launch (start us, length us, event | category | flops | bytes accessed | tf_op | source)
XLA Modules:
  0.0 45.2 jit_solution(9898563722806319971)
XLA Ops:
  0.0 3.3 %upward.1 = (f32[63,8,128]{2,1,0:T(8,128)S(1)}, f32[8,128]{1,0:T(8,128)S(1)}, f32[13,8,128]{2,1,0:T(8,128)S(1)}) custom-call(bf16[32,8,128]{2,1,0:T(8,128)(2,1)} %src_ref.1, s32[2,4]{1,0:T(2,128)} %upper_list_hbm.1, s32[1,4]{1,0:T(1,128)} %root_list_hbm.1, bf16[32,128,128]{2,1,0:T(8,128)(2,1)} %rb_hbm.1, bf16[63,128,128]{2,1,0:T(8,128)(2,1)} %up_hbm.1, ...), custom_call_target="tpu_custom_call" | custom-call | flops 4000000000 | tf_op jit(solution)/shard_map/upward/pallas_call | solution.py:367
  3.3 0.0 copy-start.3
  3.3 0.0 copy-start.7
  3.4 2.9 %collective-permute-start = (f32[8,128]{1,0:T(8,128)S(1)}, f32[8,128]{1,0:T(8,128)S(1)}, u32[]{:S(2)}, u32[]{:S(2)}) collective-permute-start(f32[8,128]{1,0:T(8,128)S(1)} %get-tuple-element.25.g0.order), channel_id=1, source_target_pairs={{0,3},{1,2},{2,1},{3,0},{4,7},{5,6},{6,5},{7,4},{8,11},{9,10},{10,... | collective-permute-start | bytes 12296 | tf_op jit(solution)/shard_map/ppermute | solution.py:383
  6.3 0.2 collective-permute-start.1
  6.5 1.6 %collective-permute-start.2 = (f32[8,128]{1,0:T(8,128)S(1)}, f32[8,128]{1,0:T(8,128)S(1)}, u32[]{:S(2)}, u32[]{:S(2)}) collective-permute-start(f32[8,128]{1,0:T(8,128)S(1)} %get-tuple-element.25.g0.order), channel_id=1, source_target_pairs={{0,2},{1,3},{2,0},{3,1},{4,6},{5,7},{6,4},{7,5},{8,10},{9,11},{10,... | collective-permute-start | bytes 12296 | tf_op jit(solution)/shard_map/ppermute | solution.py:383
  8.1 0.0 copy-done.6
  8.1 0.0 copy-done.2
  8.2 0.0 copy-start.5
  8.2 2.2 %far.2 = (f32[60,8,128]{2,1,0:T(8,128)S(1)}, f32[60,8,128]{2,1,0:T(8,128)S(1)}, f32[60,8,128]{2,1,0:T(8,128)S(1)}) custom-call(f32[63,8,128]{2,1,0:T(8,128)S(1)} %get-tuple-element.27.coef_ref, s32[4,60]{1,0:T(4,128)S(1)} %bitcast.5, bf16[240,128,128]{2,1,0:T(8,128)(2,1)S(1)} %copy-done.2, f32[8,128]{1,0:T(8,128)S(1)} %get-tuple-element.25.g0.order), custom_call_target="tpu_custom_call" | custom-call | flops 4000000000 | tf_op jit(solution)/shard_map/far/pallas_call | solution.py:367
  10.3 0.0 collective-permute-done.g1
  10.4 0.0 collective-permute-done.1.g2
  10.4 1.3 %collective-permute-done.2.g3 = f32[8,128]{1,0:T(8,128)S(1)} collective-permute-done((f32[8,128]{1,0:T(8,128)S(1)}, f32[8,128]{1,0:T(8,128)S(1)}, u32[]{:S(2)}, u32[]{:S(2)}) %collective-permute-start.2) | collective-permute-done | bytes 4128 | tf_op jit(solution)/shard_map/ppermute | solution.py:383
  11.6 0.0 copy-done.3
  11.6 0.0 copy-done.7
  11.6 0.1 group.1.order.p0
  11.8 1.6 %collective-permute-start.3 = (f32[17,8,128]{2,1,0:T(8,128)S(1)}, f32[17,8,128]{2,1,0:T(8,128)S(1)}, u32[]{:S(2)}, u32[]{:S(2)}) collective-permute-start(f32[17,8,128]{2,1,0:T(8,128)S(1)} %group.1.order.p0), channel_id=1, source_target_pairs={{0,3},{1,2},{2,1},{3,0},{4,7},{5,6},{6,5},{7,4},{8,11},{9,10},{10,... | collective-permute-start | bytes 208904 | tf_op jit(solution)/shard_map/ppermute | solution.py:383
  13.4 0.3 collective-permute-start.4
  13.7 2.8 %collective-permute-start.5 = (f32[17,8,128]{2,1,0:T(8,128)S(1)}, f32[17,8,128]{2,1,0:T(8,128)S(1)}, u32[]{:S(2)}, u32[]{:S(2)}) collective-permute-start(f32[17,8,128]{2,1,0:T(8,128)S(1)} %group.1.order.p0), channel_id=1, source_target_pairs={{0,2},{1,3},{2,0},{3,1},{4,6},{5,7},{6,4},{7,5},{8,10},{9,11},{10,... | collective-permute-start | bytes 208904 | tf_op jit(solution)/shard_map/ppermute | solution.py:383
  16.5 0.0 slice-done
  16.5 0.0 copy-done.5
  16.5 2.3 %near.2 = (f32[92,8,128]{2,1,0:T(8,128)S(1)}, f32[92,8,128]{2,1,0:T(8,128)S(1)}, f32[92,8,128]{2,1,0:T(8,128)S(1)}) custom-call(bf16[32,8,128]{2,1,0:T(8,128)(2,1)S(1)} %copy-done.4, s32[8,32]{1,0:T(8,128)S(1)} %bitcast.4, bf16[256,128,128]{2,1,0:T(8,128)(2,1)S(1)} %bitcast.3, f32[60,8,128]{2,1,0:T(8,128)S(1)} %get-tuple-element.28.far_prev, ...), custom_call_target="tpu_custom_call" | custom-call | flops 4000000000 | tf_op jit(solution)/shard_map/near/pallas_call | solution.py:367
  18.8 0.0 collective-permute-done.3.p1
  18.8 0.0 collective-permute-done.4.p2
  18.8 0.7 %collective-permute-done.5.p3 = f32[17,8,128]{2,1,0:T(8,128)S(1)} collective-permute-done((f32[17,8,128]{2,1,0:T(8,128)S(1)}, f32[17,8,128]{2,1,0:T(8,128)S(1)}, u32[]{:S(2)}, u32[]{:S(2)}) %collective-permute-start.5) | collective-permute-done | bytes 69664 | tf_op jit(solution)/shard_map/ppermute | solution.py:383
  19.5 1.3 %pack.1 = (f32[64,8,128]{2,1,0:T(8,128)S(1)}, f32[64,8,128]{2,1,0:T(8,128)S(1)}) custom-call(f32[17,8,128]{2,1,0:T(8,128)S(1)} %group.1.order.p0, f32[17,8,128]{2,1,0:T(8,128)S(1)} %collective-permute-done.3.p1, f32[17,8,128]{2,1,0:T(8,128)S(1)} %collective-permute-done.4.p2, f32[17,8,128]{2,1,0:T(8,128)S(1)} %collective-permute-done.5.p3, ...), custom_call_target="tpu_custom_call" | custom-call | tf_op jit(solution)/shard_map/pack/pallas_call | solution.py:367
  20.8 0.1 collective-permute-start.6
  20.9 1.8 %collective-permute-start.13 = (f32[92,8,128]{2,1,0:T(8,128)S(1)}, f32[92,8,128]{2,1,0:T(8,128)S(1)}, u32[]{:S(2)}, u32[]{:S(2)}) collective-permute-start(f32[92,8,128]{2,1,0:T(8,128)S(1)} %get-tuple-element.43), channel_id=1, source_target_pairs={{0,1},{1,2},{2,3},{3,4},{4,5},{5,6},{6,7},{7,8},{8,9},{9,10},{10,1... | collective-permute-start | bytes 1130504 | tf_op jit(solution)/shard_map/ppermute | solution.py:383
  22.7 0.0 collective-permute-done.6.refs_1_
  22.7 3.3 %collective-permute-start.7 = (f32[16,8,128]{2,1,0:T(8,128)S(1)}, f32[16,8,128]{2,1,0:T(8,128)S(1)}, u32[]{:S(2)}, u32[]{:S(2)}) collective-permute-start(f32[16,8,128]{2,1,0:T(8,128)S(1)} %get-tuple-element.36), channel_id=1, source_target_pairs={{0,64},{4,68},{8,72},{12,76},{16,80},{20,84},{24,88},{28,92},{32,9... | collective-permute-start | bytes 196616 | tf_op jit(solution)/shard_map/ppermute | solution.py:383
  26.0 0.7 %collective-permute-start.8 = (f32[16,8,128]{2,1,0:T(8,128)S(1)}, f32[16,8,128]{2,1,0:T(8,128)S(1)}, u32[]{:S(2)}, u32[]{:S(2)}) collective-permute-start(f32[16,8,128]{2,1,0:T(8,128)S(1)} %get-tuple-element.37), channel_id=1, source_target_pairs={{0,32},{4,36},{8,40},{12,44},{16,48},{20,52},{24,56},{28,60},{32,0... | collective-permute-start | bytes 196616 | tf_op jit(solution)/shard_map/ppermute | solution.py:383
  26.7 0.4 collective-permute-start.9
  27.1 6.9 %collective-permute-start.14 = (f32[92,8,128]{2,1,0:T(8,128)S(1)}, f32[92,8,128]{2,1,0:T(8,128)S(1)}, u32[]{:S(2)}, u32[]{:S(2)}) collective-permute-start(f32[92,8,128]{2,1,0:T(8,128)S(1)} %get-tuple-element.44), channel_id=1, source_target_pairs={{0,127},{1,0},{2,1},{3,2},{4,3},{5,4},{6,5},{7,6},{8,7},{9,8},{10,... | collective-permute-start | bytes 1130504 | tf_op jit(solution)/shard_map/ppermute | solution.py:383
  34.0 0.0 collective-permute-done.7.refs_1_
  34.0 0.0 collective-permute-done.8.refs_2_
  34.0 0.0 collective-permute-done.9.refs_3_
  34.0 0.0 copy-start
  34.0 0.0 copy-start.1
  34.0 2.1 %collective-permute-start.10 = (f32[4,8,128]{2,1,0:T(8,128)S(1)}, f32[4,8,128]{2,1,0:T(8,128)S(1)}, u32[]{:S(2)}, u32[]{:S(2)}) collective-permute-start(f32[4,8,128]{2,1,0:T(8,128)S(1)} %get-tuple-element.40), channel_id=1, source_target_pairs={{0,16},{4,20},{8,24},{12,28},{16,0},{20,4},{24,8},{28,12},{32,48},... | collective-permute-start | bytes 49160 | tf_op jit(solution)/shard_map/ppermute | solution.py:383
  36.2 2.4 %collective-permute-start.11 = (f32[4,8,128]{2,1,0:T(8,128)S(1)}, f32[4,8,128]{2,1,0:T(8,128)S(1)}, u32[]{:S(2)}, u32[]{:S(2)}) collective-permute-start(f32[4,8,128]{2,1,0:T(8,128)S(1)} %get-tuple-element.41), channel_id=1, source_target_pairs={{0,8},{4,12},{8,0},{12,4},{16,24},{20,28},{24,16},{28,20},{32,40},... | collective-permute-start | bytes 49160 | tf_op jit(solution)/shard_map/ppermute | solution.py:383
  38.6 0.0 collective-permute-start.12
  38.6 0.0 collective-permute-done.13.prev_ref
  38.6 0.1 merge.1.own
  38.6 0.8 %collective-permute-done.10.t1 = f32[4,8,128]{2,1,0:T(8,128)S(1)} collective-permute-done((f32[4,8,128]{2,1,0:T(8,128)S(1)}, f32[4,8,128]{2,1,0:T(8,128)S(1)}, u32[]{:S(2)}, u32[]{:S(2)}) %collective-permute-start.10) | collective-permute-done | bytes 16416 | tf_op jit(solution)/shard_map/ppermute | solution.py:383
  39.5 1.0 %collective-permute-done.11.t2 = f32[4,8,128]{2,1,0:T(8,128)S(1)} collective-permute-done((f32[4,8,128]{2,1,0:T(8,128)S(1)}, f32[4,8,128]{2,1,0:T(8,128)S(1)}, u32[]{:S(2)}, u32[]{:S(2)}) %collective-permute-start.11) | collective-permute-done | bytes 16416 | tf_op jit(solution)/shard_map/ppermute | solution.py:383
  40.4 3.1 %collective-permute-done.12.t3 = f32[4,8,128]{2,1,0:T(8,128)S(1)} collective-permute-done((f32[4,8,128]{2,1,0:T(8,128)S(1)}, f32[4,8,128]{2,1,0:T(8,128)S(1)}, u32[]{:S(2)}, u32[]{:S(2)}) %collective-permute-start.12) | collective-permute-done | bytes 16416 | tf_op jit(solution)/shard_map/ppermute | solution.py:383
  43.5 0.0 collective-permute-done.14.from_next
  43.5 1.7 %downward.1 = f32[32,8,128]{2,1,0:T(8,128)} custom-call(f32[4,8,128]{2,1,0:T(8,128)S(1)} %get-tuple-element.39.t0, f32[4,8,128]{2,1,0:T(8,128)S(1)} %collective-permute-done.10.t1, f32[4,8,128]{2,1,0:T(8,128)S(1)} %collective-permute-done.11.t2, f32[4,8,128]{2,1,0:T(8,128)S(1)} %collective-permute-done.12.t3, f32[92,8,128]{2,1,0:T(8,128)S(1)} %merge.1.own, ...), custom_call_target="tpu_custom_call" | custom-call | tf_op jit(solution)/shard_map/downward/pallas_call | solution.py:367
  (12 shorter events, 0.1 us)
Async XLA Ops:
  0.0 8.1 %copy-start.6 = (s32[60,4]{0,1:T(4,128)S(1)}, s32[60,4]{0,1:T(4,128)}, u32[]{:S(2)}) copy-start(s32[60,4]{0,1:T(4,128)} %param.23) | copy-start | bytes 2884
  0.0 8.1 %copy-start.2 = (bf16[240,128,128]{2,1,0:T(8,128)(2,1)S(1)}, bf16[240,128,128]{2,1,0:T(8,128)(2,1)}, u32[]{:S(2)}) copy-start(bf16[240,128,128]{2,1,0:T(8,128)(2,1)} %far.3) | copy-start | bytes 23592964
  0.0 16.5 %slice-start = ((s8[8388608]{0:T(1024)(128)(4,1)}), s8[4194304]{0:T(1024)(128)(4,1)S(1)}, s32[]{:S(2)}) async-start(s8[8388608]{0:T(1024)(128)(4,1)} %bitcast.2), calls=%async_computation | async-start | bytes 8388608
  3.3 8.3 %copy-start.3 = (bf16[4,128,128]{2,1,0:T(8,128)(2,1)S(1)}, bf16[4,128,128]{2,1,0:T(8,128)(2,1)}, u32[]{:S(2)}) copy-start(bf16[4,128,128]{2,1,0:T(8,128)(2,1)} %blocks.1) | copy-start | bytes 393220
  3.3 8.3 %copy-start.7 = (s32[1,4]{1,0:T(1,128)S(1)}, s32[1,4]{1,0:T(1,128)}, u32[]{:S(2)}) copy-start(s32[1,4]{1,0:T(1,128)} %group_list.1) | copy-start | bytes 52
  3.4 7.0 %collective-permute-start = (f32[8,128]{1,0:T(8,128)S(1)}, f32[8,128]{1,0:T(8,128)S(1)}, u32[]{:S(2)}, u32[]{:S(2)}) collective-permute-start(f32[8,128]{1,0:T(8,128)S(1)} %get-tuple-element.25.g0.order), channel_id=1, source_target_pairs={{0,3},{1,2},{2,1},{3,0},{4,7},{5,6},{6,5},{7,4},{8,11},{9,10},{10,... | collective-permute-start | bytes 12296 | tf_op jit(solution)/shard_map/ppermute | solution.py:383
  6.3 4.1 %collective-permute-start.1 = (f32[8,128]{1,0:T(8,128)S(1)}, f32[8,128]{1,0:T(8,128)S(1)}, u32[]{:S(2)}, u32[]{:S(2)}) collective-permute-start(f32[8,128]{1,0:T(8,128)S(1)} %get-tuple-element.25.g0.order), channel_id=1, source_target_pairs={{0,1},{1,0},{2,3},{3,2},{4,5},{5,4},{6,7},{7,6},{8,9},{9,8},{10,11... | collective-permute-start | bytes 12296 | tf_op jit(solution)/shard_map/ppermute | solution.py:383
  6.5 5.1 %collective-permute-start.2 = (f32[8,128]{1,0:T(8,128)S(1)}, f32[8,128]{1,0:T(8,128)S(1)}, u32[]{:S(2)}, u32[]{:S(2)}) collective-permute-start(f32[8,128]{1,0:T(8,128)S(1)} %get-tuple-element.25.g0.order), channel_id=1, source_target_pairs={{0,2},{1,3},{2,0},{3,1},{4,6},{5,7},{6,4},{7,5},{8,10},{9,11},{10,... | collective-permute-start | bytes 12296 | tf_op jit(solution)/shard_map/ppermute | solution.py:383
  8.1 8.3 %slice-start.1 = ((s8[8388608]{0:T(1024)(128)(4,1)}), s8[4194304]{0:T(1024)(128)(4,1)S(1)}, s32[]{:S(2)}) async-start(s8[8388608]{0:T(1024)(128)(4,1)} %bitcast.2), calls=%async_computation.1 | async-start | bytes 8388608
  8.1 8.3 %copy-start.4 = (bf16[32,8,128]{2,1,0:T(8,128)(2,1)S(1)}, bf16[32,8,128]{2,1,0:T(8,128)(2,1)}, u32[]{:S(2)}) copy-start(bf16[32,8,128]{2,1,0:T(8,128)(2,1)} %src_ref.1) | copy-start | bytes 196612
  8.2 8.3 %copy-start.5 = (s32[32,8]{0,1:T(8,128)S(1)}, s32[32,8]{0,1:T(8,128)}, u32[]{:S(2)}) copy-start(s32[32,8]{0,1:T(8,128)} %param.21) | copy-start | bytes 3076
  11.8 7.0 %collective-permute-start.3 = (f32[17,8,128]{2,1,0:T(8,128)S(1)}, f32[17,8,128]{2,1,0:T(8,128)S(1)}, u32[]{:S(2)}, u32[]{:S(2)}) collective-permute-start(f32[17,8,128]{2,1,0:T(8,128)S(1)} %group.1.order.p0), channel_id=1, source_target_pairs={{0,3},{1,2},{2,1},{3,0},{4,7},{5,6},{6,5},{7,4},{8,11},{9,10},{10,... | collective-permute-start | bytes 208904 | tf_op jit(solution)/shard_map/ppermute | solution.py:383
  13.4 5.4 %collective-permute-start.4 = (f32[17,8,128]{2,1,0:T(8,128)S(1)}, f32[17,8,128]{2,1,0:T(8,128)S(1)}, u32[]{:S(2)}, u32[]{:S(2)}) collective-permute-start(f32[17,8,128]{2,1,0:T(8,128)S(1)} %group.1.order.p0), channel_id=1, source_target_pairs={{0,1},{1,0},{2,3},{3,2},{4,5},{5,4},{6,7},{7,6},{8,9},{9,8},{10,11... | collective-permute-start | bytes 208904 | tf_op jit(solution)/shard_map/ppermute | solution.py:383
  13.7 5.8 %collective-permute-start.5 = (f32[17,8,128]{2,1,0:T(8,128)S(1)}, f32[17,8,128]{2,1,0:T(8,128)S(1)}, u32[]{:S(2)}, u32[]{:S(2)}) collective-permute-start(f32[17,8,128]{2,1,0:T(8,128)S(1)} %group.1.order.p0), channel_id=1, source_target_pairs={{0,2},{1,3},{2,0},{3,1},{4,6},{5,7},{6,4},{7,5},{8,10},{9,11},{10,... | collective-permute-start | bytes 208904 | tf_op jit(solution)/shard_map/ppermute | solution.py:383
  20.8 1.9 %collective-permute-start.6 = (f32[64,8,128]{2,1,0:T(8,128)S(1)}, f32[64,8,128]{2,1,0:T(8,128)S(1)}, u32[]{:S(2)}, u32[]{:S(2)}) collective-permute-start(f32[64,8,128]{2,1,0:T(8,128)S(1)} %get-tuple-element.33), channel_id=1, source_target_pairs={{0,4},{4,0},{8,12},{12,8},{16,20},{20,16},{24,28},{28,24},{32,36},... | collective-permute-start | bytes 786440 | tf_op jit(solution)/shard_map/ppermute | solution.py:383
  20.9 17.7 %collective-permute-start.13 = (f32[92,8,128]{2,1,0:T(8,128)S(1)}, f32[92,8,128]{2,1,0:T(8,128)S(1)}, u32[]{:S(2)}, u32[]{:S(2)}) collective-permute-start(f32[92,8,128]{2,1,0:T(8,128)S(1)} %get-tuple-element.43), channel_id=1, source_target_pairs={{0,1},{1,2},{2,3},{3,4},{4,5},{5,6},{6,7},{7,8},{8,9},{9,10},{10,1... | collective-permute-start | bytes 1130504 | tf_op jit(solution)/shard_map/ppermute | solution.py:383
  22.7 11.2 %collective-permute-start.7 = (f32[16,8,128]{2,1,0:T(8,128)S(1)}, f32[16,8,128]{2,1,0:T(8,128)S(1)}, u32[]{:S(2)}, u32[]{:S(2)}) collective-permute-start(f32[16,8,128]{2,1,0:T(8,128)S(1)} %get-tuple-element.36), channel_id=1, source_target_pairs={{0,64},{4,68},{8,72},{12,76},{16,80},{20,84},{24,88},{28,92},{32,9... | collective-permute-start | bytes 196616 | tf_op jit(solution)/shard_map/ppermute | solution.py:383
  26.0 8.0 %collective-permute-start.8 = (f32[16,8,128]{2,1,0:T(8,128)S(1)}, f32[16,8,128]{2,1,0:T(8,128)S(1)}, u32[]{:S(2)}, u32[]{:S(2)}) collective-permute-start(f32[16,8,128]{2,1,0:T(8,128)S(1)} %get-tuple-element.37), channel_id=1, source_target_pairs={{0,32},{4,36},{8,40},{12,44},{16,48},{20,52},{24,56},{28,60},{32,0... | collective-permute-start | bytes 196616 | tf_op jit(solution)/shard_map/ppermute | solution.py:383
  26.7 7.3 %collective-permute-start.9 = (f32[16,8,128]{2,1,0:T(8,128)S(1)}, f32[16,8,128]{2,1,0:T(8,128)S(1)}, u32[]{:S(2)}, u32[]{:S(2)}) collective-permute-start(f32[16,8,128]{2,1,0:T(8,128)S(1)} %get-tuple-element.38), channel_id=1, source_target_pairs={{0,96},{4,100},{8,104},{12,108},{16,112},{20,116},{24,120},{28,124... | collective-permute-start | bytes 196616 | tf_op jit(solution)/shard_map/ppermute | solution.py:383
  27.1 16.5 %collective-permute-start.14 = (f32[92,8,128]{2,1,0:T(8,128)S(1)}, f32[92,8,128]{2,1,0:T(8,128)S(1)}, u32[]{:S(2)}, u32[]{:S(2)}) collective-permute-start(f32[92,8,128]{2,1,0:T(8,128)S(1)} %get-tuple-element.44), channel_id=1, source_target_pairs={{0,127},{1,0},{2,1},{3,2},{4,3},{5,4},{6,5},{7,6},{8,7},{9,8},{10,... | collective-permute-start | bytes 1130504 | tf_op jit(solution)/shard_map/ppermute | solution.py:383
  34.0 9.5 %copy-start = (bf16[63,128,128]{2,1,0:T(8,128)(2,1)S(1)}, bf16[63,128,128]{2,1,0:T(8,128)(2,1)}, u32[]{:S(2)}) copy-start(bf16[63,128,128]{2,1,0:T(8,128)(2,1)} %down.1) | copy-start | bytes 6193156
  34.0 9.5 %copy-start.1 = (bf16[32,128,128]{2,1,0:T(8,128)(2,1)S(1)}, bf16[32,128,128]{2,1,0:T(8,128)(2,1)}, u32[]{:S(2)}) copy-start(bf16[32,128,128]{2,1,0:T(8,128)(2,1)} %col.1) | copy-start | bytes 3145732
  34.0 5.4 %collective-permute-start.10 = (f32[4,8,128]{2,1,0:T(8,128)S(1)}, f32[4,8,128]{2,1,0:T(8,128)S(1)}, u32[]{:S(2)}, u32[]{:S(2)}) collective-permute-start(f32[4,8,128]{2,1,0:T(8,128)S(1)} %get-tuple-element.40), channel_id=1, source_target_pairs={{0,16},{4,20},{8,24},{12,28},{16,0},{20,4},{24,8},{28,12},{32,48},... | collective-permute-start | bytes 49160 | tf_op jit(solution)/shard_map/ppermute | solution.py:383
  36.2 4.3 %collective-permute-start.11 = (f32[4,8,128]{2,1,0:T(8,128)S(1)}, f32[4,8,128]{2,1,0:T(8,128)S(1)}, u32[]{:S(2)}, u32[]{:S(2)}) collective-permute-start(f32[4,8,128]{2,1,0:T(8,128)S(1)} %get-tuple-element.41), channel_id=1, source_target_pairs={{0,8},{4,12},{8,0},{12,4},{16,24},{20,28},{24,16},{28,20},{32,40},... | collective-permute-start | bytes 49160 | tf_op jit(solution)/shard_map/ppermute | solution.py:383
  38.6 4.9 %collective-permute-start.12 = (f32[4,8,128]{2,1,0:T(8,128)S(1)}, f32[4,8,128]{2,1,0:T(8,128)S(1)}, u32[]{:S(2)}, u32[]{:S(2)}) collective-permute-start(f32[4,8,128]{2,1,0:T(8,128)S(1)} %get-tuple-element.42), channel_id=1, source_target_pairs={{0,24},{4,28},{8,16},{12,20},{16,8},{20,12},{24,0},{28,4},{32,56},... | collective-permute-start | bytes 49160 | tf_op jit(solution)/shard_map/ppermute | solution.py:383

commit v6 on v4

--- a/solution.py
+++ b/solution.py
@@ -14,7 +14,7 @@
 REPLICAS = 4
 UPPER_TERMS, ROOT_TERMS, GROUP_TERMS = 8, 4, 4
 TOP_TERMS = UPPER_TERMS + ROOT_TERMS
-TERMS = TOP_TERMS + GROUP_TERMS
+GROUP_ROW, ID_ROW, PAYLOAD = TOP_TERMS, TOP_TERMS + 1, TOP_TERMS + 2
 
 
 def rounded(x):
@@ -75,8 +75,8 @@
 
 
 def up_kernel(
-    src_hbm, upper_list_hbm, root_list_hbm, rb_hbm, up_hbm, ub_hbm, rt_hbm,
-    coef_ref, group_ref, top_ref, src, upper_list, root_list, rb, up, ub, rt, sem,
+    src_hbm, upper_list_hbm, root_list_hbm, group_list_hbm, rb_hbm, up_hbm, ub_hbm, rt_hbm,
+    coef_ref, top_ref, src, upper_list, root_list, group_list, rb, up, ub, rt, sem,
 ):
     leaves = src.shape[0]
     levels = leaves.bit_length() - 1
@@ -85,10 +85,10 @@
     src_copy = fetch(src_hbm, src)
     rb_copies = [fetch.rows(rb_hbm, rb, i * quarter, quarter) for i in range(4)]
     up_copies = [fetch.rows(up_hbm, up, i * quarter, quarter) for i in range(4)]
-    rest = fetch.rows(up_hbm, up, leaves, leaves - 1)
+    rest = [fetch.rows(up_hbm, up, leaves, leaves // 2), fetch.rows(up_hbm, up, leaves + leaves // 2, leaves // 2 - 1)]
     tail = [
         fetch(ub_hbm, ub), fetch(rt_hbm, rt),
-        fetch(upper_list_hbm, upper_list), fetch(root_list_hbm, root_list),
+        fetch(upper_list_hbm, upper_list), fetch(root_list_hbm, root_list), fetch(group_list_hbm, group_list),
     ]
 
     src_copy.wait()
@@ -102,8 +102,8 @@
     for level in range(levels):
         width = leaves >> level
         offset = level_offset(leaves, level)
-        if level == 1:
-            rest.wait()
+        if level in (1, 2):
+            rest[level - 1].wait()
         for t in range(0, width, 4):
             if level == 0 and t % quarter == 0:
                 up_copies[t // quarter].wait()
@@ -123,7 +123,7 @@
                 coef_ref[parent] = rounded(out[:n, :m])
                 coef_ref[parent + 1] = rounded(out[n:, m:])
     top = 2 * leaves - 2
-    group_ref[...] = dot(coef_ref[top], up[top])
+    top_ref[GROUP_ROW] = dot(coef_ref[top], up[top])
     for c in tail:
         c.wait()
     n, m = src.shape[1:]
@@ -138,9 +138,10 @@
         out = dot(coef_ref[top], jnp.concatenate([rt[k], rt[k + 1]], axis=1))
         top_ref[UPPER_TERMS + k] = out[:, :m]
         top_ref[UPPER_TERMS + k + 1] = out[:, m:]
-    top_ref[TOP_TERMS] = jnp.zeros((n, m), F32)
-    top_ref[TOP_TERMS, 0:2, 0:4] = upper_list[...].astype(F32)
-    top_ref[TOP_TERMS, 2:3, 0:4] = root_list[...].astype(F32)
+    top_ref[ID_ROW] = jnp.zeros((n, m), F32)
+    top_ref[ID_ROW, 0:2, 0:4] = upper_list[...].astype(F32)
+    top_ref[ID_ROW, 2:3, 0:4] = root_list[...].astype(F32)
+    top_ref[ID_ROW, 3:4, 0:4] = group_list[...].astype(F32)
 
 
 def scatter_steps(left_of, mats, target_of, accs, slots, first, count, step, level, levels, start, span):
@@ -219,24 +220,21 @@
     store_totals(accs, nodes, (prev_ref, own_ref, next_ref))
 
 
-def group_kernel(g0, g1, g2, g3, top_ref, group_list, blocks, out_ref):
-    coef = (g0[...] + g1[...]) + (g2[...] + g3[...])
+def group_kernel(p0, p1, p2, p3, blocks, out_ref):
+    coef = (p0[GROUP_ROW] + p1[GROUP_ROW]) + (p2[GROUP_ROW] + p3[GROUP_ROW])
     parts = exact_parts(coef)
     m = coef.shape[1]
     for k in range(0, GROUP_TERMS, 2):
         out = exact_dot(parts, jnp.concatenate([blocks[k], blocks[k + 1]], axis=1))
-        out_ref[TOP_TERMS + k] = out[:, :m]
-        out_ref[TOP_TERMS + k + 1] = out[:, m:]
-    out_ref[0:TOP_TERMS] = top_ref[0:TOP_TERMS]
-    out_ref[TERMS] = top_ref[TOP_TERMS]
-    out_ref[TERMS, 3:4, 0:4] = group_list[...].astype(F32)
-
-
-def pack_kernel(p0, p1, p2, p3, order, keep_ref, send_ref, ids, a0, a1, a2, a3, sem):
+        out_ref[k] = out[:, :m]
+        out_ref[k + 1] = out[:, m:]
+
+
+def pack_kernel(p0, p1, p2, p3, g0, g1, g2, g3, order, keep_ref, send_ref, ids, a0, a1, a2, a3, sem):
     half = keep_ref.shape[0]
     parts = (p0, p1, p2, p3)
     accs = (a0, a1, a2, a3)
-    copies = [pltpu.make_async_copy(p.at[TERMS], ids.at[i], sem.at[i]) for i, p in enumerate(parts)]
+    copies = [pltpu.make_async_copy(p.at[ID_ROW], ids.at[i], sem.at[i]) for i, p in enumerate(parts)]
     for c in copies:
         c.start()
     for acc in accs:
@@ -263,9 +261,9 @@
             root = ids[i, 2, j].astype(jnp.int32)
             add(acc, root, 2, p[UPPER_TERMS + j])
     for j in range(GROUP_TERMS):
-        for i, (p, acc) in enumerate(zip(parts, accs)):
+        for i, (g, acc) in enumerate(zip((g0, g1, g2, g3), accs)):
             row = place(ids[i, 3, j].astype(jnp.int32), 3)
-            acc[row] = acc[row] + p[TOP_TERMS + j]
+            acc[row] = acc[row] + g[j]
 
     def total(first):
         part = pl.ds(first, half)
@@ -331,9 +329,10 @@
 ):
     in_hbm = functools.partial(pltpu.with_memory_space_constraint, memory_space=pltpu.HBM)
     up_sources, row_basis, up_transfer, col_basis = map(in_hbm, (sources, row_basis, up_transfer, col_basis))
-    near_list, far_list, upper_blocks, upper_list, root_blocks, root_list = map(
-        in_hbm, (near_list.T, far_list.T, upper_blocks, upper_list, root_blocks, root_list)
-    )
+    upper_blocks, upper_list, root_blocks, root_list, group_list = map(
+        in_hbm, (upper_blocks, upper_list, root_blocks, root_list, group_list)
+    )
+    near_list, far_list = near_list.T, far_list.T
     leaves, columns, size = sources.shape
     nodes = up_transfer.shape[0]
     far_slots, far_nodes = far_list.shape
@@ -377,26 +376,26 @@
     def gathered(x):
         return [x] + [permuted(x, "sub", lambda i, s=s: i ^ s) for s in (2, 1, 3)]
 
-    coef, group, top = call(
-        up_kernel, "upward", 4, (shape(nodes), shape(), shape(TOP_TERMS + 1)),
-        (up_sources, upper_list, root_list, row_basis, up_transfer, upper_blocks, root_blocks),
-        [ANY] * 7,
+    coef, top = call(
+        up_kernel, "upward", 4, (shape(nodes), shape(PAYLOAD)),
+        (up_sources, upper_list, root_list, group_list, row_basis, up_transfer, upper_blocks, root_blocks),
+        [ANY] * 8,
         [
             pltpu.VMEM((leaves,) + row, BF16),
             pltpu.VMEM(upper_list.shape, jnp.int32), pltpu.VMEM(root_list.shape, jnp.int32),
-            buffer(leaves), buffer(nodes), buffer(UPPER_TERMS), buffer(ROOT_TERMS), copies(14),
+            pltpu.VMEM(group_list.shape, jnp.int32),
+            buffer(leaves), buffer(nodes), buffer(UPPER_TERMS), buffer(ROOT_TERMS), copies(16),
         ],
     )
-    group_parts = gathered(group)
+    top_parts = gathered(top)
     far_prev, far_own, far_next = call(
         functools.partial(far_kernel, leaves), "far", 4, (shape(far_nodes),) * 3,
-        (coef, far_list, far_blocks, group),
+        (coef, far_list, far_blocks, top),
         [VMEM, ANY, VMEM, ANY],
         [pltpu.SMEM((far_slots, far_nodes), jnp.int32)] + accumulators(far_nodes) + [copies(1)],
     )
     terms = call(
-        group_kernel, "group", 1, shape(TERMS + 1), (*group_parts, top, group_list, group_blocks),
-        [VMEM] * 7, [],
+        group_kernel, "group", 1, shape(GROUP_TERMS), (*top_parts, group_blocks), [VMEM] * 5, []
     )
     term_parts = gathered(terms)
     to_prev, own, to_next = call(
@@ -411,7 +410,7 @@
     from_next = permuted(to_prev, everyone, lambda i: (i - 1) % devices)
 
     keep, send = call(
-        pack_kernel, "pack", 0, (shape(half), shape(half)), (*term_parts, own), [VMEM] * 4 + [ANY],
+        pack_kernel, "pack", 0, (shape(half), shape(half)), (*top_parts, *term_parts, own), [VMEM] * 8 + [ANY],
         [pltpu.SMEM((subs,) + row, F32)] + [plane(2 * half + 1)] * 4 + [copies(subs)],
     )
     from_core = permuted(send, "leaf", lambda i: i ^ 1)

time: 44.9 us -> 45.3 us (level)
  waiting for transfers between devices: 10.3 us -> 11.1 us
    all_to_all x1, waiting for transfers between devices: 5.1 us -> 5.82 us  [shards(): lax.all_to_all(planes, 'leaf', 0, 0, tiled=True, axis_index_groups=[list(...]
  transfers between devices with their start and end apart: 10 -> 10, of which waited for: 3 -> 4; matrix products, arithmetic and copies ran while one was open for 0% -> 0% of each run, Pallas kernels for 15% -> 13%
where the time goes in v6:
time: 45.3 us; the launch traced here: 45.1 us
  starting transfers between devices  20.5 us (45%)
  Pallas kernels  13.3 us (29%)
  waiting for transfers between devices  11.1 us (25%)
    ppermute x9, starting transfers between devices, permuted(): return lax.ppermute(x, axis, [(i, target(i)) for i in range(count)])  16.3 us
    pallas_call x7, Pallas kernels, call(): pl.pallas_call(kernel, out_shape=outs, in_specs=specs, out_specs=out_spec...  13.3 us
    all_to_all x1, waiting for transfers between devices, shards(): lax.all_to_all(planes, 'leaf', 0, 0, tiled=True, axis_index_groups=[list(...  5.82 us
    ppermute x9, waiting for transfers between devices, permuted(): return lax.ppermute(x, axis, [(i, target(i)) for i in range(count)])  5.33 us
    all_to_all x1, starting transfers between devices, shards(): lax.all_to_all(planes, 'leaf', 0, 0, tiled=True, axis_index_groups=[list(...  4.23 us
  transfers between devices with their start and end apart: 10, of which 4 were waited for; matrix products, arithmetic and copies ran while one was open for 0% of the time, Pallas kernels for 13%

profile of v6, /device:TPU:0, one launch (start us, length us, event | category | flops | bytes accessed | tf_op | source)
XLA Modules:
  0.0 45.1 jit_solution(6372382340508270163)
XLA Ops:
  0.0 0.0 copy-start.5
  0.0 0.0 copy-start.1
  0.0 0.0 slice-start
  0.0 3.4 %upward.1 = (f32[63,8,128]{2,1,0:T(8,128)S(1)}, f32[14,8,128]{2,1,0:T(8,128)S(1)}) custom-call(bf16[32,8,128]{2,1,0:T(8,128)(2,1)} %src_ref.1, s32[2,4]{1,0:T(2,128)} %upper_list_hbm.1, s32[1,4]{1,0:T(1,128)} %root_list_hbm.1, s32[1,4]{1,0:T(1,128)} %group_list_hbm.1, bf16[32,128,128]{2,1,0:T(8,128)(2,1)} %rb_hbm.1, bf16[63,128,128]{2,1,0:T(8,128)(2,1)} %up_hbm.1, ...), custom_call_target="tpu_custom_call" | custom-call | flops 4000000000 | tf_op jit(solution)/shard_map/upward/pallas_call | solution.py:358
  3.4 0.0 copy-start.2
  3.4 3.2 %collective-permute-start = (f32[14,8,128]{2,1,0:T(8,128)S(1)}, f32[14,8,128]{2,1,0:T(8,128)S(1)}, u32[]{:S(2)}, u32[]{:S(2)}) collective-permute-start(f32[14,8,128]{2,1,0:T(8,128)S(1)} %get-tuple-element.15.p0.order), channel_id=1, source_target_pairs={{0,2},{1,3},{2,0},{3,1},{4,6},{5,7},{6,4},{7,5},{8,10},{9,11},{10,... | collective-permute-start | bytes 172040 | tf_op jit(solution)/shard_map/ppermute | solution.py:374
  6.6 0.6 %collective-permute-start.1 = (f32[14,8,128]{2,1,0:T(8,128)S(1)}, f32[14,8,128]{2,1,0:T(8,128)S(1)}, u32[]{:S(2)}, u32[]{:S(2)}) collective-permute-start(f32[14,8,128]{2,1,0:T(8,128)S(1)} %get-tuple-element.15.p0.order), channel_id=1, source_target_pairs={{0,1},{1,0},{2,3},{3,2},{4,5},{5,4},{6,7},{7,6},{8,9},{9,8},{10,11... | collective-permute-start | bytes 172040 | tf_op jit(solution)/shard_map/ppermute | solution.py:374
  7.2 0.6 %collective-permute-start.2 = (f32[14,8,128]{2,1,0:T(8,128)S(1)}, f32[14,8,128]{2,1,0:T(8,128)S(1)}, u32[]{:S(2)}, u32[]{:S(2)}) collective-permute-start(f32[14,8,128]{2,1,0:T(8,128)S(1)} %get-tuple-element.15.p0.order), channel_id=1, source_target_pairs={{0,3},{1,2},{2,1},{3,0},{4,7},{5,6},{6,5},{7,4},{8,11},{9,10},{10,... | collective-permute-start | bytes 172040 | tf_op jit(solution)/shard_map/ppermute | solution.py:374
  7.7 0.0 copy-done.5
  7.7 0.0 copy-done.1
  7.7 0.0 slice-start.1
  7.8 0.0 copy-start.3
  7.8 0.0 copy-start.4
  7.8 2.2 %far.2 = (f32[60,8,128]{2,1,0:T(8,128)S(1)}, f32[60,8,128]{2,1,0:T(8,128)S(1)}, f32[60,8,128]{2,1,0:T(8,128)S(1)}) custom-call(f32[63,8,128]{2,1,0:T(8,128)S(1)} %get-tuple-element.16.coef_ref, s32[4,60]{1,0:T(4,128)S(1)} %bitcast.5, bf16[240,128,128]{2,1,0:T(8,128)(2,1)S(1)} %copy-done.1, f32[14,8,128]{2,1,0:T(8,128)S(1)} %get-tuple-element.15.p0.order), custom_call_target="tpu_custom_call" | custom-call | flops 4000000000 | tf_op jit(solution)/shard_map/far/pallas_call | solution.py:358
  9.9 0.0 collective-permute-done.p1
  10.0 0.8 %collective-permute-done.1.p2 = f32[14,8,128]{2,1,0:T(8,128)S(1)} collective-permute-done((f32[14,8,128]{2,1,0:T(8,128)S(1)}, f32[14,8,128]{2,1,0:T(8,128)S(1)}, u32[]{:S(2)}, u32[]{:S(2)}) %collective-permute-start.1) | collective-permute-done | bytes 57376 | tf_op jit(solution)/shard_map/ppermute | solution.py:374
  10.8 1.8 %collective-permute-done.2.p3 = f32[14,8,128]{2,1,0:T(8,128)S(1)} collective-permute-done((f32[14,8,128]{2,1,0:T(8,128)S(1)}, f32[14,8,128]{2,1,0:T(8,128)S(1)}, u32[]{:S(2)}, u32[]{:S(2)}) %collective-permute-start.2) | collective-permute-done | bytes 57376 | tf_op jit(solution)/shard_map/ppermute | solution.py:374
  12.6 0.0 copy-done.2
  12.6 0.1 group.1.order.g0
  12.7 0.8 %collective-permute-start.3 = (f32[4,8,128]{2,1,0:T(8,128)S(1)}, f32[4,8,128]{2,1,0:T(8,128)S(1)}, u32[]{:S(2)}, u32[]{:S(2)}) collective-permute-start(f32[4,8,128]{2,1,0:T(8,128)S(1)} %group.1.order.g0), channel_id=1, source_target_pairs={{0,2},{1,3},{2,0},{3,1},{4,6},{5,7},{6,4},{7,5},{8,10},{9,11},{10,... | collective-permute-start | bytes 49160 | tf_op jit(solution)/shard_map/ppermute | solution.py:374
  13.5 0.7 %collective-permute-start.4 = (f32[4,8,128]{2,1,0:T(8,128)S(1)}, f32[4,8,128]{2,1,0:T(8,128)S(1)}, u32[]{:S(2)}, u32[]{:S(2)}) collective-permute-start(f32[4,8,128]{2,1,0:T(8,128)S(1)} %group.1.order.g0), channel_id=1, source_target_pairs={{0,1},{1,0},{2,3},{3,2},{4,5},{5,4},{6,7},{7,6},{8,9},{9,8},{10,11... | collective-permute-start | bytes 49160 | tf_op jit(solution)/shard_map/ppermute | solution.py:374
  14.2 2.6 %collective-permute-start.5 = (f32[4,8,128]{2,1,0:T(8,128)S(1)}, f32[4,8,128]{2,1,0:T(8,128)S(1)}, u32[]{:S(2)}, u32[]{:S(2)}) collective-permute-start(f32[4,8,128]{2,1,0:T(8,128)S(1)} %group.1.order.g0), channel_id=1, source_target_pairs={{0,3},{1,2},{2,1},{3,0},{4,7},{5,6},{6,5},{7,4},{8,11},{9,10},{10,... | collective-permute-start | bytes 49160 | tf_op jit(solution)/shard_map/ppermute | solution.py:374
  16.8 0.0 slice-done
  16.8 0.0 slice-done.1
  16.8 0.0 copy-done.3
  16.8 0.0 copy-done.4
  16.8 0.0 copy-start
  16.9 3.1 %near.2 = (f32[92,8,128]{2,1,0:T(8,128)}, f32[92,8,128]{2,1,0:T(8,128)S(1)}, f32[92,8,128]{2,1,0:T(8,128)}) custom-call(bf16[32,8,128]{2,1,0:T(8,128)(2,1)S(1)} %copy-done.3, s32[8,32]{1,0:T(8,128)S(1)} %bitcast.4, bf16[256,128,128]{2,1,0:T(8,128)(2,1)S(1)} %bitcast.3, f32[60,8,128]{2,1,0:T(8,128)S(1)} %get-tuple-element.17.far_prev, ...), custom_call_target="tpu_custom_call" | custom-call | flops 4000000000 | tf_op jit(solution)/shard_map/near/pallas_call | solution.py:358
  20.0 0.0 collective-permute-done.3.g1
  20.0 0.0 collective-permute-done.4.g2
  20.0 0.0 collective-permute-done.5.g3
  20.0 1.3 %pack.1 = (f32[64,8,128]{2,1,0:T(8,128)S(1)}, f32[64,8,128]{2,1,0:T(8,128)S(1)}) custom-call(f32[14,8,128]{2,1,0:T(8,128)S(1)} %get-tuple-element.15.p0.order, f32[14,8,128]{2,1,0:T(8,128)S(1)} %collective-permute-done.p1, f32[14,8,128]{2,1,0:T(8,128)S(1)} %collective-permute-done.1.p2, f32[14,8,128]{2,1,0:T(8,128)S(1)} %collective-permute-done.2.p3, ...), custom_call_target="tpu_custom_call" | custom-call | tf_op jit(solution)/shard_map/pack/pallas_call | solution.py:358
  21.3 0.1 collective-permute-start.6
  21.4 0.3 collective-permute-start.7
  21.7 7.5 %collective-permute-start.8 = (f32[92,8,128]{2,1,0:T(8,128)}, f32[92,8,128]{2,1,0:T(8,128)S(1)}, u32[]{:S(2)}, u32[]{:S(2)}) collective-permute-start(f32[92,8,128]{2,1,0:T(8,128)} %get-tuple-element.24), channel_id=1, source_target_pairs={{0,127},{1,0},{2,1},{3,2},{4,3},{5,4},{6,5},{7,6},{8,7},{9,8},{10,... | collective-permute-start | bytes 1130504 | tf_op jit(solution)/shard_map/ppermute | solution.py:374
  29.2 0.0 collective-permute-done.6.core_ref
  29.2 0.7 %core.1 = f32[16,4,8,128]{3,2,1,0:T(8,128)} custom-call(f32[64,8,128]{2,1,0:T(8,128)S(1)} %get-tuple-element.21.keep_ref, f32[64,8,128]{2,1,0:T(8,128)S(1)} %collective-permute-done.6.core_ref), custom_call_target="tpu_custom_call" | custom-call | tf_op jit(solution)/shard_map/core/pallas_call | solution.py:358
  29.9 4.2 %all-to-all-start = ((f32[16,4,8,128]{3,2,1,0:T(8,128)}), f32[16,4,8,128]{3,2,1,0:T(8,128)S(1)}, u32[]{:S(2)}, u32[]{:S(2)}) async-start(f32[16,4,8,128]{3,2,1,0:T(8,128)} %core.1), calls=%async_computation | async-start | bytes 524288 | tf_op jit(solution)/shard_map/all_to_all | solution.py:418
  34.2 2.7 %collective-permute-done.7.from_prev = f32[92,8,128]{2,1,0:T(8,128)S(1)} collective-permute-done((f32[92,8,128]{2,1,0:T(8,128)}, f32[92,8,128]{2,1,0:T(8,128)S(1)}, u32[]{:S(2)}, u32[]{:S(2)}) %collective-permute-start.7) | collective-permute-done | bytes 376864 | tf_op jit(solution)/shard_map/ppermute | solution.py:374
  36.9 0.0 collective-permute-done.8.from_next
  36.9 5.8 %all-to-all-done.top = f32[16,4,8,128]{3,2,1,0:T(8,128)S(1)} async-done(((f32[16,4,8,128]{3,2,1,0:T(8,128)}), f32[16,4,8,128]{3,2,1,0:T(8,128)S(1)}, u32[]{:S(2)}, u32[]{:S(2)}) %all-to-all-start) | async-done | bytes 262176 | tf_op jit(solution)/shard_map/all_to_all | solution.py:418
  42.7 0.0 copy-done
  42.7 2.4 %downward.1 = f32[32,8,128]{2,1,0:T(8,128)} custom-call(f32[16,4,8,128]{3,2,1,0:T(8,128)S(1)} %all-to-all-done.top, f32[92,8,128]{2,1,0:T(8,128)S(1)} %get-tuple-element.20.order.own, f32[92,8,128]{2,1,0:T(8,128)S(1)} %collective-permute-done.7.from_prev, f32[92,8,128]{2,1,0:T(8,128)S(1)} %collective-permute-done.8.from_next, ...), custom_call_target="tpu_custom_call" | custom-call | tf_op jit(solution)/shard_map/downward/pallas_call | solution.py:358
  (1 shorter events, 0.0 us)
Async XLA Ops:
  0.0 7.7 %copy-start.5 = (s32[60,4]{0,1:T(4,128)S(1)}, s32[60,4]{0,1:T(4,128)}, u32[]{:S(2)}) copy-start(s32[60,4]{0,1:T(4,128)} %param.23) | copy-start | bytes 2884
  0.0 7.7 %copy-start.1 = (bf16[240,128,128]{2,1,0:T(8,128)(2,1)S(1)}, bf16[240,128,128]{2,1,0:T(8,128)(2,1)}, u32[]{:S(2)}) copy-start(bf16[240,128,128]{2,1,0:T(8,128)(2,1)} %far.3) | copy-start | bytes 23592964
  0.0 16.8 %slice-start = ((s8[8388608]{0:T(1024)(128)(4,1)}), s8[4194304]{0:T(1024)(128)(4,1)S(1)}, s32[]{:S(2)}) async-start(s8[8388608]{0:T(1024)(128)(4,1)} %bitcast.2), calls=%async_computation.1 | async-start | bytes 8388608
  3.4 9.2 %copy-start.2 = (bf16[4,128,128]{2,1,0:T(8,128)(2,1)S(1)}, bf16[4,128,128]{2,1,0:T(8,128)(2,1)}, u32[]{:S(2)}) copy-start(bf16[4,128,128]{2,1,0:T(8,128)(2,1)} %blocks.1) | copy-start | bytes 393220
  3.4 6.5 %collective-permute-start = (f32[14,8,128]{2,1,0:T(8,128)S(1)}, f32[14,8,128]{2,1,0:T(8,128)S(1)}, u32[]{:S(2)}, u32[]{:S(2)}) collective-permute-start(f32[14,8,128]{2,1,0:T(8,128)S(1)} %get-tuple-element.15.p0.order), channel_id=1, source_target_pairs={{0,2},{1,3},{2,0},{3,1},{4,6},{5,7},{6,4},{7,5},{8,10},{9,11},{10,... | collective-permute-start | bytes 172040 | tf_op jit(solution)/shard_map/ppermute | solution.py:374
  6.6 4.2 %collective-permute-start.1 = (f32[14,8,128]{2,1,0:T(8,128)S(1)}, f32[14,8,128]{2,1,0:T(8,128)S(1)}, u32[]{:S(2)}, u32[]{:S(2)}) collective-permute-start(f32[14,8,128]{2,1,0:T(8,128)S(1)} %get-tuple-element.15.p0.order), channel_id=1, source_target_pairs={{0,1},{1,0},{2,3},{3,2},{4,5},{5,4},{6,7},{7,6},{8,9},{9,8},{10,11... | collective-permute-start | bytes 172040 | tf_op jit(solution)/shard_map/ppermute | solution.py:374
  7.2 5.4 %collective-permute-start.2 = (f32[14,8,128]{2,1,0:T(8,128)S(1)}, f32[14,8,128]{2,1,0:T(8,128)S(1)}, u32[]{:S(2)}, u32[]{:S(2)}) collective-permute-start(f32[14,8,128]{2,1,0:T(8,128)S(1)} %get-tuple-element.15.p0.order), channel_id=1, source_target_pairs={{0,3},{1,2},{2,1},{3,0},{4,7},{5,6},{6,5},{7,4},{8,11},{9,10},{10,... | collective-permute-start | bytes 172040 | tf_op jit(solution)/shard_map/ppermute | solution.py:374
  7.7 9.1 %slice-start.1 = ((s8[8388608]{0:T(1024)(128)(4,1)}), s8[4194304]{0:T(1024)(128)(4,1)S(1)}, s32[]{:S(2)}) async-start(s8[8388608]{0:T(1024)(128)(4,1)} %bitcast.2), calls=%async_computation.2 | async-start | bytes 8388608
  7.8 9.1 %copy-start.3 = (bf16[32,8,128]{2,1,0:T(8,128)(2,1)S(1)}, bf16[32,8,128]{2,1,0:T(8,128)(2,1)}, u32[]{:S(2)}) copy-start(bf16[32,8,128]{2,1,0:T(8,128)(2,1)} %src_ref.1) | copy-start | bytes 196612
  7.8 9.1 %copy-start.4 = (s32[32,8]{0,1:T(8,128)S(1)}, s32[32,8]{0,1:T(8,128)}, u32[]{:S(2)}) copy-start(s32[32,8]{0,1:T(8,128)} %param.21) | copy-start | bytes 3076
  12.7 7.3 %collective-permute-start.3 = (f32[4,8,128]{2,1,0:T(8,128)S(1)}, f32[4,8,128]{2,1,0:T(8,128)S(1)}, u32[]{:S(2)}, u32[]{:S(2)}) collective-permute-start(f32[4,8,128]{2,1,0:T(8,128)S(1)} %group.1.order.g0), channel_id=1, source_target_pairs={{0,2},{1,3},{2,0},{3,1},{4,6},{5,7},{6,4},{7,5},{8,10},{9,11},{10,... | collective-permute-start | bytes 49160 | tf_op jit(solution)/shard_map/ppermute | solution.py:374
  13.5 6.5 %collective-permute-start.4 = (f32[4,8,128]{2,1,0:T(8,128)S(1)}, f32[4,8,128]{2,1,0:T(8,128)S(1)}, u32[]{:S(2)}, u32[]{:S(2)}) collective-permute-start(f32[4,8,128]{2,1,0:T(8,128)S(1)} %group.1.order.g0), channel_id=1, source_target_pairs={{0,1},{1,0},{2,3},{3,2},{4,5},{5,4},{6,7},{7,6},{8,9},{9,8},{10,11... | collective-permute-start | bytes 49160 | tf_op jit(solution)/shard_map/ppermute | solution.py:374
  14.2 5.8 %collective-permute-start.5 = (f32[4,8,128]{2,1,0:T(8,128)S(1)}, f32[4,8,128]{2,1,0:T(8,128)S(1)}, u32[]{:S(2)}, u32[]{:S(2)}) collective-permute-start(f32[4,8,128]{2,1,0:T(8,128)S(1)} %group.1.order.g0), channel_id=1, source_target_pairs={{0,3},{1,2},{2,1},{3,0},{4,7},{5,6},{6,5},{7,4},{8,11},{9,10},{10,... | collective-permute-start | bytes 49160 | tf_op jit(solution)/shard_map/ppermute | solution.py:374
  16.8 25.8 %copy-start = (bf16[63,128,128]{2,1,0:T(8,128)(2,1)S(1)}, bf16[63,128,128]{2,1,0:T(8,128)(2,1)}, u32[]{:S(2)}) copy-start(bf16[63,128,128]{2,1,0:T(8,128)(2,1)} %down.1) | copy-start | bytes 6193156
  21.3 7.9 %collective-permute-start.6 = (f32[64,8,128]{2,1,0:T(8,128)S(1)}, f32[64,8,128]{2,1,0:T(8,128)S(1)}, u32[]{:S(2)}, u32[]{:S(2)}) collective-permute-start(f32[64,8,128]{2,1,0:T(8,128)S(1)} %get-tuple-element.22), channel_id=1, source_target_pairs={{0,4},{4,0},{8,12},{12,8},{16,20},{20,16},{24,28},{28,24},{32,36},... | collective-permute-start | bytes 786440 | tf_op jit(solution)/shard_map/ppermute | solution.py:374
  21.4 15.4 %collective-permute-start.7 = (f32[92,8,128]{2,1,0:T(8,128)}, f32[92,8,128]{2,1,0:T(8,128)S(1)}, u32[]{:S(2)}, u32[]{:S(2)}) collective-permute-start(f32[92,8,128]{2,1,0:T(8,128)} %get-tuple-element.23), channel_id=1, source_target_pairs={{0,1},{1,2},{2,3},{3,4},{4,5},{5,6},{6,7},{7,8},{8,9},{9,10},{10,1... | collective-permute-start | bytes 1130504 | tf_op jit(solution)/shard_map/ppermute | solution.py:374
  21.7 15.1 %collective-permute-start.8 = (f32[92,8,128]{2,1,0:T(8,128)}, f32[92,8,128]{2,1,0:T(8,128)S(1)}, u32[]{:S(2)}, u32[]{:S(2)}) collective-permute-start(f32[92,8,128]{2,1,0:T(8,128)} %get-tuple-element.24), channel_id=1, source_target_pairs={{0,127},{1,0},{2,1},{3,2},{4,3},{5,4},{6,5},{7,6},{8,7},{9,8},{10,... | collective-permute-start | bytes 1130504 | tf_op jit(solution)/shard_map/ppermute | solution.py:374
  29.9 12.7 %all-to-all-start = ((f32[16,4,8,128]{3,2,1,0:T(8,128)}), f32[16,4,8,128]{3,2,1,0:T(8,128)S(1)}, u32[]{:S(2)}, u32[]{:S(2)}) async-start(f32[16,4,8,128]{3,2,1,0:T(8,128)} %core.1), calls=%async_computation | async-start | bytes 524288 | tf_op jit(solution)/shard_map/all_to_all | solution.py:418

commit v7 on v6

--- a/solution.py
+++ b/solution.py
@@ -180,8 +180,7 @@
 
 
 def near_kernel(
-    src_ref, list_hbm, near, far_prev, far_own, far_next, order,
-    prev_ref, own_ref, next_ref, near_list, a0, a1, a2, a3, sem,
+    src_ref, list_hbm, near, far_prev, order, prev_ref, own_ref, next_ref, near_list, a0, a1, a2, a3, sem,
 ):
     leaves = src_ref.shape[0]
     slots = near_list.shape[0]
@@ -190,8 +189,7 @@
     accs = (a0, a1, a2, a3)
     for acc in accs:
         acc[...] = jnp.zeros(acc.shape, F32)
-    for out, part in ((prev_ref, far_prev), (own_ref, far_own), (next_ref, far_next)):
-        out[leaves:] = part[...]
+    prev_ref[leaves:] = far_prev[...]
     first.wait()
     scatter_steps(
         lambda t: src_ref[t].astype(F32), near, lambda t, k: near_list[k, t], accs,
@@ -230,7 +228,7 @@
         out_ref[k + 1] = out[:, m:]
 
 
-def pack_kernel(p0, p1, p2, p3, g0, g1, g2, g3, order, keep_ref, send_ref, ids, a0, a1, a2, a3, sem):
+def pack_kernel(p0, p1, p2, p3, g0, g1, g2, g3, order, arrived, keep_ref, send_ref, ids, a0, a1, a2, a3, sem):
     half = keep_ref.shape[0]
     parts = (p0, p1, p2, p3)
     accs = (a0, a1, a2, a3)
@@ -273,11 +271,13 @@
     send_ref[...] = total((1 - own_core) * half)
 
 
-def core_kernel(keep_ref, core_ref, out_ref):
+def core_kernel(keep_ref, core_ref, near_next, out_ref, held):
     out_ref[...] = (keep_ref[...] + core_ref[...]).reshape(out_ref.shape)
 
 
-def down_kernel(top, own, from_prev, from_next, down, col_hbm, out_ref, col, level_down, sem):
+def down_kernel(
+    top, far_own, far_from_prev, near_own, near_from_prev, from_next, down, col_hbm, out_ref, col, level_down, sem,
+):
     leaves = out_ref.shape[0]
     levels = leaves.bit_length() - 1
     quarter = leaves // 4
@@ -285,8 +285,8 @@
     fetch = Fetches(sem)
     col_copies = [fetch.rows(col_hbm, col, i * quarter, quarter) for i in range(4)]
 
-    def total(i):
-        return (own[i] + from_prev[i]) + from_next[i]
+    def far_total(i):
+        return (far_own[i] + far_from_prev[i]) + from_next[leaves + i]
 
     fields = top[0]
     for i in range(1, top.shape[0]):
@@ -306,14 +306,14 @@
             out = dot(left, square(down[a], down[a + 1], down[a + 2], down[a + 3]))
             outs = (out[:n, :m], out[:n, m:], out[n:, :m], out[n:, m:])
             for i in range(4):
-                level_down[a + i] = rounded(total(leaves + a + i) + outs[i])
+                level_down[a + i] = rounded(far_total(a + i) + outs[i])
     for t in range(0, leaves, 4):
         if t % quarter == 0:
             col_copies[t // quarter].wait()
         span = range(t, t + 4)
         outs = quad([level_down[i] for i in span], [col[i] for i in span])
         for i, out in zip(span, outs):
-            out_ref[i] = total(i) + out
+            out_ref[i] = ((near_own[i] + near_from_prev[i]) + from_next[i]) + out
 
 
 PARAMS = pltpu.CompilerParams(vmem_limit_bytes=24 * 1024 * 1024)
@@ -374,7 +374,7 @@
         return lax.ppermute(x, axis, [(i, target(i)) for i in range(count)])
 
     def gathered(x):
-        return [x] + [permuted(x, "sub", lambda i, s=s: i ^ s) for s in (2, 1, 3)]
+        return [x] + [permuted(x, "sub", lambda i, s=s: i ^ s) for s in (3, 1, 2)]
 
     coef, top = call(
         up_kernel, "upward", 4, (shape(nodes), shape(PAYLOAD)),
@@ -398,28 +398,36 @@
         group_kernel, "group", 1, shape(GROUP_TERMS), (*top_parts, group_blocks), [VMEM] * 5, []
     )
     term_parts = gathered(terms)
-    to_prev, own, to_next = call(
-        near_kernel, "near", 4, (shape(leaves + far_nodes),) * 3,
-        (sources, near_list, near_blocks, far_prev, far_own, far_next, terms),
-        [VMEM, ANY, VMEM, VMEM, VMEM, VMEM, ANY],
+    to_prev, near_own, near_next = call(
+        near_kernel, "near", 4, (shape(leaves + far_nodes), shape(leaves), shape(leaves)),
+        (sources, near_list, near_blocks, far_prev, terms), [VMEM, ANY, VMEM, VMEM, ANY],
         [pltpu.SMEM((near_slots, leaves), jnp.int32)] + accumulators(leaves) + [copies(1)],
     )
     half = groups // 2 * 4
     everyone = ("leaf", "sub")
-    from_prev = permuted(to_next, everyone, lambda i: (i + 1) % devices)
-    from_next = permuted(to_prev, everyone, lambda i: (i - 1) % devices)
-
+    def ahead(x):
+        return permuted(x, everyone, lambda i: (i + 1) % devices)
+
+    def back(x):
+        return permuted(x, everyone, lambda i: (i - 1) % devices)
+
+    far_from_prev, from_next = ahead(far_next), back(to_prev)
     keep, send = call(
-        pack_kernel, "pack", 0, (shape(half), shape(half)), (*top_parts, *term_parts, own), [VMEM] * 8 + [ANY],
+        pack_kernel, "pack", 10, (shape(half), shape(half)), (*top_parts, *term_parts, near_own, far_from_prev), [VMEM] * 8 + [ANY] * 2,
         [pltpu.SMEM((subs,) + row, F32)] + [plane(2 * half + 1)] * 4 + [copies(subs)],
     )
     from_core = permuted(send, "leaf", lambda i: i ^ 1)
-    planes = call(core_kernel, "core", 0, shape(groups // 2, 4), (keep, from_core), [VMEM] * 2, [])
+    planes, near_next = call(
+        core_kernel, "core", 10, (shape(groups // 2, 4), shape(leaves)), (keep, from_core, near_next),
+        [VMEM] * 2 + [ANY], [], out_specs=(VMEM, ANY), input_output_aliases={2: 1},
+    )
+    near_from_prev = ahead(near_next)
     fields = lax.all_to_all(
         planes, "leaf", 0, 0, tiled=True, axis_index_groups=[list(range(c, groups, 2)) for c in range(2)]
     )
     return call(
-        down_kernel, "downward", 0, shape(leaves), (fields, own, from_prev, from_next, down_transfer, col_basis), [VMEM] * 5 + [ANY],
+        down_kernel, "downward", 0, shape(leaves), (fields, far_own, far_from_prev, near_own, near_from_prev, from_next, down_transfer, col_basis),
+        [VMEM] * 7 + [ANY],
         [buffer(leaves), plane(nodes), copies(4)],
     )
 

time: 45.3 us -> 47 us (1.038)
  waiting for transfers between devices: 11.1 us -> 13.3 us
  starting transfers between devices: 20.5 us -> 19.5 us
  local copies, waits for them, and re-layouts: 0.04 us -> 0.69 us
    ppermute x9 -> x10, waiting for transfers between devices: 5.33 us -> 13.3 us  [permuted(): return lax.ppermute(x, axis, [(i, target(i)) for i in range(count)])]
    all_to_all x1, waiting for transfers between devices: 5.82 us -> 0.01 us  [shards(): lax.all_to_all(planes, 'leaf', 0, 0, tiled=True, axis_index_groups=[list(...]
    all_to_all x1, starting transfers between devices: 4.23 us -> 3.53 us  [shards(): lax.all_to_all(planes, 'leaf', 0, 0, tiled=True, axis_index_groups=[list(...]
    unnamed x16 -> x18, local copies, waits for them, and re-layouts: 0.04 us -> 0.69 us
    ppermute x9 -> x10, starting transfers between devices: 16.3 us -> 15.9 us  [permuted(): return lax.ppermute(x, axis, [(i, target(i)) for i in range(count)])]
  transfers between devices with their start and end apart: 10 -> 11, of which waited for: 4 -> 4; matrix products, arithmetic and copies ran while one was open for 0% -> 0% of each run, Pallas kernels for 13% -> 13%
where the time goes in v7:
time: 47 us; the launch traced here: 46.8 us
  starting transfers between devices  19.5 us (41%)
  waiting for transfers between devices  13.3 us (28%)
  Pallas kernels  13.1 us (28%)
  local copies, waits for them, and re-layouts  0.69 us (1%)
    ppermute x10, starting transfers between devices, permuted(): return lax.ppermute(x, axis, [(i, target(i)) for i in range(count)])  15.9 us
    ppermute x10, waiting for transfers between devices, permuted(): return lax.ppermute(x, axis, [(i, target(i)) for i in range(count)])  13.3 us
    pallas_call x7, Pallas kernels, call(): pl.pallas_call(kernel, out_shape=outs, in_specs=specs, out_specs=out_spec...  13.1 us
    all_to_all x1, starting transfers between devices, shards(): lax.all_to_all(planes, 'leaf', 0, 0, tiled=True, axis_index_groups=[list(...  3.53 us
  transfers between devices with their start and end apart: 11, of which 4 were waited for; matrix products, arithmetic and copies ran while one was open for 0% of the time, Pallas kernels for 13%

profile of v7, /device:TPU:0, one launch (start us, length us, event | category | flops | bytes accessed | tf_op | source)
XLA Modules:
  0.0 46.8 jit_solution(4773456762172749659)
XLA Ops:
  0.0 0.0 copy-start.6
  0.0 0.0 copy-start.1
  0.0 0.0 slice-start
  0.0 3.4 %upward.1 = (f32[63,8,128]{2,1,0:T(8,128)S(1)}, f32[14,8,128]{2,1,0:T(8,128)S(1)}) custom-call(bf16[32,8,128]{2,1,0:T(8,128)(2,1)} %src_ref.1, s32[2,4]{1,0:T(2,128)} %upper_list_hbm.1, s32[1,4]{1,0:T(1,128)} %root_list_hbm.1, s32[1,4]{1,0:T(1,128)} %group_list_hbm.1, bf16[32,128,128]{2,1,0:T(8,128)(2,1)} %rb_hbm.1, bf16[63,128,128]{2,1,0:T(8,128)(2,1)} %up_hbm.1, ...), custom_call_target="tpu_custom_call" | custom-call | flops 4000000000 | tf_op jit(solution)/shard_map/upward/pallas_call | solution.py:358
  3.4 0.0 copy-start.2
  3.4 3.2 %collective-permute-start.2 = (f32[14,8,128]{2,1,0:T(8,128)S(1)}, f32[14,8,128]{2,1,0:T(8,128)S(1)}, u32[]{:S(2)}, u32[]{:S(2)}) collective-permute-start(f32[14,8,128]{2,1,0:T(8,128)S(1)} %get-tuple-element.17.p0.order), channel_id=1, source_target_pairs={{0,2},{1,3},{2,0},{3,1},{4,6},{5,7},{6,4},{7,5},{8,10},{9,11},{10,... | collective-permute-start | bytes 172040 | tf_op jit(solution)/shard_map/ppermute | solution.py:374
  6.6 0.6 %collective-permute-start.1 = (f32[14,8,128]{2,1,0:T(8,128)S(1)}, f32[14,8,128]{2,1,0:T(8,128)S(1)}, u32[]{:S(2)}, u32[]{:S(2)}) collective-permute-start(f32[14,8,128]{2,1,0:T(8,128)S(1)} %get-tuple-element.17.p0.order), channel_id=1, source_target_pairs={{0,1},{1,0},{2,3},{3,2},{4,5},{5,4},{6,7},{7,6},{8,9},{9,8},{10,11... | collective-permute-start | bytes 172040 | tf_op jit(solution)/shard_map/ppermute | solution.py:374
  7.2 0.6 %collective-permute-start = (f32[14,8,128]{2,1,0:T(8,128)S(1)}, f32[14,8,128]{2,1,0:T(8,128)S(1)}, u32[]{:S(2)}, u32[]{:S(2)}) collective-permute-start(f32[14,8,128]{2,1,0:T(8,128)S(1)} %get-tuple-element.17.p0.order), channel_id=1, source_target_pairs={{0,3},{1,2},{2,1},{3,0},{4,7},{5,6},{6,5},{7,4},{8,11},{9,10},{10,... | collective-permute-start | bytes 172040 | tf_op jit(solution)/shard_map/ppermute | solution.py:374
  7.7 0.0 copy-done.6
  7.7 0.0 copy-done.1
  7.7 0.0 slice-start.1
  7.8 0.0 copy-start.4
  7.8 0.0 copy-start.5
  7.8 2.2 %far.2 = (f32[60,8,128]{2,1,0:T(8,128)S(1)}, f32[60,8,128]{2,1,0:T(8,128)S(1)}, f32[60,8,128]{2,1,0:T(8,128)S(1)}) custom-call(f32[63,8,128]{2,1,0:T(8,128)S(1)} %get-tuple-element.18.coef_ref, s32[4,60]{1,0:T(4,128)S(1)} %bitcast.5, bf16[240,128,128]{2,1,0:T(8,128)(2,1)S(1)} %copy-done.1, f32[14,8,128]{2,1,0:T(8,128)S(1)} %get-tuple-element.17.p0.order), custom_call_target="tpu_custom_call" | custom-call | flops 4000000000 | tf_op jit(solution)/shard_map/far/pallas_call | solution.py:358
  9.9 1.5 %collective-permute-start.6 = (f32[60,8,128]{2,1,0:T(8,128)S(1)}, f32[60,8,128]{2,1,0:T(8,128)S(1)}, u32[]{:S(2)}, u32[]{:S(2)}) collective-permute-start(f32[60,8,128]{2,1,0:T(8,128)S(1)} %get-tuple-element.21), channel_id=1, source_target_pairs={{0,1},{1,2},{2,3},{3,4},{4,5},{5,6},{6,7},{7,8},{8,9},{9,10},{10,1... | collective-permute-start | bytes 737288 | tf_op jit(solution)/shard_map/ppermute | solution.py:374
  11.4 0.0 collective-permute-done.2.p3
  11.4 0.0 collective-permute-done.1.p2
  11.4 1.1 %collective-permute-done.p1 = f32[14,8,128]{2,1,0:T(8,128)S(1)} collective-permute-done((f32[14,8,128]{2,1,0:T(8,128)S(1)}, f32[14,8,128]{2,1,0:T(8,128)S(1)}, u32[]{:S(2)}, u32[]{:S(2)}) %collective-permute-start) | collective-permute-done | bytes 57376 | tf_op jit(solution)/shard_map/ppermute | solution.py:374
  12.6 0.0 copy-done.2
  12.6 0.1 group.1.order.g0
  12.7 1.6 %collective-permute-start.5 = (f32[4,8,128]{2,1,0:T(8,128)S(1)}, f32[4,8,128]{2,1,0:T(8,128)S(1)}, u32[]{:S(2)}, u32[]{:S(2)}) collective-permute-start(f32[4,8,128]{2,1,0:T(8,128)S(1)} %group.1.order.g0), channel_id=1, source_target_pairs={{0,2},{1,3},{2,0},{3,1},{4,6},{5,7},{6,4},{7,5},{8,10},{9,11},{10,... | collective-permute-start | bytes 49160 | tf_op jit(solution)/shard_map/ppermute | solution.py:374
  14.3 0.0 collective-permute-start.4
  14.3 2.5 %collective-permute-start.3 = (f32[4,8,128]{2,1,0:T(8,128)S(1)}, f32[4,8,128]{2,1,0:T(8,128)S(1)}, u32[]{:S(2)}, u32[]{:S(2)}) collective-permute-start(f32[4,8,128]{2,1,0:T(8,128)S(1)} %group.1.order.g0), channel_id=1, source_target_pairs={{0,3},{1,2},{2,1},{3,0},{4,7},{5,6},{6,5},{7,4},{8,11},{9,10},{10,... | collective-permute-start | bytes 49160 | tf_op jit(solution)/shard_map/ppermute | solution.py:374
  16.8 0.0 slice-done
  16.8 0.0 slice-done.1
  16.8 0.0 copy-done.4
  16.8 0.0 copy-done.5
  16.8 3.0 %near.2 = (f32[92,8,128]{2,1,0:T(8,128)}, f32[32,8,128]{2,1,0:T(8,128)S(1)}, f32[32,8,128]{2,1,0:T(8,128)S(1)}) custom-call(bf16[32,8,128]{2,1,0:T(8,128)(2,1)S(1)} %copy-done.4, s32[8,32]{1,0:T(8,128)S(1)} %bitcast.4, bf16[256,128,128]{2,1,0:T(8,128)(2,1)S(1)} %bitcast.3, f32[60,8,128]{2,1,0:T(8,128)S(1)} %get-tuple-element.19.far_prev, ...), custom_call_target="tpu_custom_call" | custom-call | flops 4000000000 | tf_op jit(solution)/shard_map/near/pallas_call | solution.py:358
  19.9 0.0 collective-permute-done.5.g3
  19.9 0.0 collective-permute-done.4.g2
  19.9 0.0 collective-permute-done.3.g1
  19.9 2.1 %collective-permute-done.6.arrived.far_from_prev = f32[60,8,128]{2,1,0:T(8,128)S(1)} collective-permute-done((f32[60,8,128]{2,1,0:T(8,128)S(1)}, f32[60,8,128]{2,1,0:T(8,128)S(1)}, u32[]{:S(2)}, u32[]{:S(2)}) %collective-permute-start.6) | collective-permute-done | bytes 245792 | tf_op jit(solution)/shard_map/ppermute | solution.py:374
  22.0 1.3 %pack.1 = (f32[64,8,128]{2,1,0:T(8,128)S(1)}, f32[64,8,128]{2,1,0:T(8,128)S(1)}) custom-call(f32[14,8,128]{2,1,0:T(8,128)S(1)} %get-tuple-element.17.p0.order, f32[14,8,128]{2,1,0:T(8,128)S(1)} %collective-permute-done.p1, f32[14,8,128]{2,1,0:T(8,128)S(1)} %collective-permute-done.1.p2, f32[14,8,128]{2,1,0:T(8,128)S(1)} %collective-permute-done.2.p3, ...), custom_call_target="tpu_custom_call" | custom-call | flops 10000000000 | tf_op jit(solution)/shard_map/pack/pallas_call | solution.py:358
  23.3 0.1 collective-permute-start.7
  23.4 5.8 %collective-permute-start.9 = (f32[92,8,128]{2,1,0:T(8,128)}, f32[92,8,128]{2,1,0:T(8,128)S(1)}, u32[]{:S(2)}, u32[]{:S(2)}) collective-permute-start(f32[92,8,128]{2,1,0:T(8,128)} %get-tuple-element.28), channel_id=1, source_target_pairs={{0,127},{1,0},{2,1},{3,2},{4,3},{5,4},{6,5},{7,6},{8,7},{9,8},{10,... | collective-permute-start | bytes 1130504 | tf_op jit(solution)/shard_map/ppermute | solution.py:374
  29.3 0.0 collective-permute-done.7.core_ref
  29.3 0.0 copy-start
  29.3 0.7 %core.1 = (f32[16,4,8,128]{3,2,1,0:T(8,128)}, f32[32,8,128]{2,1,0:T(8,128)S(1)}) custom-call(f32[64,8,128]{2,1,0:T(8,128)S(1)} %get-tuple-element.22.keep_ref, f32[64,8,128]{2,1,0:T(8,128)S(1)} %collective-permute-done.7.core_ref, f32[32,8,128]{2,1,0:T(8,128)S(1)} %get-tuple-element.24.near_next), custom_call_target="tpu_custom_call", output_to_operand_aliasing={{1}: (2, {})} | custom-call | flops 10000000000 | tf_op jit(solution)/shard_map/core/pallas_call | solution.py:358
  30.0 0.0 copy-start.3
  30.0 0.7 %copy-done.3 = f32[32,8,128]{2,1,0:T(8,128)} copy-done((f32[32,8,128]{2,1,0:T(8,128)}, f32[32,8,128]{2,1,0:T(8,128)S(1)}, u32[]{:S(2)}) %copy-start.3) | copy-done | bytes 131096
  30.7 3.5 %all-to-all-start = ((f32[16,4,8,128]{3,2,1,0:T(8,128)}), f32[16,4,8,128]{3,2,1,0:T(8,128)S(1)}, u32[]{:S(2)}, u32[]{:S(2)}) async-start(f32[16,4,8,128]{3,2,1,0:T(8,128)} %get-tuple-element.25), calls=%async_computation | async-start | bytes 524288 | tf_op jit(solution)/shard_map/all_to_all | solution.py:425
  34.2 0.1 collective-permute-start.8
  34.3 0.5 %collective-permute-done.9.from_next = f32[92,8,128]{2,1,0:T(8,128)S(1)} collective-permute-done((f32[92,8,128]{2,1,0:T(8,128)}, f32[92,8,128]{2,1,0:T(8,128)S(1)}, u32[]{:S(2)}, u32[]{:S(2)}) %collective-permute-start.9) | collective-permute-done | bytes 376864 | tf_op jit(solution)/shard_map/ppermute | solution.py:374
  34.8 9.5 %collective-permute-done.8.near_from_prev = f32[32,8,128]{2,1,0:T(8,128)S(1)} collective-permute-done((f32[32,8,128]{2,1,0:T(8,128)}, f32[32,8,128]{2,1,0:T(8,128)S(1)}, u32[]{:S(2)}, u32[]{:S(2)}) %collective-permute-start.8) | collective-permute-done | bytes 131104 | tf_op jit(solution)/shard_map/ppermute | solution.py:374
  44.3 0.0 all-to-all-done.top
  44.3 0.0 copy-done
  44.3 2.4 %downward.1 = f32[32,8,128]{2,1,0:T(8,128)} custom-call(f32[16,4,8,128]{3,2,1,0:T(8,128)S(1)} %all-to-all-done.top, f32[60,8,128]{2,1,0:T(8,128)S(1)} %get-tuple-element.26.far_own, f32[60,8,128]{2,1,0:T(8,128)S(1)} %collective-permute-done.6.arrived.far_from_prev, f32[32,8,128]{2,1,0:T(8,128)S(1)} %get-tuple-element.20.order.near_own, ...), custom_call_target="tpu_custom_call" | custom-call | tf_op jit(solution)/shard_map/downward/pallas_call | solution.py:358
  (1 shorter events, 0.0 us)
Async XLA Ops:
  0.0 7.7 %copy-start.6 = (s32[60,4]{0,1:T(4,128)S(1)}, s32[60,4]{0,1:T(4,128)}, u32[]{:S(2)}) copy-start(s32[60,4]{0,1:T(4,128)} %param.23) | copy-start | bytes 2884
  0.0 7.7 %copy-start.1 = (bf16[240,128,128]{2,1,0:T(8,128)(2,1)S(1)}, bf16[240,128,128]{2,1,0:T(8,128)(2,1)}, u32[]{:S(2)}) copy-start(bf16[240,128,128]{2,1,0:T(8,128)(2,1)} %far.3) | copy-start | bytes 23592964
  0.0 16.8 %slice-start = ((s8[8388608]{0:T(1024)(128)(4,1)}), s8[4194304]{0:T(1024)(128)(4,1)S(1)}, s32[]{:S(2)}) async-start(s8[8388608]{0:T(1024)(128)(4,1)} %bitcast.2), calls=%async_computation.1 | async-start | bytes 8388608
  3.4 9.2 %copy-start.2 = (bf16[4,128,128]{2,1,0:T(8,128)(2,1)S(1)}, bf16[4,128,128]{2,1,0:T(8,128)(2,1)}, u32[]{:S(2)}) copy-start(bf16[4,128,128]{2,1,0:T(8,128)(2,1)} %blocks.1) | copy-start | bytes 393220
  3.4 8.0 %collective-permute-start.2 = (f32[14,8,128]{2,1,0:T(8,128)S(1)}, f32[14,8,128]{2,1,0:T(8,128)S(1)}, u32[]{:S(2)}, u32[]{:S(2)}) collective-permute-start(f32[14,8,128]{2,1,0:T(8,128)S(1)} %get-tuple-element.17.p0.order), channel_id=1, source_target_pairs={{0,2},{1,3},{2,0},{3,1},{4,6},{5,7},{6,4},{7,5},{8,10},{9,11},{10,... | collective-permute-start | bytes 172040 | tf_op jit(solution)/shard_map/ppermute | solution.py:374
  6.6 4.8 %collective-permute-start.1 = (f32[14,8,128]{2,1,0:T(8,128)S(1)}, f32[14,8,128]{2,1,0:T(8,128)S(1)}, u32[]{:S(2)}, u32[]{:S(2)}) collective-permute-start(f32[14,8,128]{2,1,0:T(8,128)S(1)} %get-tuple-element.17.p0.order), channel_id=1, source_target_pairs={{0,1},{1,0},{2,3},{3,2},{4,5},{5,4},{6,7},{7,6},{8,9},{9,8},{10,11... | collective-permute-start | bytes 172040 | tf_op jit(solution)/shard_map/ppermute | solution.py:374
  7.2 5.4 %collective-permute-start = (f32[14,8,128]{2,1,0:T(8,128)S(1)}, f32[14,8,128]{2,1,0:T(8,128)S(1)}, u32[]{:S(2)}, u32[]{:S(2)}) collective-permute-start(f32[14,8,128]{2,1,0:T(8,128)S(1)} %get-tuple-element.17.p0.order), channel_id=1, source_target_pairs={{0,3},{1,2},{2,1},{3,0},{4,7},{5,6},{6,5},{7,4},{8,11},{9,10},{10,... | collective-permute-start | bytes 172040 | tf_op jit(solution)/shard_map/ppermute | solution.py:374
  7.7 9.1 %slice-start.1 = ((s8[8388608]{0:T(1024)(128)(4,1)}), s8[4194304]{0:T(1024)(128)(4,1)S(1)}, s32[]{:S(2)}) async-start(s8[8388608]{0:T(1024)(128)(4,1)} %bitcast.2), calls=%async_computation.2 | async-start | bytes 8388608
  7.8 9.1 %copy-start.4 = (bf16[32,8,128]{2,1,0:T(8,128)(2,1)S(1)}, bf16[32,8,128]{2,1,0:T(8,128)(2,1)}, u32[]{:S(2)}) copy-start(bf16[32,8,128]{2,1,0:T(8,128)(2,1)} %src_ref.1) | copy-start | bytes 196612
  7.8 9.1 %copy-start.5 = (s32[32,8]{0,1:T(8,128)S(1)}, s32[32,8]{0,1:T(8,128)}, u32[]{:S(2)}) copy-start(s32[32,8]{0,1:T(8,128)} %param.21) | copy-start | bytes 3076
  9.9 12.1 %collective-permute-start.6 = (f32[60,8,128]{2,1,0:T(8,128)S(1)}, f32[60,8,128]{2,1,0:T(8,128)S(1)}, u32[]{:S(2)}, u32[]{:S(2)}) collective-permute-start(f32[60,8,128]{2,1,0:T(8,128)S(1)} %get-tuple-element.21), channel_id=1, source_target_pairs={{0,1},{1,2},{2,3},{3,4},{4,5},{5,6},{6,7},{7,8},{8,9},{9,10},{10,1... | collective-permute-start | bytes 737288 | tf_op jit(solution)/shard_map/ppermute | solution.py:374
  12.7 7.1 %collective-permute-start.5 = (f32[4,8,128]{2,1,0:T(8,128)S(1)}, f32[4,8,128]{2,1,0:T(8,128)S(1)}, u32[]{:S(2)}, u32[]{:S(2)}) collective-permute-start(f32[4,8,128]{2,1,0:T(8,128)S(1)} %group.1.order.g0), channel_id=1, source_target_pairs={{0,2},{1,3},{2,0},{3,1},{4,6},{5,7},{6,4},{7,5},{8,10},{9,11},{10,... | collective-permute-start | bytes 49160 | tf_op jit(solution)/shard_map/ppermute | solution.py:374
  14.3 5.5 %collective-permute-start.4 = (f32[4,8,128]{2,1,0:T(8,128)S(1)}, f32[4,8,128]{2,1,0:T(8,128)S(1)}, u32[]{:S(2)}, u32[]{:S(2)}) collective-permute-start(f32[4,8,128]{2,1,0:T(8,128)S(1)} %group.1.order.g0), channel_id=1, source_target_pairs={{0,1},{1,0},{2,3},{3,2},{4,5},{5,4},{6,7},{7,6},{8,9},{9,8},{10,11... | collective-permute-start | bytes 49160 | tf_op jit(solution)/shard_map/ppermute | solution.py:374
  14.3 5.5 %collective-permute-start.3 = (f32[4,8,128]{2,1,0:T(8,128)S(1)}, f32[4,8,128]{2,1,0:T(8,128)S(1)}, u32[]{:S(2)}, u32[]{:S(2)}) collective-permute-start(f32[4,8,128]{2,1,0:T(8,128)S(1)} %group.1.order.g0), channel_id=1, source_target_pairs={{0,3},{1,2},{2,1},{3,0},{4,7},{5,6},{6,5},{7,4},{8,11},{9,10},{10,... | collective-permute-start | bytes 49160 | tf_op jit(solution)/shard_map/ppermute | solution.py:374
  23.3 5.9 %collective-permute-start.7 = (f32[64,8,128]{2,1,0:T(8,128)S(1)}, f32[64,8,128]{2,1,0:T(8,128)S(1)}, u32[]{:S(2)}, u32[]{:S(2)}) collective-permute-start(f32[64,8,128]{2,1,0:T(8,128)S(1)} %get-tuple-element.23), channel_id=1, source_target_pairs={{0,4},{4,0},{8,12},{12,8},{16,20},{20,16},{24,28},{28,24},{32,36},... | collective-permute-start | bytes 786440 | tf_op jit(solution)/shard_map/ppermute | solution.py:374
  23.4 11.4 %collective-permute-start.9 = (f32[92,8,128]{2,1,0:T(8,128)}, f32[92,8,128]{2,1,0:T(8,128)S(1)}, u32[]{:S(2)}, u32[]{:S(2)}) collective-permute-start(f32[92,8,128]{2,1,0:T(8,128)} %get-tuple-element.28), channel_id=1, source_target_pairs={{0,127},{1,0},{2,1},{3,2},{4,3},{5,4},{6,5},{7,6},{8,7},{9,8},{10,... | collective-permute-start | bytes 1130504 | tf_op jit(solution)/shard_map/ppermute | solution.py:374
  29.3 15.1 %copy-start = (bf16[63,128,128]{2,1,0:T(8,128)(2,1)S(1)}, bf16[63,128,128]{2,1,0:T(8,128)(2,1)}, u32[]{:S(2)}) copy-start(bf16[63,128,128]{2,1,0:T(8,128)(2,1)} %down.1) | copy-start | bytes 6193156
  30.0 0.7 %copy-start.3 = (f32[32,8,128]{2,1,0:T(8,128)}, f32[32,8,128]{2,1,0:T(8,128)S(1)}, u32[]{:S(2)}) copy-start(f32[32,8,128]{2,1,0:T(8,128)S(1)} %get-tuple-element.27) | copy-start | bytes 393220
  30.7 13.7 %all-to-all-start = ((f32[16,4,8,128]{3,2,1,0:T(8,128)}), f32[16,4,8,128]{3,2,1,0:T(8,128)S(1)}, u32[]{:S(2)}, u32[]{:S(2)}) async-start(f32[16,4,8,128]{3,2,1,0:T(8,128)} %get-tuple-element.25), calls=%async_computation | async-start | bytes 524288 | tf_op jit(solution)/shard_map/all_to_all | solution.py:425
  34.2 10.1 %collective-permute-start.8 = (f32[32,8,128]{2,1,0:T(8,128)}, f32[32,8,128]{2,1,0:T(8,128)S(1)}, u32[]{:S(2)}, u32[]{:S(2)}) collective-permute-start(f32[32,8,128]{2,1,0:T(8,128)} %copy-done.3), channel_id=1, source_target_pairs={{0,1},{1,2},{2,3},{3,4},{4,5},{5,6},{6,7},{7,8},{8,9},{9,10},{10,1... | collective-permute-start | bytes 393224 | tf_op jit(solution)/shard_map/ppermute | solution.py:374

commit v8 on v4

--- a/solution.py
+++ b/solution.py
@@ -173,14 +173,15 @@
 
 
 def store_totals(accs, span, refs):
-    for i, ref in enumerate(refs):
-        parts = [acc[pl.ds(i * span, span)] for acc in accs]
+    odd = lax.axis_index("sub") & 1
+    for first, ref in zip((2 - 2 * odd, 1, 2 * odd), refs):
+        parts = [acc[pl.ds(first * span, span)] for acc in accs]
         ref[0:span] = (parts[0] + parts[1]) + (parts[2] + parts[3])
 
 
 def near_kernel(
-    src_ref, list_hbm, near, far_prev, far_own, far_next, order,
-    prev_ref, own_ref, next_ref, near_list, a0, a1, a2, a3, sem,
+    src_ref, list_hbm, near, far_a, far_own, far_b, order,
+    a_ref, own_ref, b_ref, near_list, a0, a1, a2, a3, sem,
 ):
     leaves = src_ref.shape[0]
     slots = near_list.shape[0]
@@ -189,18 +190,18 @@
     accs = (a0, a1, a2, a3)
     for acc in accs:
         acc[...] = jnp.zeros(acc.shape, F32)
-    for out, part in ((prev_ref, far_prev), (own_ref, far_own), (next_ref, far_next)):
+    for out, part in ((a_ref, far_a), (own_ref, far_own), (b_ref, far_b)):
         out[leaves:] = part[...]
     first.wait()
     scatter_steps(
         lambda t: src_ref[t].astype(F32), near, lambda t, k: near_list[k, t], accs,
         slots, 0, leaves, 8, 0, leaves.bit_length() - 1, 0, leaves,
     )
-    store_totals(accs, leaves, (prev_ref, own_ref, next_ref))
+    store_totals(accs, leaves, (a_ref, own_ref, b_ref))
 
 
 def far_kernel(
-    leaves, coef_ref, list_hbm, far, order, prev_ref, own_ref, next_ref, far_list, a0, a1, a2, a3, sem,
+    leaves, coef_ref, list_hbm, far, order, a_ref, own_ref, b_ref, far_list, a0, a1, a2, a3, sem,
 ):
     levels = leaves.bit_length() - 1
     slots, nodes = far_list.shape
@@ -216,7 +217,7 @@
             lambda t: coef_ref[t], far, lambda t, k: far_list[k, t], accs,
             slots, offset, leaves >> level, min(16, leaves >> level), level, levels, offset, nodes,
         )
-    store_totals(accs, nodes, (prev_ref, own_ref, next_ref))
+    store_totals(accs, nodes, (a_ref, own_ref, b_ref))
 
 
 def group_kernel(g0, g1, g2, g3, top_ref, group_list, blocks, out_ref):
@@ -279,7 +280,7 @@
     out_ref[...] = (keep_ref[...] + core_ref[...]).reshape(out_ref.shape)
 
 
-def down_kernel(top, own, from_prev, from_next, down, col_hbm, out_ref, col, level_down, sem):
+def down_kernel(top, own, from_a, from_b, down, col_hbm, out_ref, col, level_down, sem):
     leaves = out_ref.shape[0]
     levels = leaves.bit_length() - 1
     quarter = leaves // 4
@@ -288,7 +289,7 @@
     col_copies = [fetch.rows(col_hbm, col, i * quarter, quarter) for i in range(4)]
 
     def total(i):
-        return (own[i] + from_prev[i]) + from_next[i]
+        return (own[i] + from_a[i]) + from_b[i]
 
     fields = top[0]
     for i in range(1, top.shape[0]):
@@ -388,7 +389,7 @@
         ],
     )
     group_parts = gathered(group)
-    far_prev, far_own, far_next = call(
+    far_a, far_own, far_b = call(
         functools.partial(far_kernel, leaves), "far", 4, (shape(far_nodes),) * 3,
         (coef, far_list, far_blocks, group),
         [VMEM, ANY, VMEM, ANY],
@@ -399,16 +400,16 @@
         [VMEM] * 7, [],
     )
     term_parts = gathered(terms)
-    to_prev, own, to_next = call(
+    to_a, own, to_b = call(
         near_kernel, "near", 4, (shape(leaves + far_nodes),) * 3,
-        (sources, near_list, near_blocks, far_prev, far_own, far_next, terms),
+        (sources, near_list, near_blocks, far_a, far_own, far_b, terms),
         [VMEM, ANY, VMEM, VMEM, VMEM, VMEM, ANY],
         [pltpu.SMEM((near_slots, leaves), jnp.int32)] + accumulators(leaves) + [copies(1)],
     )
     half = groups // 2 * 4
     everyone = ("leaf", "sub")
-    from_prev = permuted(to_next, everyone, lambda i: (i + 1) % devices)
-    from_next = permuted(to_prev, everyone, lambda i: (i - 1) % devices)
+    from_a = permuted(to_a, everyone, lambda i: i ^ 1)
+    from_b = permuted(to_b, everyone, lambda i: (((i + 1) ^ 1) - 1) % devices)
 
     keep, send = call(
         pack_kernel, "pack", 0, (shape(half), shape(half)), (*term_parts, own), [VMEM] * 4 + [ANY],
@@ -417,10 +418,10 @@
     from_core = permuted(send, "leaf", lambda i: i ^ 1)
     planes = call(core_kernel, "core", 0, shape(groups // 2, 4), (keep, from_core), [VMEM] * 2, [])
     fields = lax.all_to_all(
-        planes, "leaf", 0, 0, tiled=True, axis_index_groups=[list(range(c, groups, 2)) for c in range(2)]
+        pltpu.with_memory_space_constraint(planes, pltpu.VMEM), "leaf", 0, 0, tiled=True, axis_index_groups=[list(range(c, groups, 2)) for c in range(2)]
     )
     return call(
-        down_kernel, "downward", 0, shape(leaves), (fields, own, from_prev, from_next, down_transfer, col_basis), [VMEM] * 5 + [ANY],
+        down_kernel, "downward", 0, shape(leaves), (fields, own, from_a, from_b, down_transfer, col_basis), [VMEM] * 5 + [ANY],
         [buffer(leaves), plane(nodes), copies(4)],
     )
 

time: 44.9 us -> 44.5 us (level)
  no operation moved by 1% of the time
where the time goes in v8:
time: 44.5 us; the launch traced here: 44.3 us
  starting transfers between devices  20.1 us (45%)
  Pallas kernels  13.7 us (31%)
  waiting for transfers between devices  10.3 us (23%)
    ppermute x9, starting transfers between devices, permuted(): return lax.ppermute(x, axis, [(i, target(i)) for i in range(count)])  16.6 us
    pallas_call x7, Pallas kernels, call(): pl.pallas_call(kernel, out_shape=outs, in_specs=specs, out_specs=out_spec...  13.7 us
    ppermute x9, waiting for transfers between devices, permuted(): return lax.ppermute(x, axis, [(i, target(i)) for i in range(count)])  5.52 us
    all_to_all x1, waiting for transfers between devices, shards(): lax.all_to_all(pltpu.with_memory_space_constraint(planes, pltpu.VMEM), 'l...  4.73 us
    all_to_all x1, starting transfers between devices, shards(): lax.all_to_all(pltpu.with_memory_space_constraint(planes, pltpu.VMEM), 'l...  3.53 us
  transfers between devices with their start and end apart: 10, of which 3 were waited for; matrix products, arithmetic and copies ran while one was open for 0% of the time, Pallas kernels for 15%

profile of v8, /device:TPU:0, one launch (start us, length us, event | category | flops | bytes accessed | tf_op | source)
XLA Modules:
  0.0 44.3 jit_solution(10339304028984997440)
XLA Ops:
  0.0 0.0 copy-start.1
  0.0 0.0 slice-start
  0.0 3.3 %upward.1 = (f32[63,8,128]{2,1,0:T(8,128)S(1)}, f32[8,128]{1,0:T(8,128)S(1)}, f32[13,8,128]{2,1,0:T(8,128)S(1)}) custom-call(bf16[32,8,128]{2,1,0:T(8,128)(2,1)} %src_ref.1, s32[2,4]{1,0:T(2,128)} %upper_list_hbm.1, s32[1,4]{1,0:T(1,128)} %root_list_hbm.1, bf16[32,128,128]{2,1,0:T(8,128)(2,1)} %rb_hbm.1, bf16[63,128,128]{2,1,0:T(8,128)(2,1)} %up_hbm.1, ...), custom_call_target="tpu_custom_call" | custom-call | flops 4000000000 | tf_op jit(solution)/shard_map/upward/pallas_call | solution.py:360
  3.3 0.0 copy-start.2
  3.3 0.0 copy-start.4
  3.4 3.2 %collective-permute-start = (f32[8,128]{1,0:T(8,128)S(1)}, f32[8,128]{1,0:T(8,128)S(1)}, u32[]{:S(2)}, u32[]{:S(2)}) collective-permute-start(f32[8,128]{1,0:T(8,128)S(1)} %get-tuple-element.16.g0.order), channel_id=1, source_target_pairs={{0,2},{1,3},{2,0},{3,1},{4,6},{5,7},{6,4},{7,5},{8,10},{9,11},{10,... | collective-permute-start | bytes 12296 | tf_op jit(solution)/shard_map/ppermute | solution.py:376
  6.5 0.6 %collective-permute-start.1 = (f32[8,128]{1,0:T(8,128)S(1)}, f32[8,128]{1,0:T(8,128)S(1)}, u32[]{:S(2)}, u32[]{:S(2)}) collective-permute-start(f32[8,128]{1,0:T(8,128)S(1)} %get-tuple-element.16.g0.order), channel_id=1, source_target_pairs={{0,1},{1,0},{2,3},{3,2},{4,5},{5,4},{6,7},{7,6},{8,9},{9,8},{10,11... | collective-permute-start | bytes 12296 | tf_op jit(solution)/shard_map/ppermute | solution.py:376
  7.1 0.6 %collective-permute-start.2 = (f32[8,128]{1,0:T(8,128)S(1)}, f32[8,128]{1,0:T(8,128)S(1)}, u32[]{:S(2)}, u32[]{:S(2)}) collective-permute-start(f32[8,128]{1,0:T(8,128)S(1)} %get-tuple-element.16.g0.order), channel_id=1, source_target_pairs={{0,3},{1,2},{2,1},{3,0},{4,7},{5,6},{6,5},{7,4},{8,11},{9,10},{10,... | collective-permute-start | bytes 12296 | tf_op jit(solution)/shard_map/ppermute | solution.py:376
  7.7 0.0 copy-done.1
  7.7 0.0 slice-start.1
  7.7 0.0 copy-start.3
  7.7 2.4 %far.2 = (f32[60,8,128]{2,1,0:T(8,128)S(1)}, f32[60,8,128]{2,1,0:T(8,128)S(1)}, f32[60,8,128]{2,1,0:T(8,128)S(1)}) custom-call(f32[63,8,128]{2,1,0:T(8,128)S(1)} %get-tuple-element.18.coef_ref, s32[4,60]{1,0:T(4,128)} %bitcast.5, bf16[240,128,128]{2,1,0:T(8,128)(2,1)S(1)} %copy-done.1, f32[8,128]{1,0:T(8,128)S(1)} %get-tuple-element.16.g0.order), custom_call_target="tpu_custom_call" | custom-call | flops 4000000000 | tf_op jit(solution)/shard_map/far/pallas_call | solution.py:360
  10.1 0.0 collective-permute-done.g1
  10.1 0.0 collective-permute-done.1.g2
  10.2 1.8 %collective-permute-done.2.g3 = f32[8,128]{1,0:T(8,128)S(1)} collective-permute-done((f32[8,128]{1,0:T(8,128)S(1)}, f32[8,128]{1,0:T(8,128)S(1)}, u32[]{:S(2)}, u32[]{:S(2)}) %collective-permute-start.2) | collective-permute-done | bytes 4128 | tf_op jit(solution)/shard_map/ppermute | solution.py:376
  12.0 0.0 copy-done.2
  12.0 0.0 copy-done.4
  12.0 0.1 group.1.order.p0
  12.1 1.2 %collective-permute-start.3 = (f32[17,8,128]{2,1,0:T(8,128)S(1)}, f32[17,8,128]{2,1,0:T(8,128)S(1)}, u32[]{:S(2)}, u32[]{:S(2)}) collective-permute-start(f32[17,8,128]{2,1,0:T(8,128)S(1)} %group.1.order.p0), channel_id=1, source_target_pairs={{0,2},{1,3},{2,0},{3,1},{4,6},{5,7},{6,4},{7,5},{8,10},{9,11},{10,... | collective-permute-start | bytes 208904 | tf_op jit(solution)/shard_map/ppermute | solution.py:376
  13.3 0.6 %collective-permute-start.4 = (f32[17,8,128]{2,1,0:T(8,128)S(1)}, f32[17,8,128]{2,1,0:T(8,128)S(1)}, u32[]{:S(2)}, u32[]{:S(2)}) collective-permute-start(f32[17,8,128]{2,1,0:T(8,128)S(1)} %group.1.order.p0), channel_id=1, source_target_pairs={{0,1},{1,0},{2,3},{3,2},{4,5},{5,4},{6,7},{7,6},{8,9},{9,8},{10,11... | collective-permute-start | bytes 208904 | tf_op jit(solution)/shard_map/ppermute | solution.py:376
  13.9 2.3 %collective-permute-start.5 = (f32[17,8,128]{2,1,0:T(8,128)S(1)}, f32[17,8,128]{2,1,0:T(8,128)S(1)}, u32[]{:S(2)}, u32[]{:S(2)}) collective-permute-start(f32[17,8,128]{2,1,0:T(8,128)S(1)} %group.1.order.p0), channel_id=1, source_target_pairs={{0,3},{1,2},{2,1},{3,0},{4,7},{5,6},{6,5},{7,4},{8,11},{9,10},{10,... | collective-permute-start | bytes 208904 | tf_op jit(solution)/shard_map/ppermute | solution.py:376
  16.2 0.0 slice-done
  16.2 0.0 slice-done.1
  16.2 0.0 copy-done.3
  16.2 0.0 copy-start
  16.2 3.4 %near.2 = (f32[92,8,128]{2,1,0:T(8,128)}, f32[92,8,128]{2,1,0:T(8,128)S(1)}, f32[92,8,128]{2,1,0:T(8,128)}) custom-call(bf16[32,8,128]{2,1,0:T(8,128)(2,1)S(1)} %copy-done.3, s32[8,32]{1,0:T(8,128)} %bitcast.4, bf16[256,128,128]{2,1,0:T(8,128)(2,1)S(1)} %bitcast.3, f32[60,8,128]{2,1,0:T(8,128)S(1)} %get-tuple-element.19.far_a, ...), custom_call_target="tpu_custom_call" | custom-call | flops 4000000000 | tf_op jit(solution)/shard_map/near/pallas_call | solution.py:360
  19.7 0.0 collective-permute-done.3.p1
  19.7 0.0 collective-permute-done.4.p2
  19.7 0.0 collective-permute-done.5.p3
  19.7 1.3 %pack.1 = (f32[64,8,128]{2,1,0:T(8,128)S(1)}, f32[64,8,128]{2,1,0:T(8,128)S(1)}) custom-call(f32[17,8,128]{2,1,0:T(8,128)S(1)} %group.1.order.p0, f32[17,8,128]{2,1,0:T(8,128)S(1)} %collective-permute-done.3.p1, f32[17,8,128]{2,1,0:T(8,128)S(1)} %collective-permute-done.4.p2, f32[17,8,128]{2,1,0:T(8,128)S(1)} %collective-permute-done.5.p3, ...), custom_call_target="tpu_custom_call" | custom-call | tf_op jit(solution)/shard_map/pack/pallas_call | solution.py:360
  21.0 0.1 collective-permute-start.6
  21.1 0.3 collective-permute-start.7
  21.4 7.8 %collective-permute-start.8 = (f32[92,8,128]{2,1,0:T(8,128)}, f32[92,8,128]{2,1,0:T(8,128)S(1)}, u32[]{:S(2)}, u32[]{:S(2)}) collective-permute-start(f32[92,8,128]{2,1,0:T(8,128)} %get-tuple-element.26), channel_id=1, source_target_pairs={{0,127},{1,2},{2,1},{3,4},{4,3},{5,6},{6,5},{7,8},{8,7},{9,10},{10... | collective-permute-start | bytes 1130504 | tf_op jit(solution)/shard_map/ppermute | solution.py:376
  29.1 0.0 collective-permute-done.6.core_ref
  29.1 0.7 %core.1 = f32[16,4,8,128]{3,2,1,0:T(8,128)} custom-call(f32[64,8,128]{2,1,0:T(8,128)S(1)} %get-tuple-element.23.keep_ref, f32[64,8,128]{2,1,0:T(8,128)S(1)} %collective-permute-done.6.core_ref), custom_call_target="tpu_custom_call" | custom-call | tf_op jit(solution)/shard_map/core/pallas_call | solution.py:360
  29.9 3.5 %all-to-all-start = ((f32[16,4,8,128]{3,2,1,0:T(8,128)}), f32[16,4,8,128]{3,2,1,0:T(8,128)S(1)}, u32[]{:S(2)}, u32[]{:S(2)}) async-start(f32[16,4,8,128]{3,2,1,0:T(8,128)} %core.1), calls=%async_computation | async-start | bytes 524288 | tf_op jit(solution)/shard_map/all_to_all | solution.py:420
  33.4 0.0 collective-permute-done.7.from_a
  33.4 3.7 %collective-permute-done.8.from_b = f32[92,8,128]{2,1,0:T(8,128)S(1)} collective-permute-done((f32[92,8,128]{2,1,0:T(8,128)}, f32[92,8,128]{2,1,0:T(8,128)S(1)}, u32[]{:S(2)}, u32[]{:S(2)}) %collective-permute-start.8) | collective-permute-done | bytes 376864 | tf_op jit(solution)/shard_map/ppermute | solution.py:376
  37.1 4.7 %all-to-all-done.top = f32[16,4,8,128]{3,2,1,0:T(8,128)S(1)} async-done(((f32[16,4,8,128]{3,2,1,0:T(8,128)}), f32[16,4,8,128]{3,2,1,0:T(8,128)S(1)}, u32[]{:S(2)}, u32[]{:S(2)}) %all-to-all-start) | async-done | bytes 262176 | tf_op jit(solution)/shard_map/all_to_all | solution.py:420
  41.8 0.0 copy-done
  41.8 2.4 %downward.1 = f32[32,8,128]{2,1,0:T(8,128)} custom-call(f32[16,4,8,128]{3,2,1,0:T(8,128)S(1)} %all-to-all-done.top, f32[92,8,128]{2,1,0:T(8,128)S(1)} %get-tuple-element.22.order.own, f32[92,8,128]{2,1,0:T(8,128)S(1)} %collective-permute-done.7.from_a, f32[92,8,128]{2,1,0:T(8,128)S(1)} %collective-permute-done.8.from_b, bf16[63,128,128]{2,1,0:T(8,128)(2,1)S(1)} %copy-done, ...), custom_call_target="tpu_custom_call" | custom-call | tf_op jit(solution)/shard_map/downward/pallas_call | solution.py:360
  (1 shorter events, 0.0 us)
Async XLA Ops:
  0.0 7.7 %copy-start.1 = (bf16[240,128,128]{2,1,0:T(8,128)(2,1)S(1)}, bf16[240,128,128]{2,1,0:T(8,128)(2,1)}, u32[]{:S(2)}) copy-start(bf16[240,128,128]{2,1,0:T(8,128)(2,1)} %far.3) | copy-start | bytes 23592964
  0.0 16.2 %slice-start = ((s8[8388608]{0:T(1024)(128)(4,1)}), s8[4194304]{0:T(1024)(128)(4,1)S(1)}, s32[]{:S(2)}) async-start(s8[8388608]{0:T(1024)(128)(4,1)} %bitcast.2), calls=%async_computation.1 | async-start | bytes 8388608
  3.3 8.6 %copy-start.2 = (bf16[4,128,128]{2,1,0:T(8,128)(2,1)S(1)}, bf16[4,128,128]{2,1,0:T(8,128)(2,1)}, u32[]{:S(2)}) copy-start(bf16[4,128,128]{2,1,0:T(8,128)(2,1)} %blocks.1) | copy-start | bytes 393220
  3.3 8.6 %copy-start.4 = (s32[1,4]{1,0:T(1,128)S(1)}, s32[1,4]{1,0:T(1,128)}, u32[]{:S(2)}) copy-start(s32[1,4]{1,0:T(1,128)} %group_list.1) | copy-start | bytes 52
  3.4 6.8 %collective-permute-start = (f32[8,128]{1,0:T(8,128)S(1)}, f32[8,128]{1,0:T(8,128)S(1)}, u32[]{:S(2)}, u32[]{:S(2)}) collective-permute-start(f32[8,128]{1,0:T(8,128)S(1)} %get-tuple-element.16.g0.order), channel_id=1, source_target_pairs={{0,2},{1,3},{2,0},{3,1},{4,6},{5,7},{6,4},{7,5},{8,10},{9,11},{10,... | collective-permute-start | bytes 12296 | tf_op jit(solution)/shard_map/ppermute | solution.py:376
  6.5 3.6 %collective-permute-start.1 = (f32[8,128]{1,0:T(8,128)S(1)}, f32[8,128]{1,0:T(8,128)S(1)}, u32[]{:S(2)}, u32[]{:S(2)}) collective-permute-start(f32[8,128]{1,0:T(8,128)S(1)} %get-tuple-element.16.g0.order), channel_id=1, source_target_pairs={{0,1},{1,0},{2,3},{3,2},{4,5},{5,4},{6,7},{7,6},{8,9},{9,8},{10,11... | collective-permute-start | bytes 12296 | tf_op jit(solution)/shard_map/ppermute | solution.py:376
  7.1 4.8 %collective-permute-start.2 = (f32[8,128]{1,0:T(8,128)S(1)}, f32[8,128]{1,0:T(8,128)S(1)}, u32[]{:S(2)}, u32[]{:S(2)}) collective-permute-start(f32[8,128]{1,0:T(8,128)S(1)} %get-tuple-element.16.g0.order), channel_id=1, source_target_pairs={{0,3},{1,2},{2,1},{3,0},{4,7},{5,6},{6,5},{7,4},{8,11},{9,10},{10,... | collective-permute-start | bytes 12296 | tf_op jit(solution)/shard_map/ppermute | solution.py:376
  7.7 8.5 %slice-start.1 = ((s8[8388608]{0:T(1024)(128)(4,1)}), s8[4194304]{0:T(1024)(128)(4,1)S(1)}, s32[]{:S(2)}) async-start(s8[8388608]{0:T(1024)(128)(4,1)} %bitcast.2), calls=%async_computation.2 | async-start | bytes 8388608
  7.7 8.5 %copy-start.3 = (bf16[32,8,128]{2,1,0:T(8,128)(2,1)S(1)}, bf16[32,8,128]{2,1,0:T(8,128)(2,1)}, u32[]{:S(2)}) copy-start(bf16[32,8,128]{2,1,0:T(8,128)(2,1)} %src_ref.1) | copy-start | bytes 196612
  12.1 7.6 %collective-permute-start.3 = (f32[17,8,128]{2,1,0:T(8,128)S(1)}, f32[17,8,128]{2,1,0:T(8,128)S(1)}, u32[]{:S(2)}, u32[]{:S(2)}) collective-permute-start(f32[17,8,128]{2,1,0:T(8,128)S(1)} %group.1.order.p0), channel_id=1, source_target_pairs={{0,2},{1,3},{2,0},{3,1},{4,6},{5,7},{6,4},{7,5},{8,10},{9,11},{10,... | collective-permute-start | bytes 208904 | tf_op jit(solution)/shard_map/ppermute | solution.py:376
  13.3 6.4 %collective-permute-start.4 = (f32[17,8,128]{2,1,0:T(8,128)S(1)}, f32[17,8,128]{2,1,0:T(8,128)S(1)}, u32[]{:S(2)}, u32[]{:S(2)}) collective-permute-start(f32[17,8,128]{2,1,0:T(8,128)S(1)} %group.1.order.p0), channel_id=1, source_target_pairs={{0,1},{1,0},{2,3},{3,2},{4,5},{5,4},{6,7},{7,6},{8,9},{9,8},{10,11... | collective-permute-start | bytes 208904 | tf_op jit(solution)/shard_map/ppermute | solution.py:376
  13.9 5.8 %collective-permute-start.5 = (f32[17,8,128]{2,1,0:T(8,128)S(1)}, f32[17,8,128]{2,1,0:T(8,128)S(1)}, u32[]{:S(2)}, u32[]{:S(2)}) collective-permute-start(f32[17,8,128]{2,1,0:T(8,128)S(1)} %group.1.order.p0), channel_id=1, source_target_pairs={{0,3},{1,2},{2,1},{3,0},{4,7},{5,6},{6,5},{7,4},{8,11},{9,10},{10,... | collective-permute-start | bytes 208904 | tf_op jit(solution)/shard_map/ppermute | solution.py:376
  16.2 25.6 %copy-start = (bf16[63,128,128]{2,1,0:T(8,128)(2,1)S(1)}, bf16[63,128,128]{2,1,0:T(8,128)(2,1)}, u32[]{:S(2)}) copy-start(bf16[63,128,128]{2,1,0:T(8,128)(2,1)} %down.1) | copy-start | bytes 6193156
  21.0 8.2 %collective-permute-start.6 = (f32[64,8,128]{2,1,0:T(8,128)S(1)}, f32[64,8,128]{2,1,0:T(8,128)S(1)}, u32[]{:S(2)}, u32[]{:S(2)}) collective-permute-start(f32[64,8,128]{2,1,0:T(8,128)S(1)} %get-tuple-element.24), channel_id=1, source_target_pairs={{0,4},{4,0},{8,12},{12,8},{16,20},{20,16},{24,28},{28,24},{32,36},... | collective-permute-start | bytes 786440 | tf_op jit(solution)/shard_map/ppermute | solution.py:376
  21.1 12.3 %collective-permute-start.7 = (f32[92,8,128]{2,1,0:T(8,128)}, f32[92,8,128]{2,1,0:T(8,128)S(1)}, u32[]{:S(2)}, u32[]{:S(2)}) collective-permute-start(f32[92,8,128]{2,1,0:T(8,128)} %get-tuple-element.25), channel_id=1, source_target_pairs={{0,1},{1,0},{2,3},{3,2},{4,5},{5,4},{6,7},{7,6},{8,9},{9,8},{10,11... | collective-permute-start | bytes 1130504 | tf_op jit(solution)/shard_map/ppermute | solution.py:376
  21.4 15.7 %collective-permute-start.8 = (f32[92,8,128]{2,1,0:T(8,128)}, f32[92,8,128]{2,1,0:T(8,128)S(1)}, u32[]{:S(2)}, u32[]{:S(2)}) collective-permute-start(f32[92,8,128]{2,1,0:T(8,128)} %get-tuple-element.26), channel_id=1, source_target_pairs={{0,127},{1,2},{2,1},{3,4},{4,3},{5,6},{6,5},{7,8},{8,7},{9,10},{10... | collective-permute-start | bytes 1130504 | tf_op jit(solution)/shard_map/ppermute | solution.py:376
  29.9 12.0 %all-to-all-start = ((f32[16,4,8,128]{3,2,1,0:T(8,128)}), f32[16,4,8,128]{3,2,1,0:T(8,128)S(1)}, u32[]{:S(2)}, u32[]{:S(2)}) async-start(f32[16,4,8,128]{3,2,1,0:T(8,128)} %core.1), calls=%async_computation | async-start | bytes 524288 | tf_op jit(solution)/shard_map/all_to_all | solution.py:420

commit v9 on v8

--- a/solution.py
+++ b/solution.py
@@ -233,19 +233,19 @@
     out_ref[TERMS, 3:4, 0:4] = group_list[...].astype(F32)
 
 
-def pack_kernel(p0, p1, p2, p3, order, keep_ref, send_ref, ids, a0, a1, a2, a3, sem):
+def pack_kernel(p0, p1, p2, p3, order, keep_ref, send_ref, whole, ids, a0, a1, a2, a3, sem):
     half = keep_ref.shape[0]
     parts = (p0, p1, p2, p3)
     accs = (a0, a1, a2, a3)
-    copies = [pltpu.make_async_copy(p.at[TERMS], ids.at[i], sem.at[i]) for i, p in enumerate(parts)]
-    for c in copies:
-        c.start()
+    for i, p in enumerate(parts):
+        whole[i] = p[TERMS].astype(jnp.int32)
+    copy = pltpu.make_async_copy(whole, ids, sem.at[0])
+    copy.start()
     for acc in accs:
         acc[...] = jnp.zeros(acc.shape, F32)
     own_sub = lax.axis_index("sub")
     own_core = lax.axis_index("leaf") & 1
-    for c in copies:
-        c.wait()
+    copy.wait()
 
     def place(leaf, entry):
         return (leaf & 1) * half + lax.shift_right_arithmetic(leaf, 1) * 4 + entry
@@ -257,15 +257,15 @@
 
     for j in range(UPPER_TERMS):
         for i, (p, acc) in enumerate(zip(parts, accs)):
-            node = ids[i, j // 4, j % 4].astype(jnp.int32)
+            node = ids[i, j // 4, j % 4]
             add(acc, lax.shift_right_arithmetic(node, 1), node & 1, p[j])
     for j in range(ROOT_TERMS):
         for i, (p, acc) in enumerate(zip(parts, accs)):
-            root = ids[i, 2, j].astype(jnp.int32)
+            root = ids[i, 2, j]
             add(acc, root, 2, p[UPPER_TERMS + j])
     for j in range(GROUP_TERMS):
         for i, (p, acc) in enumerate(zip(parts, accs)):
-            row = place(ids[i, 3, j].astype(jnp.int32), 3)
+            row = place(ids[i, 3, j], 3)
             acc[row] = acc[row] + p[TOP_TERMS + j]
 
     def total(first):
@@ -413,7 +413,8 @@
 
     keep, send = call(
         pack_kernel, "pack", 0, (shape(half), shape(half)), (*term_parts, own), [VMEM] * 4 + [ANY],
-        [pltpu.SMEM((subs,) + row, F32)] + [plane(2 * half + 1)] * 4 + [copies(subs)],
+        [pltpu.VMEM((subs,) + row, jnp.int32), pltpu.SMEM((subs,) + row, jnp.int32)] + [plane(2 * half + 1)] * 4
+        + [copies(1)],
     )
     from_core = permuted(send, "leaf", lambda i: i ^ 1)
     planes = call(core_kernel, "core", 0, shape(groups // 2, 4), (keep, from_core), [VMEM] * 2, [])

time: 44.5 us -> 44.6 us (level)
  no operation moved by 1% of the time
where the time goes in v9:
time: 44.6 us; the launch traced here: 44.3 us
  starting transfers between devices  20.1 us (45%)
  Pallas kernels  13.8 us (31%)
  waiting for transfers between devices  10.3 us (23%)
    ppermute x9, starting transfers between devices, permuted(): return lax.ppermute(x, axis, [(i, target(i)) for i in range(count)])  16.6 us
    pallas_call x7, Pallas kernels, call(): pl.pallas_call(kernel, out_shape=outs, in_specs=specs, out_specs=out_spec...  13.8 us
    ppermute x9, waiting for transfers between devices, permuted(): return lax.ppermute(x, axis, [(i, target(i)) for i in range(count)])  5.52 us
    all_to_all x1, waiting for transfers between devices, shards(): lax.all_to_all(pltpu.with_memory_space_constraint(planes, pltpu.VMEM), 'l...  4.73 us
    all_to_all x1, starting transfers between devices, shards(): lax.all_to_all(pltpu.with_memory_space_constraint(planes, pltpu.VMEM), 'l...  3.53 us
  transfers between devices with their start and end apart: 10, of which 3 were waited for; matrix products, arithmetic and copies ran while one was open for 0% of the time, Pallas kernels for 15%

profile of v9, /device:TPU:0, one launch (start us, length us, event | category | flops | bytes accessed | tf_op | source)
XLA Modules:
  0.0 44.3 jit_solution(13443374391851649300)
XLA Ops:
  0.0 0.0 copy-start.1
  0.0 0.0 slice-start
  0.0 3.3 %upward.1 = (f32[63,8,128]{2,1,0:T(8,128)S(1)}, f32[8,128]{1,0:T(8,128)S(1)}, f32[13,8,128]{2,1,0:T(8,128)S(1)}) custom-call(bf16[32,8,128]{2,1,0:T(8,128)(2,1)} %src_ref.1, s32[2,4]{1,0:T(2,128)} %upper_list_hbm.1, s32[1,4]{1,0:T(1,128)} %root_list_hbm.1, bf16[32,128,128]{2,1,0:T(8,128)(2,1)} %rb_hbm.1, bf16[63,128,128]{2,1,0:T(8,128)(2,1)} %up_hbm.1, ...), custom_call_target="tpu_custom_call" | custom-call | flops 4000000000 | tf_op jit(solution)/shard_map/upward/pallas_call | solution.py:360
  3.3 0.0 copy-start.2
  3.3 0.0 copy-start.4
  3.4 3.2 %collective-permute-start = (f32[8,128]{1,0:T(8,128)S(1)}, f32[8,128]{1,0:T(8,128)S(1)}, u32[]{:S(2)}, u32[]{:S(2)}) collective-permute-start(f32[8,128]{1,0:T(8,128)S(1)} %get-tuple-element.16.g0.order), channel_id=1, source_target_pairs={{0,2},{1,3},{2,0},{3,1},{4,6},{5,7},{6,4},{7,5},{8,10},{9,11},{10,... | collective-permute-start | bytes 12296 | tf_op jit(solution)/shard_map/ppermute | solution.py:376
  6.5 0.6 %collective-permute-start.1 = (f32[8,128]{1,0:T(8,128)S(1)}, f32[8,128]{1,0:T(8,128)S(1)}, u32[]{:S(2)}, u32[]{:S(2)}) collective-permute-start(f32[8,128]{1,0:T(8,128)S(1)} %get-tuple-element.16.g0.order), channel_id=1, source_target_pairs={{0,1},{1,0},{2,3},{3,2},{4,5},{5,4},{6,7},{7,6},{8,9},{9,8},{10,11... | collective-permute-start | bytes 12296 | tf_op jit(solution)/shard_map/ppermute | solution.py:376
  7.1 0.6 %collective-permute-start.2 = (f32[8,128]{1,0:T(8,128)S(1)}, f32[8,128]{1,0:T(8,128)S(1)}, u32[]{:S(2)}, u32[]{:S(2)}) collective-permute-start(f32[8,128]{1,0:T(8,128)S(1)} %get-tuple-element.16.g0.order), channel_id=1, source_target_pairs={{0,3},{1,2},{2,1},{3,0},{4,7},{5,6},{6,5},{7,4},{8,11},{9,10},{10,... | collective-permute-start | bytes 12296 | tf_op jit(solution)/shard_map/ppermute | solution.py:376
  7.7 0.0 copy-done.1
  7.7 0.0 slice-start.1
  7.7 0.0 copy-start.3
  7.7 2.4 %far.2 = (f32[60,8,128]{2,1,0:T(8,128)S(1)}, f32[60,8,128]{2,1,0:T(8,128)S(1)}, f32[60,8,128]{2,1,0:T(8,128)S(1)}) custom-call(f32[63,8,128]{2,1,0:T(8,128)S(1)} %get-tuple-element.18.coef_ref, s32[4,60]{1,0:T(4,128)} %bitcast.5, bf16[240,128,128]{2,1,0:T(8,128)(2,1)S(1)} %copy-done.1, f32[8,128]{1,0:T(8,128)S(1)} %get-tuple-element.16.g0.order), custom_call_target="tpu_custom_call" | custom-call | flops 4000000000 | tf_op jit(solution)/shard_map/far/pallas_call | solution.py:360
  10.1 0.0 collective-permute-done.g1
  10.1 0.0 collective-permute-done.1.g2
  10.2 1.8 %collective-permute-done.2.g3 = f32[8,128]{1,0:T(8,128)S(1)} collective-permute-done((f32[8,128]{1,0:T(8,128)S(1)}, f32[8,128]{1,0:T(8,128)S(1)}, u32[]{:S(2)}, u32[]{:S(2)}) %collective-permute-start.2) | collective-permute-done | bytes 4128 | tf_op jit(solution)/shard_map/ppermute | solution.py:376
  12.0 0.0 copy-done.2
  12.0 0.0 copy-done.4
  12.0 0.1 group.1.order.p0
  12.1 1.2 %collective-permute-start.3 = (f32[17,8,128]{2,1,0:T(8,128)S(1)}, f32[17,8,128]{2,1,0:T(8,128)S(1)}, u32[]{:S(2)}, u32[]{:S(2)}) collective-permute-start(f32[17,8,128]{2,1,0:T(8,128)S(1)} %group.1.order.p0), channel_id=1, source_target_pairs={{0,2},{1,3},{2,0},{3,1},{4,6},{5,7},{6,4},{7,5},{8,10},{9,11},{10,... | collective-permute-start | bytes 208904 | tf_op jit(solution)/shard_map/ppermute | solution.py:376
  13.3 0.6 %collective-permute-start.4 = (f32[17,8,128]{2,1,0:T(8,128)S(1)}, f32[17,8,128]{2,1,0:T(8,128)S(1)}, u32[]{:S(2)}, u32[]{:S(2)}) collective-permute-start(f32[17,8,128]{2,1,0:T(8,128)S(1)} %group.1.order.p0), channel_id=1, source_target_pairs={{0,1},{1,0},{2,3},{3,2},{4,5},{5,4},{6,7},{7,6},{8,9},{9,8},{10,11... | collective-permute-start | bytes 208904 | tf_op jit(solution)/shard_map/ppermute | solution.py:376
  13.9 2.3 %collective-permute-start.5 = (f32[17,8,128]{2,1,0:T(8,128)S(1)}, f32[17,8,128]{2,1,0:T(8,128)S(1)}, u32[]{:S(2)}, u32[]{:S(2)}) collective-permute-start(f32[17,8,128]{2,1,0:T(8,128)S(1)} %group.1.order.p0), channel_id=1, source_target_pairs={{0,3},{1,2},{2,1},{3,0},{4,7},{5,6},{6,5},{7,4},{8,11},{9,10},{10,... | collective-permute-start | bytes 208904 | tf_op jit(solution)/shard_map/ppermute | solution.py:376
  16.2 0.0 slice-done
  16.2 0.0 slice-done.1
  16.2 0.0 copy-done.3
  16.2 0.0 copy-start
  16.2 3.4 %near.2 = (f32[92,8,128]{2,1,0:T(8,128)}, f32[92,8,128]{2,1,0:T(8,128)S(1)}, f32[92,8,128]{2,1,0:T(8,128)}) custom-call(bf16[32,8,128]{2,1,0:T(8,128)(2,1)S(1)} %copy-done.3, s32[8,32]{1,0:T(8,128)} %bitcast.4, bf16[256,128,128]{2,1,0:T(8,128)(2,1)S(1)} %bitcast.3, f32[60,8,128]{2,1,0:T(8,128)S(1)} %get-tuple-element.19.far_a, ...), custom_call_target="tpu_custom_call" | custom-call | flops 4000000000 | tf_op jit(solution)/shard_map/near/pallas_call | solution.py:360
  19.7 0.0 collective-permute-done.3.p1
  19.7 0.0 collective-permute-done.4.p2
  19.7 0.0 collective-permute-done.5.p3
  19.7 1.3 %pack.1 = (f32[64,8,128]{2,1,0:T(8,128)S(1)}, f32[64,8,128]{2,1,0:T(8,128)S(1)}) custom-call(f32[17,8,128]{2,1,0:T(8,128)S(1)} %group.1.order.p0, f32[17,8,128]{2,1,0:T(8,128)S(1)} %collective-permute-done.3.p1, f32[17,8,128]{2,1,0:T(8,128)S(1)} %collective-permute-done.4.p2, f32[17,8,128]{2,1,0:T(8,128)S(1)} %collective-permute-done.5.p3, ...), custom_call_target="tpu_custom_call" | custom-call | tf_op jit(solution)/shard_map/pack/pallas_call | solution.py:360
  21.0 0.1 collective-permute-start.6
  21.1 0.3 collective-permute-start.7
  21.4 7.8 %collective-permute-start.8 = (f32[92,8,128]{2,1,0:T(8,128)}, f32[92,8,128]{2,1,0:T(8,128)S(1)}, u32[]{:S(2)}, u32[]{:S(2)}) collective-permute-start(f32[92,8,128]{2,1,0:T(8,128)} %get-tuple-element.26), channel_id=1, source_target_pairs={{0,127},{1,2},{2,1},{3,4},{4,3},{5,6},{6,5},{7,8},{8,7},{9,10},{10... | collective-permute-start | bytes 1130504 | tf_op jit(solution)/shard_map/ppermute | solution.py:376
  29.2 0.0 collective-permute-done.6.core_ref
  29.2 0.7 %core.1 = f32[16,4,8,128]{3,2,1,0:T(8,128)} custom-call(f32[64,8,128]{2,1,0:T(8,128)S(1)} %get-tuple-element.23.keep_ref, f32[64,8,128]{2,1,0:T(8,128)S(1)} %collective-permute-done.6.core_ref), custom_call_target="tpu_custom_call" | custom-call | tf_op jit(solution)/shard_map/core/pallas_call | solution.py:360
  29.9 3.5 %all-to-all-start = ((f32[16,4,8,128]{3,2,1,0:T(8,128)}), f32[16,4,8,128]{3,2,1,0:T(8,128)S(1)}, u32[]{:S(2)}, u32[]{:S(2)}) async-start(f32[16,4,8,128]{3,2,1,0:T(8,128)} %core.1), calls=%async_computation | async-start | bytes 524288 | tf_op jit(solution)/shard_map/all_to_all | solution.py:421
  33.4 0.0 collective-permute-done.7.from_a
  33.4 3.7 %collective-permute-done.8.from_b = f32[92,8,128]{2,1,0:T(8,128)S(1)} collective-permute-done((f32[92,8,128]{2,1,0:T(8,128)}, f32[92,8,128]{2,1,0:T(8,128)S(1)}, u32[]{:S(2)}, u32[]{:S(2)}) %collective-permute-start.8) | collective-permute-done | bytes 376864 | tf_op jit(solution)/shard_map/ppermute | solution.py:376
  37.1 4.7 %all-to-all-done.top = f32[16,4,8,128]{3,2,1,0:T(8,128)S(1)} async-done(((f32[16,4,8,128]{3,2,1,0:T(8,128)}), f32[16,4,8,128]{3,2,1,0:T(8,128)S(1)}, u32[]{:S(2)}, u32[]{:S(2)}) %all-to-all-start) | async-done | bytes 262176 | tf_op jit(solution)/shard_map/all_to_all | solution.py:421
  41.9 0.0 copy-done
  41.9 2.4 %downward.1 = f32[32,8,128]{2,1,0:T(8,128)} custom-call(f32[16,4,8,128]{3,2,1,0:T(8,128)S(1)} %all-to-all-done.top, f32[92,8,128]{2,1,0:T(8,128)S(1)} %get-tuple-element.22.order.own, f32[92,8,128]{2,1,0:T(8,128)S(1)} %collective-permute-done.7.from_a, f32[92,8,128]{2,1,0:T(8,128)S(1)} %collective-permute-done.8.from_b, bf16[63,128,128]{2,1,0:T(8,128)(2,1)S(1)} %copy-done, ...), custom_call_target="tpu_custom_call" | custom-call | tf_op jit(solution)/shard_map/downward/pallas_call | solution.py:360
  (1 shorter events, 0.0 us)
Async XLA Ops:
  0.0 7.7 %copy-start.1 = (bf16[240,128,128]{2,1,0:T(8,128)(2,1)S(1)}, bf16[240,128,128]{2,1,0:T(8,128)(2,1)}, u32[]{:S(2)}) copy-start(bf16[240,128,128]{2,1,0:T(8,128)(2,1)} %far.3) | copy-start | bytes 23592964
  0.0 16.2 %slice-start = ((s8[8388608]{0:T(1024)(128)(4,1)}), s8[4194304]{0:T(1024)(128)(4,1)S(1)}, s32[]{:S(2)}) async-start(s8[8388608]{0:T(1024)(128)(4,1)} %bitcast.2), calls=%async_computation.1 | async-start | bytes 8388608
  3.3 8.6 %copy-start.2 = (bf16[4,128,128]{2,1,0:T(8,128)(2,1)S(1)}, bf16[4,128,128]{2,1,0:T(8,128)(2,1)}, u32[]{:S(2)}) copy-start(bf16[4,128,128]{2,1,0:T(8,128)(2,1)} %blocks.1) | copy-start | bytes 393220
  3.3 8.6 %copy-start.4 = (s32[1,4]{1,0:T(1,128)S(1)}, s32[1,4]{1,0:T(1,128)}, u32[]{:S(2)}) copy-start(s32[1,4]{1,0:T(1,128)} %group_list.1) | copy-start | bytes 52
  3.4 6.8 %collective-permute-start = (f32[8,128]{1,0:T(8,128)S(1)}, f32[8,128]{1,0:T(8,128)S(1)}, u32[]{:S(2)}, u32[]{:S(2)}) collective-permute-start(f32[8,128]{1,0:T(8,128)S(1)} %get-tuple-element.16.g0.order), channel_id=1, source_target_pairs={{0,2},{1,3},{2,0},{3,1},{4,6},{5,7},{6,4},{7,5},{8,10},{9,11},{10,... | collective-permute-start | bytes 12296 | tf_op jit(solution)/shard_map/ppermute | solution.py:376
  6.5 3.6 %collective-permute-start.1 = (f32[8,128]{1,0:T(8,128)S(1)}, f32[8,128]{1,0:T(8,128)S(1)}, u32[]{:S(2)}, u32[]{:S(2)}) collective-permute-start(f32[8,128]{1,0:T(8,128)S(1)} %get-tuple-element.16.g0.order), channel_id=1, source_target_pairs={{0,1},{1,0},{2,3},{3,2},{4,5},{5,4},{6,7},{7,6},{8,9},{9,8},{10,11... | collective-permute-start | bytes 12296 | tf_op jit(solution)/shard_map/ppermute | solution.py:376
  7.1 4.8 %collective-permute-start.2 = (f32[8,128]{1,0:T(8,128)S(1)}, f32[8,128]{1,0:T(8,128)S(1)}, u32[]{:S(2)}, u32[]{:S(2)}) collective-permute-start(f32[8,128]{1,0:T(8,128)S(1)} %get-tuple-element.16.g0.order), channel_id=1, source_target_pairs={{0,3},{1,2},{2,1},{3,0},{4,7},{5,6},{6,5},{7,4},{8,11},{9,10},{10,... | collective-permute-start | bytes 12296 | tf_op jit(solution)/shard_map/ppermute | solution.py:376
  7.7 8.5 %slice-start.1 = ((s8[8388608]{0:T(1024)(128)(4,1)}), s8[4194304]{0:T(1024)(128)(4,1)S(1)}, s32[]{:S(2)}) async-start(s8[8388608]{0:T(1024)(128)(4,1)} %bitcast.2), calls=%async_computation.2 | async-start | bytes 8388608
  7.7 8.5 %copy-start.3 = (bf16[32,8,128]{2,1,0:T(8,128)(2,1)S(1)}, bf16[32,8,128]{2,1,0:T(8,128)(2,1)}, u32[]{:S(2)}) copy-start(bf16[32,8,128]{2,1,0:T(8,128)(2,1)} %src_ref.1) | copy-start | bytes 196612
  12.1 7.6 %collective-permute-start.3 = (f32[17,8,128]{2,1,0:T(8,128)S(1)}, f32[17,8,128]{2,1,0:T(8,128)S(1)}, u32[]{:S(2)}, u32[]{:S(2)}) collective-permute-start(f32[17,8,128]{2,1,0:T(8,128)S(1)} %group.1.order.p0), channel_id=1, source_target_pairs={{0,2},{1,3},{2,0},{3,1},{4,6},{5,7},{6,4},{7,5},{8,10},{9,11},{10,... | collective-permute-start | bytes 208904 | tf_op jit(solution)/shard_map/ppermute | solution.py:376
  13.3 6.4 %collective-permute-start.4 = (f32[17,8,128]{2,1,0:T(8,128)S(1)}, f32[17,8,128]{2,1,0:T(8,128)S(1)}, u32[]{:S(2)}, u32[]{:S(2)}) collective-permute-start(f32[17,8,128]{2,1,0:T(8,128)S(1)} %group.1.order.p0), channel_id=1, source_target_pairs={{0,1},{1,0},{2,3},{3,2},{4,5},{5,4},{6,7},{7,6},{8,9},{9,8},{10,11... | collective-permute-start | bytes 208904 | tf_op jit(solution)/shard_map/ppermute | solution.py:376
  13.9 5.8 %collective-permute-start.5 = (f32[17,8,128]{2,1,0:T(8,128)S(1)}, f32[17,8,128]{2,1,0:T(8,128)S(1)}, u32[]{:S(2)}, u32[]{:S(2)}) collective-permute-start(f32[17,8,128]{2,1,0:T(8,128)S(1)} %group.1.order.p0), channel_id=1, source_target_pairs={{0,3},{1,2},{2,1},{3,0},{4,7},{5,6},{6,5},{7,4},{8,11},{9,10},{10,... | collective-permute-start | bytes 208904 | tf_op jit(solution)/shard_map/ppermute | solution.py:376
  16.2 25.7 %copy-start = (bf16[63,128,128]{2,1,0:T(8,128)(2,1)S(1)}, bf16[63,128,128]{2,1,0:T(8,128)(2,1)}, u32[]{:S(2)}) copy-start(bf16[63,128,128]{2,1,0:T(8,128)(2,1)} %down.1) | copy-start | bytes 6193156
  21.0 8.2 %collective-permute-start.6 = (f32[64,8,128]{2,1,0:T(8,128)S(1)}, f32[64,8,128]{2,1,0:T(8,128)S(1)}, u32[]{:S(2)}, u32[]{:S(2)}) collective-permute-start(f32[64,8,128]{2,1,0:T(8,128)S(1)} %get-tuple-element.24), channel_id=1, source_target_pairs={{0,4},{4,0},{8,12},{12,8},{16,20},{20,16},{24,28},{28,24},{32,36},... | collective-permute-start | bytes 786440 | tf_op jit(solution)/shard_map/ppermute | solution.py:376
  21.1 12.3 %collective-permute-start.7 = (f32[92,8,128]{2,1,0:T(8,128)}, f32[92,8,128]{2,1,0:T(8,128)S(1)}, u32[]{:S(2)}, u32[]{:S(2)}) collective-permute-start(f32[92,8,128]{2,1,0:T(8,128)} %get-tuple-element.25), channel_id=1, source_target_pairs={{0,1},{1,0},{2,3},{3,2},{4,5},{5,4},{6,7},{7,6},{8,9},{9,8},{10,11... | collective-permute-start | bytes 1130504 | tf_op jit(solution)/shard_map/ppermute | solution.py:376
  21.4 15.7 %collective-permute-start.8 = (f32[92,8,128]{2,1,0:T(8,128)}, f32[92,8,128]{2,1,0:T(8,128)S(1)}, u32[]{:S(2)}, u32[]{:S(2)}) collective-permute-start(f32[92,8,128]{2,1,0:T(8,128)} %get-tuple-element.26), channel_id=1, source_target_pairs={{0,127},{1,2},{2,1},{3,4},{4,3},{5,6},{6,5},{7,8},{8,7},{9,10},{10... | collective-permute-start | bytes 1130504 | tf_op jit(solution)/shard_map/ppermute | solution.py:376
  29.9 12.0 %all-to-all-start = ((f32[16,4,8,128]{3,2,1,0:T(8,128)}), f32[16,4,8,128]{3,2,1,0:T(8,128)S(1)}, u32[]{:S(2)}, u32[]{:S(2)}) async-start(f32[16,4,8,128]{3,2,1,0:T(8,128)} %core.1), calls=%async_computation | async-start | bytes 524288 | tf_op jit(solution)/shard_map/all_to_all | solution.py:421

commit v10 on v9

--- a/solution.py
+++ b/solution.py
@@ -276,10 +276,6 @@
     send_ref[...] = total((1 - own_core) * half)
 
 
-def core_kernel(keep_ref, core_ref, out_ref):
-    out_ref[...] = (keep_ref[...] + core_ref[...]).reshape(out_ref.shape)
-
-
 def down_kernel(top, own, from_a, from_b, down, col_hbm, out_ref, col, level_down, sem):
     leaves = out_ref.shape[0]
     levels = leaves.bit_length() - 1
@@ -417,7 +413,7 @@
         + [copies(1)],
     )
     from_core = permuted(send, "leaf", lambda i: i ^ 1)
-    planes = call(core_kernel, "core", 0, shape(groups // 2, 4), (keep, from_core), [VMEM] * 2, [])
+    planes = (keep + from_core).reshape((groups // 2, 4) + row)
     fields = lax.all_to_all(
         pltpu.with_memory_space_constraint(planes, pltpu.VMEM), "leaf", 0, 0, tiled=True, axis_index_groups=[list(range(c, groups, 2)) for c in range(2)]
     )

time: 44.6 us -> 44.6 us (level)
  other arithmetic: 0.01 us -> 0.73 us
  Pallas kernels: 13.8 us -> 13.1 us
    add x0 -> x1, other arithmetic: none -> 0.73 us  [shards(): planes = (keep + from_core).reshape((groups // 2, 4) + row)]
    pallas_call x7 -> x6, Pallas kernels: 13.8 us -> 13.1 us  [call(): pl.pallas_call(kernel, out_shape=outs, in_specs=specs, out_specs=out_spec...]
  transfers between devices with their start and end apart: 10 -> 10, of which waited for: 3 -> 3; matrix products, arithmetic and copies ran while one was open for 0% -> 2% of each run, Pallas kernels for 15% -> 13%
where the time goes in v10:
time: 44.6 us; the launch traced here: 44.3 us
  starting transfers between devices  20.1 us (45%)
  Pallas kernels  13.1 us (29%)
  waiting for transfers between devices  10.3 us (23%)
  other arithmetic  0.73 us (2%)
    ppermute x9, starting transfers between devices, permuted(): return lax.ppermute(x, axis, [(i, target(i)) for i in range(count)])  16.6 us
    pallas_call x6, Pallas kernels, call(): pl.pallas_call(kernel, out_shape=outs, in_specs=specs, out_specs=out_spec...  13.1 us
    ppermute x9, waiting for transfers between devices, permuted(): return lax.ppermute(x, axis, [(i, target(i)) for i in range(count)])  5.51 us
    all_to_all x1, waiting for transfers between devices, shards(): lax.all_to_all(pltpu.with_memory_space_constraint(planes, pltpu.VMEM), 'l...  4.75 us
    all_to_all x1, starting transfers between devices, shards(): lax.all_to_all(pltpu.with_memory_space_constraint(planes, pltpu.VMEM), 'l...  3.53 us
  transfers between devices with their start and end apart: 10, of which 3 were waited for; matrix products, arithmetic and copies ran while one was open for 2% of the time, Pallas kernels for 13%

profile of v10, /device:TPU:0, one launch (start us, length us, event | category | flops | bytes accessed | tf_op | source)
XLA Modules:
  0.0 44.3 jit_solution(18326332097496819191)
XLA Ops:
  0.0 0.0 copy-start.1
  0.0 0.0 slice-start
  0.0 3.3 %upward.1 = (f32[63,8,128]{2,1,0:T(8,128)S(1)}, f32[8,128]{1,0:T(8,128)S(1)}, f32[13,8,128]{2,1,0:T(8,128)S(1)}) custom-call(bf16[32,8,128]{2,1,0:T(8,128)(2,1)} %src_ref.1, s32[2,4]{1,0:T(2,128)} %upper_list_hbm.1, s32[1,4]{1,0:T(1,128)} %root_list_hbm.1, bf16[32,128,128]{2,1,0:T(8,128)(2,1)} %rb_hbm.1, bf16[63,128,128]{2,1,0:T(8,128)(2,1)} %up_hbm.1, ...), custom_call_target="tpu_custom_call" | custom-call | flops 4000000000 | tf_op jit(solution)/shard_map/upward/pallas_call | solution.py:356
  3.3 0.0 copy-start.2
  3.4 0.0 copy-start.4
  3.4 3.2 %collective-permute-start = (f32[8,128]{1,0:T(8,128)S(1)}, f32[8,128]{1,0:T(8,128)S(1)}, u32[]{:S(2)}, u32[]{:S(2)}) collective-permute-start(f32[8,128]{1,0:T(8,128)S(1)} %get-tuple-element.16.g0.order), channel_id=1, source_target_pairs={{0,2},{1,3},{2,0},{3,1},{4,6},{5,7},{6,4},{7,5},{8,10},{9,11},{10,... | collective-permute-start | bytes 12296 | tf_op jit(solution)/shard_map/ppermute | solution.py:372
  6.6 0.6 %collective-permute-start.1 = (f32[8,128]{1,0:T(8,128)S(1)}, f32[8,128]{1,0:T(8,128)S(1)}, u32[]{:S(2)}, u32[]{:S(2)}) collective-permute-start(f32[8,128]{1,0:T(8,128)S(1)} %get-tuple-element.16.g0.order), channel_id=1, source_target_pairs={{0,1},{1,0},{2,3},{3,2},{4,5},{5,4},{6,7},{7,6},{8,9},{9,8},{10,11... | collective-permute-start | bytes 12296 | tf_op jit(solution)/shard_map/ppermute | solution.py:372
  7.1 0.6 %collective-permute-start.2 = (f32[8,128]{1,0:T(8,128)S(1)}, f32[8,128]{1,0:T(8,128)S(1)}, u32[]{:S(2)}, u32[]{:S(2)}) collective-permute-start(f32[8,128]{1,0:T(8,128)S(1)} %get-tuple-element.16.g0.order), channel_id=1, source_target_pairs={{0,3},{1,2},{2,1},{3,0},{4,7},{5,6},{6,5},{7,4},{8,11},{9,10},{10,... | collective-permute-start | bytes 12296 | tf_op jit(solution)/shard_map/ppermute | solution.py:372
  7.7 0.0 copy-done.1
  7.7 0.0 slice-start.1
  7.7 0.0 copy-start.3
  7.7 2.4 %far.2 = (f32[60,8,128]{2,1,0:T(8,128)S(1)}, f32[60,8,128]{2,1,0:T(8,128)S(1)}, f32[60,8,128]{2,1,0:T(8,128)S(1)}) custom-call(f32[63,8,128]{2,1,0:T(8,128)S(1)} %get-tuple-element.18.coef_ref, s32[4,60]{1,0:T(4,128)} %bitcast.7, bf16[240,128,128]{2,1,0:T(8,128)(2,1)S(1)} %copy-done.1, f32[8,128]{1,0:T(8,128)S(1)} %get-tuple-element.16.g0.order), custom_call_target="tpu_custom_call" | custom-call | flops 4000000000 | tf_op jit(solution)/shard_map/far/pallas_call | solution.py:356
  10.1 0.0 collective-permute-done.g1
  10.2 0.0 collective-permute-done.1.g2
  10.2 1.8 %collective-permute-done.2.g3 = f32[8,128]{1,0:T(8,128)S(1)} collective-permute-done((f32[8,128]{1,0:T(8,128)S(1)}, f32[8,128]{1,0:T(8,128)S(1)}, u32[]{:S(2)}, u32[]{:S(2)}) %collective-permute-start.2) | collective-permute-done | bytes 4128 | tf_op jit(solution)/shard_map/ppermute | solution.py:372
  12.0 0.0 copy-done.2
  12.0 0.0 copy-done.4
  12.0 0.1 group.1.order.p0
  12.1 1.2 %collective-permute-start.3 = (f32[17,8,128]{2,1,0:T(8,128)S(1)}, f32[17,8,128]{2,1,0:T(8,128)S(1)}, u32[]{:S(2)}, u32[]{:S(2)}) collective-permute-start(f32[17,8,128]{2,1,0:T(8,128)S(1)} %group.1.order.p0), channel_id=1, source_target_pairs={{0,2},{1,3},{2,0},{3,1},{4,6},{5,7},{6,4},{7,5},{8,10},{9,11},{10,... | collective-permute-start | bytes 208904 | tf_op jit(solution)/shard_map/ppermute | solution.py:372
  13.3 0.6 %collective-permute-start.4 = (f32[17,8,128]{2,1,0:T(8,128)S(1)}, f32[17,8,128]{2,1,0:T(8,128)S(1)}, u32[]{:S(2)}, u32[]{:S(2)}) collective-permute-start(f32[17,8,128]{2,1,0:T(8,128)S(1)} %group.1.order.p0), channel_id=1, source_target_pairs={{0,1},{1,0},{2,3},{3,2},{4,5},{5,4},{6,7},{7,6},{8,9},{9,8},{10,11... | collective-permute-start | bytes 208904 | tf_op jit(solution)/shard_map/ppermute | solution.py:372
  13.9 2.3 %collective-permute-start.5 = (f32[17,8,128]{2,1,0:T(8,128)S(1)}, f32[17,8,128]{2,1,0:T(8,128)S(1)}, u32[]{:S(2)}, u32[]{:S(2)}) collective-permute-start(f32[17,8,128]{2,1,0:T(8,128)S(1)} %group.1.order.p0), channel_id=1, source_target_pairs={{0,3},{1,2},{2,1},{3,0},{4,7},{5,6},{6,5},{7,4},{8,11},{9,10},{10,... | collective-permute-start | bytes 208904 | tf_op jit(solution)/shard_map/ppermute | solution.py:372
  16.2 0.0 slice-done
  16.2 0.0 slice-done.1
  16.2 0.0 copy-done.3
  16.2 0.0 copy-start
  16.2 3.4 %near.2 = (f32[92,8,128]{2,1,0:T(8,128)}, f32[92,8,128]{2,1,0:T(8,128)S(1)}, f32[92,8,128]{2,1,0:T(8,128)}) custom-call(bf16[32,8,128]{2,1,0:T(8,128)(2,1)S(1)} %copy-done.3, s32[8,32]{1,0:T(8,128)} %bitcast.6, bf16[256,128,128]{2,1,0:T(8,128)(2,1)S(1)} %bitcast.4, f32[60,8,128]{2,1,0:T(8,128)S(1)} %get-tuple-element.19.far_a, ...), custom_call_target="tpu_custom_call" | custom-call | flops 4000000000 | tf_op jit(solution)/shard_map/near/pallas_call | solution.py:356
  19.7 0.0 collective-permute-done.3.p1
  19.7 0.0 collective-permute-done.4.p2
  19.7 0.0 collective-permute-done.5.p3
  19.7 1.3 %pack.1 = (f32[64,8,128]{2,1,0:T(8,128)S(1)}, f32[64,8,128]{2,1,0:T(8,128)S(1)}) custom-call(f32[17,8,128]{2,1,0:T(8,128)S(1)} %group.1.order.p0, f32[17,8,128]{2,1,0:T(8,128)S(1)} %collective-permute-done.3.p1, f32[17,8,128]{2,1,0:T(8,128)S(1)} %collective-permute-done.4.p2, f32[17,8,128]{2,1,0:T(8,128)S(1)} %collective-permute-done.5.p3, ...), custom_call_target="tpu_custom_call" | custom-call | tf_op jit(solution)/shard_map/pack/pallas_call | solution.py:356
  21.0 0.1 collective-permute-start.6
  21.1 0.3 collective-permute-start.7
  21.4 7.8 %collective-permute-start.8 = (f32[92,8,128]{2,1,0:T(8,128)}, f32[92,8,128]{2,1,0:T(8,128)S(1)}, u32[]{:S(2)}, u32[]{:S(2)}) collective-permute-start(f32[92,8,128]{2,1,0:T(8,128)} %get-tuple-element.26), channel_id=1, source_target_pairs={{0,127},{1,2},{2,1},{3,4},{4,3},{5,6},{6,5},{7,8},{8,7},{9,10},{10... | collective-permute-start | bytes 1130504 | tf_op jit(solution)/shard_map/ppermute | solution.py:372
  29.2 0.0 collective-permute-done.6
  29.2 0.7 %add.3 = f32[64,8,128]{2,1,0:T(8,128)} add(f32[64,8,128]{2,1,0:T(8,128)S(1)} %get-tuple-element.23, f32[64,8,128]{2,1,0:T(8,128)S(1)} %collective-permute-done.6) | non-fusion elementwise | flops 65536 | bytes 786432 | tf_op jit(solution)/shard_map/add | solution.py:416
  29.9 3.5 %all-to-all-start = ((f32[16,4,8,128]{3,2,1,0:T(8,128)}), f32[16,4,8,128]{3,2,1,0:T(8,128)S(1)}, u32[]{:S(2)}, u32[]{:S(2)}) async-start(f32[16,4,8,128]{3,2,1,0:T(8,128)} %bitcast.5), calls=%async_computation | async-start | bytes 524288 | tf_op jit(solution)/shard_map/all_to_all | solution.py:417
  33.5 0.0 collective-permute-done.7.from_a
  33.5 3.7 %collective-permute-done.8.from_b = f32[92,8,128]{2,1,0:T(8,128)S(1)} collective-permute-done((f32[92,8,128]{2,1,0:T(8,128)}, f32[92,8,128]{2,1,0:T(8,128)S(1)}, u32[]{:S(2)}, u32[]{:S(2)}) %collective-permute-start.8) | collective-permute-done | bytes 376864 | tf_op jit(solution)/shard_map/ppermute | solution.py:372
  37.1 4.7 %all-to-all-done.top = f32[16,4,8,128]{3,2,1,0:T(8,128)S(1)} async-done(((f32[16,4,8,128]{3,2,1,0:T(8,128)}), f32[16,4,8,128]{3,2,1,0:T(8,128)S(1)}, u32[]{:S(2)}, u32[]{:S(2)}) %all-to-all-start) | async-done | bytes 262176 | tf_op jit(solution)/shard_map/all_to_all | solution.py:417
  41.9 0.0 copy-done
  41.9 2.4 %downward.1 = f32[32,8,128]{2,1,0:T(8,128)} custom-call(f32[16,4,8,128]{3,2,1,0:T(8,128)S(1)} %all-to-all-done.top, f32[92,8,128]{2,1,0:T(8,128)S(1)} %get-tuple-element.22.order.own, f32[92,8,128]{2,1,0:T(8,128)S(1)} %collective-permute-done.7.from_a, f32[92,8,128]{2,1,0:T(8,128)S(1)} %collective-permute-done.8.from_b, bf16[63,128,128]{2,1,0:T(8,128)(2,1)S(1)} %copy-done, ...), custom_call_target="tpu_custom_call" | custom-call | tf_op jit(solution)/shard_map/downward/pallas_call | solution.py:356
  (1 shorter events, 0.0 us)
Async XLA Ops:
  0.0 7.7 %copy-start.1 = (bf16[240,128,128]{2,1,0:T(8,128)(2,1)S(1)}, bf16[240,128,128]{2,1,0:T(8,128)(2,1)}, u32[]{:S(2)}) copy-start(bf16[240,128,128]{2,1,0:T(8,128)(2,1)} %far.3) | copy-start | bytes 23592964
  0.0 16.2 %slice-start = ((s8[8388608]{0:T(1024)(128)(4,1)}), s8[4194304]{0:T(1024)(128)(4,1)S(1)}, s32[]{:S(2)}) async-start(s8[8388608]{0:T(1024)(128)(4,1)} %bitcast.3), calls=%async_computation.1 | async-start | bytes 8388608
  3.3 8.6 %copy-start.2 = (bf16[4,128,128]{2,1,0:T(8,128)(2,1)S(1)}, bf16[4,128,128]{2,1,0:T(8,128)(2,1)}, u32[]{:S(2)}) copy-start(bf16[4,128,128]{2,1,0:T(8,128)(2,1)} %blocks.1) | copy-start | bytes 393220
  3.4 8.6 %copy-start.4 = (s32[1,4]{1,0:T(1,128)S(1)}, s32[1,4]{1,0:T(1,128)}, u32[]{:S(2)}) copy-start(s32[1,4]{1,0:T(1,128)} %group_list.1) | copy-start | bytes 52
  3.4 6.8 %collective-permute-start = (f32[8,128]{1,0:T(8,128)S(1)}, f32[8,128]{1,0:T(8,128)S(1)}, u32[]{:S(2)}, u32[]{:S(2)}) collective-permute-start(f32[8,128]{1,0:T(8,128)S(1)} %get-tuple-element.16.g0.order), channel_id=1, source_target_pairs={{0,2},{1,3},{2,0},{3,1},{4,6},{5,7},{6,4},{7,5},{8,10},{9,11},{10,... | collective-permute-start | bytes 12296 | tf_op jit(solution)/shard_map/ppermute | solution.py:372
  6.6 3.6 %collective-permute-start.1 = (f32[8,128]{1,0:T(8,128)S(1)}, f32[8,128]{1,0:T(8,128)S(1)}, u32[]{:S(2)}, u32[]{:S(2)}) collective-permute-start(f32[8,128]{1,0:T(8,128)S(1)} %get-tuple-element.16.g0.order), channel_id=1, source_target_pairs={{0,1},{1,0},{2,3},{3,2},{4,5},{5,4},{6,7},{7,6},{8,9},{9,8},{10,11... | collective-permute-start | bytes 12296 | tf_op jit(solution)/shard_map/ppermute | solution.py:372
  7.1 4.8 %collective-permute-start.2 = (f32[8,128]{1,0:T(8,128)S(1)}, f32[8,128]{1,0:T(8,128)S(1)}, u32[]{:S(2)}, u32[]{:S(2)}) collective-permute-start(f32[8,128]{1,0:T(8,128)S(1)} %get-tuple-element.16.g0.order), channel_id=1, source_target_pairs={{0,3},{1,2},{2,1},{3,0},{4,7},{5,6},{6,5},{7,4},{8,11},{9,10},{10,... | collective-permute-start | bytes 12296 | tf_op jit(solution)/shard_map/ppermute | solution.py:372
  7.7 8.5 %slice-start.1 = ((s8[8388608]{0:T(1024)(128)(4,1)}), s8[4194304]{0:T(1024)(128)(4,1)S(1)}, s32[]{:S(2)}) async-start(s8[8388608]{0:T(1024)(128)(4,1)} %bitcast.3), calls=%async_computation.2 | async-start | bytes 8388608
  7.7 8.5 %copy-start.3 = (bf16[32,8,128]{2,1,0:T(8,128)(2,1)S(1)}, bf16[32,8,128]{2,1,0:T(8,128)(2,1)}, u32[]{:S(2)}) copy-start(bf16[32,8,128]{2,1,0:T(8,128)(2,1)} %src_ref.1) | copy-start | bytes 196612
  12.1 7.6 %collective-permute-start.3 = (f32[17,8,128]{2,1,0:T(8,128)S(1)}, f32[17,8,128]{2,1,0:T(8,128)S(1)}, u32[]{:S(2)}, u32[]{:S(2)}) collective-permute-start(f32[17,8,128]{2,1,0:T(8,128)S(1)} %group.1.order.p0), channel_id=1, source_target_pairs={{0,2},{1,3},{2,0},{3,1},{4,6},{5,7},{6,4},{7,5},{8,10},{9,11},{10,... | collective-permute-start | bytes 208904 | tf_op jit(solution)/shard_map/ppermute | solution.py:372
  13.3 6.4 %collective-permute-start.4 = (f32[17,8,128]{2,1,0:T(8,128)S(1)}, f32[17,8,128]{2,1,0:T(8,128)S(1)}, u32[]{:S(2)}, u32[]{:S(2)}) collective-permute-start(f32[17,8,128]{2,1,0:T(8,128)S(1)} %group.1.order.p0), channel_id=1, source_target_pairs={{0,1},{1,0},{2,3},{3,2},{4,5},{5,4},{6,7},{7,6},{8,9},{9,8},{10,11... | collective-permute-start | bytes 208904 | tf_op jit(solution)/shard_map/ppermute | solution.py:372
  13.9 5.8 %collective-permute-start.5 = (f32[17,8,128]{2,1,0:T(8,128)S(1)}, f32[17,8,128]{2,1,0:T(8,128)S(1)}, u32[]{:S(2)}, u32[]{:S(2)}) collective-permute-start(f32[17,8,128]{2,1,0:T(8,128)S(1)} %group.1.order.p0), channel_id=1, source_target_pairs={{0,3},{1,2},{2,1},{3,0},{4,7},{5,6},{6,5},{7,4},{8,11},{9,10},{10,... | collective-permute-start | bytes 208904 | tf_op jit(solution)/shard_map/ppermute | solution.py:372
  16.2 25.7 %copy-start = (bf16[63,128,128]{2,1,0:T(8,128)(2,1)S(1)}, bf16[63,128,128]{2,1,0:T(8,128)(2,1)}, u32[]{:S(2)}) copy-start(bf16[63,128,128]{2,1,0:T(8,128)(2,1)} %down.1) | copy-start | bytes 6193156
  21.0 8.2 %collective-permute-start.6 = (f32[64,8,128]{2,1,0:T(8,128)S(1)}, f32[64,8,128]{2,1,0:T(8,128)S(1)}, u32[]{:S(2)}, u32[]{:S(2)}) collective-permute-start(f32[64,8,128]{2,1,0:T(8,128)S(1)} %get-tuple-element.24), channel_id=1, source_target_pairs={{0,4},{4,0},{8,12},{12,8},{16,20},{20,16},{24,28},{28,24},{32,36},... | collective-permute-start | bytes 786440 | tf_op jit(solution)/shard_map/ppermute | solution.py:372
  21.1 12.3 %collective-permute-start.7 = (f32[92,8,128]{2,1,0:T(8,128)}, f32[92,8,128]{2,1,0:T(8,128)S(1)}, u32[]{:S(2)}, u32[]{:S(2)}) collective-permute-start(f32[92,8,128]{2,1,0:T(8,128)} %get-tuple-element.25), channel_id=1, source_target_pairs={{0,1},{1,0},{2,3},{3,2},{4,5},{5,4},{6,7},{7,6},{8,9},{9,8},{10,11... | collective-permute-start | bytes 1130504 | tf_op jit(solution)/shard_map/ppermute | solution.py:372
  21.4 15.7 %collective-permute-start.8 = (f32[92,8,128]{2,1,0:T(8,128)}, f32[92,8,128]{2,1,0:T(8,128)S(1)}, u32[]{:S(2)}, u32[]{:S(2)}) collective-permute-start(f32[92,8,128]{2,1,0:T(8,128)} %get-tuple-element.26), channel_id=1, source_target_pairs={{0,127},{1,2},{2,1},{3,4},{4,3},{5,6},{6,5},{7,8},{8,7},{9,10},{10... | collective-permute-start | bytes 1130504 | tf_op jit(solution)/shard_map/ppermute | solution.py:372
  29.9 12.0 %all-to-all-start = ((f32[16,4,8,128]{3,2,1,0:T(8,128)}), f32[16,4,8,128]{3,2,1,0:T(8,128)S(1)}, u32[]{:S(2)}, u32[]{:S(2)}) async-start(f32[16,4,8,128]{3,2,1,0:T(8,128)} %bitcast.5), calls=%async_computation | async-start | bytes 524288 | tf_op jit(solution)/shard_map/all_to_all | solution.py:417

commit v11 on v9

--- a/solution.py
+++ b/solution.py
@@ -233,15 +233,15 @@
     out_ref[TERMS, 3:4, 0:4] = group_list[...].astype(F32)
 
 
-def pack_kernel(p0, p1, p2, p3, order, keep_ref, send_ref, whole, ids, a0, a1, a2, a3, sem):
+def pack_kernel(p0, p1, p2, p3, order, keep_ref, send_ref, whole, ids, a0, a1, sem):
     half = keep_ref.shape[0]
     parts = (p0, p1, p2, p3)
-    accs = (a0, a1, a2, a3)
+    accs = (a0, a1, a0, a1)
     for i, p in enumerate(parts):
         whole[i] = p[TERMS].astype(jnp.int32)
     copy = pltpu.make_async_copy(whole, ids, sem.at[0])
     copy.start()
-    for acc in accs:
+    for acc in (a0, a1):
         acc[...] = jnp.zeros(acc.shape, F32)
     own_sub = lax.axis_index("sub")
     own_core = lax.axis_index("leaf") & 1
@@ -270,7 +270,7 @@
 
     def total(first):
         part = pl.ds(first, half)
-        return (a0[part] + a1[part]) + (a2[part] + a3[part])
+        return a0[part] + a1[part]
 
     keep_ref[...] = total(own_core * half)
     send_ref[...] = total((1 - own_core) * half)
@@ -413,7 +413,7 @@
 
     keep, send = call(
         pack_kernel, "pack", 0, (shape(half), shape(half)), (*term_parts, own), [VMEM] * 4 + [ANY],
-        [pltpu.VMEM((subs,) + row, jnp.int32), pltpu.SMEM((subs,) + row, jnp.int32)] + [plane(2 * half + 1)] * 4
+        [pltpu.VMEM((subs,) + row, jnp.int32), pltpu.SMEM((subs,) + row, jnp.int32)] + [plane(2 * half + 1)] * 2
         + [copies(1)],
     )
     from_core = permuted(send, "leaf", lambda i: i ^ 1)

time: 44.6 us -> 44.4 us (level)
  no operation moved by 1% of the time
where the time goes in v11:
time: 44.4 us; the launch traced here: 44.2 us
  starting transfers between devices  20.1 us (45%)
  Pallas kernels  13.6 us (31%)
  waiting for transfers between devices  10.3 us (23%)
    ppermute x9, starting transfers between devices, permuted(): return lax.ppermute(x, axis, [(i, target(i)) for i in range(count)])  16.6 us
    pallas_call x7, Pallas kernels, call(): pl.pallas_call(kernel, out_shape=outs, in_specs=specs, out_specs=out_spec...  13.6 us
    ppermute x9, waiting for transfers between devices, permuted(): return lax.ppermute(x, axis, [(i, target(i)) for i in range(count)])  5.52 us
    all_to_all x1, waiting for transfers between devices, shards(): lax.all_to_all(pltpu.with_memory_space_constraint(planes, pltpu.VMEM), 'l...  4.73 us
    all_to_all x1, starting transfers between devices, shards(): lax.all_to_all(pltpu.with_memory_space_constraint(planes, pltpu.VMEM), 'l...  3.53 us
  transfers between devices with their start and end apart: 10, of which 3 were waited for; matrix products, arithmetic and copies ran while one was open for 0% of the time, Pallas kernels for 15%

profile of v11, /device:TPU:0, one launch (start us, length us, event | category | flops | bytes accessed | tf_op | source)
XLA Modules:
  0.0 44.2 jit_solution(7279886531450682875)
XLA Ops:
  0.0 0.0 copy-start.1
  0.0 0.0 slice-start
  0.0 3.3 %upward.1 = (f32[63,8,128]{2,1,0:T(8,128)S(1)}, f32[8,128]{1,0:T(8,128)S(1)}, f32[13,8,128]{2,1,0:T(8,128)S(1)}) custom-call(bf16[32,8,128]{2,1,0:T(8,128)(2,1)} %src_ref.1, s32[2,4]{1,0:T(2,128)} %upper_list_hbm.1, s32[1,4]{1,0:T(1,128)} %root_list_hbm.1, bf16[32,128,128]{2,1,0:T(8,128)(2,1)} %rb_hbm.1, bf16[63,128,128]{2,1,0:T(8,128)(2,1)} %up_hbm.1, ...), custom_call_target="tpu_custom_call" | custom-call | flops 4000000000 | tf_op jit(solution)/shard_map/upward/pallas_call | solution.py:360
  3.3 0.0 copy-start.2
  3.3 0.0 copy-start.4
  3.4 3.2 %collective-permute-start = (f32[8,128]{1,0:T(8,128)S(1)}, f32[8,128]{1,0:T(8,128)S(1)}, u32[]{:S(2)}, u32[]{:S(2)}) collective-permute-start(f32[8,128]{1,0:T(8,128)S(1)} %get-tuple-element.16.g0.order), channel_id=1, source_target_pairs={{0,2},{1,3},{2,0},{3,1},{4,6},{5,7},{6,4},{7,5},{8,10},{9,11},{10,... | collective-permute-start | bytes 12296 | tf_op jit(solution)/shard_map/ppermute | solution.py:376
  6.5 0.6 %collective-permute-start.1 = (f32[8,128]{1,0:T(8,128)S(1)}, f32[8,128]{1,0:T(8,128)S(1)}, u32[]{:S(2)}, u32[]{:S(2)}) collective-permute-start(f32[8,128]{1,0:T(8,128)S(1)} %get-tuple-element.16.g0.order), channel_id=1, source_target_pairs={{0,1},{1,0},{2,3},{3,2},{4,5},{5,4},{6,7},{7,6},{8,9},{9,8},{10,11... | collective-permute-start | bytes 12296 | tf_op jit(solution)/shard_map/ppermute | solution.py:376
  7.1 0.6 %collective-permute-start.2 = (f32[8,128]{1,0:T(8,128)S(1)}, f32[8,128]{1,0:T(8,128)S(1)}, u32[]{:S(2)}, u32[]{:S(2)}) collective-permute-start(f32[8,128]{1,0:T(8,128)S(1)} %get-tuple-element.16.g0.order), channel_id=1, source_target_pairs={{0,3},{1,2},{2,1},{3,0},{4,7},{5,6},{6,5},{7,4},{8,11},{9,10},{10,... | collective-permute-start | bytes 12296 | tf_op jit(solution)/shard_map/ppermute | solution.py:376
  7.7 0.0 copy-done.1
  7.7 0.0 slice-start.1
  7.7 0.0 copy-start.3
  7.7 2.4 %far.2 = (f32[60,8,128]{2,1,0:T(8,128)S(1)}, f32[60,8,128]{2,1,0:T(8,128)S(1)}, f32[60,8,128]{2,1,0:T(8,128)S(1)}) custom-call(f32[63,8,128]{2,1,0:T(8,128)S(1)} %get-tuple-element.18.coef_ref, s32[4,60]{1,0:T(4,128)} %bitcast.5, bf16[240,128,128]{2,1,0:T(8,128)(2,1)S(1)} %copy-done.1, f32[8,128]{1,0:T(8,128)S(1)} %get-tuple-element.16.g0.order), custom_call_target="tpu_custom_call" | custom-call | flops 4000000000 | tf_op jit(solution)/shard_map/far/pallas_call | solution.py:360
  10.1 0.0 collective-permute-done.g1
  10.1 0.0 collective-permute-done.1.g2
  10.2 1.8 %collective-permute-done.2.g3 = f32[8,128]{1,0:T(8,128)S(1)} collective-permute-done((f32[8,128]{1,0:T(8,128)S(1)}, f32[8,128]{1,0:T(8,128)S(1)}, u32[]{:S(2)}, u32[]{:S(2)}) %collective-permute-start.2) | collective-permute-done | bytes 4128 | tf_op jit(solution)/shard_map/ppermute | solution.py:376
  12.0 0.0 copy-done.2
  12.0 0.0 copy-done.4
  12.0 0.1 group.1.order.p0
  12.1 1.2 %collective-permute-start.3 = (f32[17,8,128]{2,1,0:T(8,128)S(1)}, f32[17,8,128]{2,1,0:T(8,128)S(1)}, u32[]{:S(2)}, u32[]{:S(2)}) collective-permute-start(f32[17,8,128]{2,1,0:T(8,128)S(1)} %group.1.order.p0), channel_id=1, source_target_pairs={{0,2},{1,3},{2,0},{3,1},{4,6},{5,7},{6,4},{7,5},{8,10},{9,11},{10,... | collective-permute-start | bytes 208904 | tf_op jit(solution)/shard_map/ppermute | solution.py:376
  13.3 0.6 %collective-permute-start.4 = (f32[17,8,128]{2,1,0:T(8,128)S(1)}, f32[17,8,128]{2,1,0:T(8,128)S(1)}, u32[]{:S(2)}, u32[]{:S(2)}) collective-permute-start(f32[17,8,128]{2,1,0:T(8,128)S(1)} %group.1.order.p0), channel_id=1, source_target_pairs={{0,1},{1,0},{2,3},{3,2},{4,5},{5,4},{6,7},{7,6},{8,9},{9,8},{10,11... | collective-permute-start | bytes 208904 | tf_op jit(solution)/shard_map/ppermute | solution.py:376
  13.9 2.3 %collective-permute-start.5 = (f32[17,8,128]{2,1,0:T(8,128)S(1)}, f32[17,8,128]{2,1,0:T(8,128)S(1)}, u32[]{:S(2)}, u32[]{:S(2)}) collective-permute-start(f32[17,8,128]{2,1,0:T(8,128)S(1)} %group.1.order.p0), channel_id=1, source_target_pairs={{0,3},{1,2},{2,1},{3,0},{4,7},{5,6},{6,5},{7,4},{8,11},{9,10},{10,... | collective-permute-start | bytes 208904 | tf_op jit(solution)/shard_map/ppermute | solution.py:376
  16.2 0.0 slice-done
  16.2 0.0 slice-done.1
  16.2 0.0 copy-done.3
  16.2 0.0 copy-start
  16.2 3.4 %near.2 = (f32[92,8,128]{2,1,0:T(8,128)}, f32[92,8,128]{2,1,0:T(8,128)S(1)}, f32[92,8,128]{2,1,0:T(8,128)}) custom-call(bf16[32,8,128]{2,1,0:T(8,128)(2,1)S(1)} %copy-done.3, s32[8,32]{1,0:T(8,128)} %bitcast.4, bf16[256,128,128]{2,1,0:T(8,128)(2,1)S(1)} %bitcast.3, f32[60,8,128]{2,1,0:T(8,128)S(1)} %get-tuple-element.19.far_a, ...), custom_call_target="tpu_custom_call" | custom-call | flops 4000000000 | tf_op jit(solution)/shard_map/near/pallas_call | solution.py:360
  19.7 0.0 collective-permute-done.3.p1
  19.7 0.0 collective-permute-done.4.p2
  19.7 0.0 collective-permute-done.5.p3
  19.7 1.2 %pack.1 = (f32[64,8,128]{2,1,0:T(8,128)S(1)}, f32[64,8,128]{2,1,0:T(8,128)S(1)}) custom-call(f32[17,8,128]{2,1,0:T(8,128)S(1)} %group.1.order.p0, f32[17,8,128]{2,1,0:T(8,128)S(1)} %collective-permute-done.3.p1, f32[17,8,128]{2,1,0:T(8,128)S(1)} %collective-permute-done.4.p2, f32[17,8,128]{2,1,0:T(8,128)S(1)} %collective-permute-done.5.p3, ...), custom_call_target="tpu_custom_call" | custom-call | tf_op jit(solution)/shard_map/pack/pallas_call | solution.py:360
  20.9 0.1 collective-permute-start.6
  21.0 0.3 collective-permute-start.7
  21.3 7.8 %collective-permute-start.8 = (f32[92,8,128]{2,1,0:T(8,128)}, f32[92,8,128]{2,1,0:T(8,128)S(1)}, u32[]{:S(2)}, u32[]{:S(2)}) collective-permute-start(f32[92,8,128]{2,1,0:T(8,128)} %get-tuple-element.26), channel_id=1, source_target_pairs={{0,127},{1,2},{2,1},{3,4},{4,3},{5,6},{6,5},{7,8},{8,7},{9,10},{10... | collective-permute-start | bytes 1130504 | tf_op jit(solution)/shard_map/ppermute | solution.py:376
  29.0 0.0 collective-permute-done.6.core_ref
  29.0 0.7 %core.1 = f32[16,4,8,128]{3,2,1,0:T(8,128)} custom-call(f32[64,8,128]{2,1,0:T(8,128)S(1)} %get-tuple-element.23.keep_ref, f32[64,8,128]{2,1,0:T(8,128)S(1)} %collective-permute-done.6.core_ref), custom_call_target="tpu_custom_call" | custom-call | tf_op jit(solution)/shard_map/core/pallas_call | solution.py:360
  29.8 3.5 %all-to-all-start = ((f32[16,4,8,128]{3,2,1,0:T(8,128)}), f32[16,4,8,128]{3,2,1,0:T(8,128)S(1)}, u32[]{:S(2)}, u32[]{:S(2)}) async-start(f32[16,4,8,128]{3,2,1,0:T(8,128)} %core.1), calls=%async_computation | async-start | bytes 524288 | tf_op jit(solution)/shard_map/all_to_all | solution.py:421
  33.3 0.0 collective-permute-done.7.from_a
  33.3 3.7 %collective-permute-done.8.from_b = f32[92,8,128]{2,1,0:T(8,128)S(1)} collective-permute-done((f32[92,8,128]{2,1,0:T(8,128)}, f32[92,8,128]{2,1,0:T(8,128)S(1)}, u32[]{:S(2)}, u32[]{:S(2)}) %collective-permute-start.8) | collective-permute-done | bytes 376864 | tf_op jit(solution)/shard_map/ppermute | solution.py:376
  37.0 4.7 %all-to-all-done.top = f32[16,4,8,128]{3,2,1,0:T(8,128)S(1)} async-done(((f32[16,4,8,128]{3,2,1,0:T(8,128)}), f32[16,4,8,128]{3,2,1,0:T(8,128)S(1)}, u32[]{:S(2)}, u32[]{:S(2)}) %all-to-all-start) | async-done | bytes 262176 | tf_op jit(solution)/shard_map/all_to_all | solution.py:421
  41.7 0.0 copy-done
  41.7 2.4 %downward.1 = f32[32,8,128]{2,1,0:T(8,128)} custom-call(f32[16,4,8,128]{3,2,1,0:T(8,128)S(1)} %all-to-all-done.top, f32[92,8,128]{2,1,0:T(8,128)S(1)} %get-tuple-element.22.order.own, f32[92,8,128]{2,1,0:T(8,128)S(1)} %collective-permute-done.7.from_a, f32[92,8,128]{2,1,0:T(8,128)S(1)} %collective-permute-done.8.from_b, bf16[63,128,128]{2,1,0:T(8,128)(2,1)S(1)} %copy-done, ...), custom_call_target="tpu_custom_call" | custom-call | tf_op jit(solution)/shard_map/downward/pallas_call | solution.py:360
  (1 shorter events, 0.0 us)
Async XLA Ops:
  0.0 7.7 %copy-start.1 = (bf16[240,128,128]{2,1,0:T(8,128)(2,1)S(1)}, bf16[240,128,128]{2,1,0:T(8,128)(2,1)}, u32[]{:S(2)}) copy-start(bf16[240,128,128]{2,1,0:T(8,128)(2,1)} %far.3) | copy-start | bytes 23592964
  0.0 16.2 %slice-start = ((s8[8388608]{0:T(1024)(128)(4,1)}), s8[4194304]{0:T(1024)(128)(4,1)S(1)}, s32[]{:S(2)}) async-start(s8[8388608]{0:T(1024)(128)(4,1)} %bitcast.2), calls=%async_computation.1 | async-start | bytes 8388608
  3.3 8.6 %copy-start.2 = (bf16[4,128,128]{2,1,0:T(8,128)(2,1)S(1)}, bf16[4,128,128]{2,1,0:T(8,128)(2,1)}, u32[]{:S(2)}) copy-start(bf16[4,128,128]{2,1,0:T(8,128)(2,1)} %blocks.1) | copy-start | bytes 393220
  3.3 8.6 %copy-start.4 = (s32[1,4]{1,0:T(1,128)S(1)}, s32[1,4]{1,0:T(1,128)}, u32[]{:S(2)}) copy-start(s32[1,4]{1,0:T(1,128)} %group_list.1) | copy-start | bytes 52
  3.4 6.8 %collective-permute-start = (f32[8,128]{1,0:T(8,128)S(1)}, f32[8,128]{1,0:T(8,128)S(1)}, u32[]{:S(2)}, u32[]{:S(2)}) collective-permute-start(f32[8,128]{1,0:T(8,128)S(1)} %get-tuple-element.16.g0.order), channel_id=1, source_target_pairs={{0,2},{1,3},{2,0},{3,1},{4,6},{5,7},{6,4},{7,5},{8,10},{9,11},{10,... | collective-permute-start | bytes 12296 | tf_op jit(solution)/shard_map/ppermute | solution.py:376
  6.5 3.6 %collective-permute-start.1 = (f32[8,128]{1,0:T(8,128)S(1)}, f32[8,128]{1,0:T(8,128)S(1)}, u32[]{:S(2)}, u32[]{:S(2)}) collective-permute-start(f32[8,128]{1,0:T(8,128)S(1)} %get-tuple-element.16.g0.order), channel_id=1, source_target_pairs={{0,1},{1,0},{2,3},{3,2},{4,5},{5,4},{6,7},{7,6},{8,9},{9,8},{10,11... | collective-permute-start | bytes 12296 | tf_op jit(solution)/shard_map/ppermute | solution.py:376
  7.1 4.8 %collective-permute-start.2 = (f32[8,128]{1,0:T(8,128)S(1)}, f32[8,128]{1,0:T(8,128)S(1)}, u32[]{:S(2)}, u32[]{:S(2)}) collective-permute-start(f32[8,128]{1,0:T(8,128)S(1)} %get-tuple-element.16.g0.order), channel_id=1, source_target_pairs={{0,3},{1,2},{2,1},{3,0},{4,7},{5,6},{6,5},{7,4},{8,11},{9,10},{10,... | collective-permute-start | bytes 12296 | tf_op jit(solution)/shard_map/ppermute | solution.py:376
  7.7 8.5 %slice-start.1 = ((s8[8388608]{0:T(1024)(128)(4,1)}), s8[4194304]{0:T(1024)(128)(4,1)S(1)}, s32[]{:S(2)}) async-start(s8[8388608]{0:T(1024)(128)(4,1)} %bitcast.2), calls=%async_computation.2 | async-start | bytes 8388608
  7.7 8.5 %copy-start.3 = (bf16[32,8,128]{2,1,0:T(8,128)(2,1)S(1)}, bf16[32,8,128]{2,1,0:T(8,128)(2,1)}, u32[]{:S(2)}) copy-start(bf16[32,8,128]{2,1,0:T(8,128)(2,1)} %src_ref.1) | copy-start | bytes 196612
  12.1 7.6 %collective-permute-start.3 = (f32[17,8,128]{2,1,0:T(8,128)S(1)}, f32[17,8,128]{2,1,0:T(8,128)S(1)}, u32[]{:S(2)}, u32[]{:S(2)}) collective-permute-start(f32[17,8,128]{2,1,0:T(8,128)S(1)} %group.1.order.p0), channel_id=1, source_target_pairs={{0,2},{1,3},{2,0},{3,1},{4,6},{5,7},{6,4},{7,5},{8,10},{9,11},{10,... | collective-permute-start | bytes 208904 | tf_op jit(solution)/shard_map/ppermute | solution.py:376
  13.3 6.4 %collective-permute-start.4 = (f32[17,8,128]{2,1,0:T(8,128)S(1)}, f32[17,8,128]{2,1,0:T(8,128)S(1)}, u32[]{:S(2)}, u32[]{:S(2)}) collective-permute-start(f32[17,8,128]{2,1,0:T(8,128)S(1)} %group.1.order.p0), channel_id=1, source_target_pairs={{0,1},{1,0},{2,3},{3,2},{4,5},{5,4},{6,7},{7,6},{8,9},{9,8},{10,11... | collective-permute-start | bytes 208904 | tf_op jit(solution)/shard_map/ppermute | solution.py:376
  13.9 5.8 %collective-permute-start.5 = (f32[17,8,128]{2,1,0:T(8,128)S(1)}, f32[17,8,128]{2,1,0:T(8,128)S(1)}, u32[]{:S(2)}, u32[]{:S(2)}) collective-permute-start(f32[17,8,128]{2,1,0:T(8,128)S(1)} %group.1.order.p0), channel_id=1, source_target_pairs={{0,3},{1,2},{2,1},{3,0},{4,7},{5,6},{6,5},{7,4},{8,11},{9,10},{10,... | collective-permute-start | bytes 208904 | tf_op jit(solution)/shard_map/ppermute | solution.py:376
  16.2 25.5 %copy-start = (bf16[63,128,128]{2,1,0:T(8,128)(2,1)S(1)}, bf16[63,128,128]{2,1,0:T(8,128)(2,1)}, u32[]{:S(2)}) copy-start(bf16[63,128,128]{2,1,0:T(8,128)(2,1)} %down.1) | copy-start | bytes 6193156
  20.9 8.2 %collective-permute-start.6 = (f32[64,8,128]{2,1,0:T(8,128)S(1)}, f32[64,8,128]{2,1,0:T(8,128)S(1)}, u32[]{:S(2)}, u32[]{:S(2)}) collective-permute-start(f32[64,8,128]{2,1,0:T(8,128)S(1)} %get-tuple-element.24), channel_id=1, source_target_pairs={{0,4},{4,0},{8,12},{12,8},{16,20},{20,16},{24,28},{28,24},{32,36},... | collective-permute-start | bytes 786440 | tf_op jit(solution)/shard_map/ppermute | solution.py:376
  21.0 12.3 %collective-permute-start.7 = (f32[92,8,128]{2,1,0:T(8,128)}, f32[92,8,128]{2,1,0:T(8,128)S(1)}, u32[]{:S(2)}, u32[]{:S(2)}) collective-permute-start(f32[92,8,128]{2,1,0:T(8,128)} %get-tuple-element.25), channel_id=1, source_target_pairs={{0,1},{1,0},{2,3},{3,2},{4,5},{5,4},{6,7},{7,6},{8,9},{9,8},{10,11... | collective-permute-start | bytes 1130504 | tf_op jit(solution)/shard_map/ppermute | solution.py:376
  21.3 15.7 %collective-permute-start.8 = (f32[92,8,128]{2,1,0:T(8,128)}, f32[92,8,128]{2,1,0:T(8,128)S(1)}, u32[]{:S(2)}, u32[]{:S(2)}) collective-permute-start(f32[92,8,128]{2,1,0:T(8,128)} %get-tuple-element.26), channel_id=1, source_target_pairs={{0,127},{1,2},{2,1},{3,4},{4,3},{5,6},{6,5},{7,8},{8,7},{9,10},{10... | collective-permute-start | bytes 1130504 | tf_op jit(solution)/shard_map/ppermute | solution.py:376
  29.8 12.0 %all-to-all-start = ((f32[16,4,8,128]{3,2,1,0:T(8,128)}), f32[16,4,8,128]{3,2,1,0:T(8,128)S(1)}, u32[]{:S(2)}, u32[]{:S(2)}) async-start(f32[16,4,8,128]{3,2,1,0:T(8,128)} %core.1), calls=%async_computation | async-start | bytes 524288 | tf_op jit(solution)/shard_map/all_to_all | solution.py:421
